TPU v7x, 32 devices: a whole 2x2x4 slice. The times are simulated.
32 devices in a mesh: dp: 2 (over x), expert: 16 (over z, y, core).
Axes of the slice: x: 2, y: 2, z: 4, core: 2. Of those that a mesh axis runs over, the one named last changes fastest.
Arguments:
- tokens: bfloat16 [16, 1024, 2048], P('expert', 'dp'), may hold values from -6 to 6
- segments: int32 [16, 1024], P('expert'), may hold values from 0 to 3, never falling along the last dimension, each value on 1 to 512 neighbouring positions
- routes: int32 [16, 1024, 6], P('expert', 'dp'), may hold values from 0 to 15, all different within a row; in each aligned block of 512 rows (0 to 511, 512 to 1023, ..., all dimensions but the last counted through in order) at most 256 rows name the same one
- combine: float32 [16, 1024, 6], P('expert', 'dp'), may hold values from 0.05 to 0.4
- input_gain: bfloat16 [2048], P(('dp', 'expert')), may hold values from 0.099609375 to 1.8984375
- query_weight: bfloat16 [2048, 3072], P(('dp', 'expert')), may hold values from -0.125 to 0.125
- latent_weight: bfloat16 [2048, 576], P(('dp', 'expert')), may hold values from -0.125 to 0.125
- latent_gain: bfloat16 [512], P(('dp', 'expert')), may hold values from 0.099609375 to 1.8984375
- expand_weight: bfloat16 [512, 4096], P(None, ('dp', 'expert')), may hold values from -0.25 to 0.25
- output_weight: bfloat16 [2048, 2048], P(None, ('dp', 'expert')), may hold values from -1 to 1
- middle_gain: bfloat16 [2048], P(('dp', 'expert')), may hold values from 0.099609375 to 1.8984375
- shared_gate: bfloat16 [2048, 2816], P(('dp', 'expert')), may hold values from -0.125 to 0.125
- shared_up: bfloat16 [2048, 2816], P(('dp', 'expert')), may hold values from -0.125 to 0.125
- shared_down: bfloat16 [2816, 2048], P(None, ('dp', 'expert')), may hold values from -0.109375 to 0.109375
- expert_gate: bfloat16 [16, 2048, 1408], P('expert', 'dp'), may hold values from -0.125 to 0.125
- expert_up: bfloat16 [16, 2048, 1408], P('expert', 'dp'), may hold values from -0.125 to 0.125
- expert_down: bfloat16 [16, 1408, 2048], P('expert', None, 'dp'), may hold values from -0.15625 to 0.15625
- cotangent: bfloat16 [16, 1024, 2048], P('expert', 'dp'), may hold values from -6 to 6
Outputs:
- output: bfloat16 [16, 1024, 2048], P('expert', 'dp')
- input_grad: float32 [16, 1024, 2048], P('expert', 'dp')
- input_gain_grad: float32 [2048], P(('dp', 'expert'))
- query_weight_grad: float32 [2048, 3072], P(('dp', 'expert'))
- latent_weight_grad: float32 [2048, 576], P(('dp', 'expert'))
- latent_gain_grad: float32 [512], P(('dp', 'expert'))
- expand_weight_grad: float32 [512, 4096], P(None, ('dp', 'expert'))
- output_weight_grad: float32 [2048, 2048], P(None, ('dp', 'expert'))
- middle_gain_grad: float32 [2048], P(('dp', 'expert'))
- shared_gate_grad: float32 [2048, 2816], P(('dp', 'expert'))
- shared_up_grad: float32 [2048, 2816], P(('dp', 'expert'))
- shared_down_grad: float32 [2816, 2048], P(None, ('dp', 'expert'))
- expert_gate_grad: float32 [16, 2048, 1408], P('expert', 'dp')
- expert_up_grad: float32 [16, 2048, 1408], P('expert', 'dp')
- expert_down_grad: float32 [16, 1408, 2048], P('expert', None, 'dp')
Inputs may be any that keep to these rules, and one draw needn't show every extreme that they name: `segments`: numbers never fall along a sequence; equal numbers mark one document of at most 512 positions. `routes`: the 6 entries of a token name different experts; in each aligned block of 512 positions of a sequence no expert is named by more than 256 tokens, and some block reaches 256.
All inputs are finite; a program needn't handle non-finite values.
Results may differ from a plain program's by a relative error of at most 0.02.
Values may be sent and summed in bfloat16 or wider, within the bound.
A program may use at most 512 MiB of HBM per device.

v0:
```python
import jax
import jax.numpy as jnp
from jax import lax
from jax.sharding import PartitionSpec as P

NOPE = 128
ROPE = 64
VDIM = 128
RANK = 512


epsilon = 1e-06


def rotate(values, cosine, sine_part):
    half_width = values.shape[-1] // 2
    first_half = values[..., :half_width]
    second_half = values[..., half_width:]
    return jnp.concatenate(
        [
            first_half * cosine - second_half * sine_part,
            second_half * cosine + first_half * sine_part,
        ],
        axis=-1,
    )


def rotate_back(gradient, cosine, sine_part):
    half_width = gradient.shape[-1] // 2
    first_half = gradient[..., :half_width]
    second_half = gradient[..., half_width:]
    return jnp.concatenate(
        [
            first_half * cosine + second_half * sine_part,
            second_half * cosine - first_half * sine_part,
        ],
        axis=-1,
    )


def norm_back(gradient, normed, scale_vec, gain_vec):
    scaled = gradient * gain_vec
    inner_mean = jnp.mean(scaled * normed, axis=-1, keepdims=True)
    gain_grad = jnp.sum(gradient * normed, axis=0)
    return (scale_vec * (scaled - normed * inner_mean), gain_grad)


def silu_parts(gate_in):
    sigmoid_gate = jax.nn.sigmoid(gate_in)
    return (gate_in * sigmoid_gate, sigmoid_gate * (1.0 + gate_in * (1.0 - sigmoid_gate)))


def rotary_tables(positions):
    frequency = jnp.power(10000.0, -jnp.arange(ROPE // 2).astype(jnp.float32) * 2.0 / ROPE)
    angles = positions.astype(jnp.float32)[:, None] * frequency[None, :]
    return (jnp.cos(angles), jnp.sin(angles))


def project_queries(rows_in, weight, cosine, sine_part, batch_size, span):
    linear = jnp.dot(rows_in, weight, preferred_element_type=jnp.float32).reshape(
        batch_size, span, -1, NOPE + ROPE
    )
    return jnp.concatenate(
        [
            linear[..., :NOPE],
            rotate(linear[..., NOPE:], cosine[None, :, None, :], sine_part[None, :, None, :]),
        ],
        axis=-1,
    ).astype(jnp.bfloat16)


def latent_parts(latent_linear, gain_vec, cosine, sine_part, batch_size, span):
    latent_raw = latent_linear[:, :RANK]
    latent_scale = lax.rsqrt(jnp.mean(latent_raw * latent_raw, axis=-1, keepdims=True) + epsilon)
    latent_normed = latent_raw * latent_scale
    latent_low = (latent_normed * gain_vec).astype(jnp.bfloat16)
    rope_keys = rotate(
        latent_linear[:, RANK:].reshape(batch_size, span, ROPE), cosine[None], sine_part[None]
    ).astype(jnp.bfloat16)
    return (latent_normed, latent_scale, latent_low, rope_keys)


def split_keys(key_values, rope_keys, heads_count):
    batch_size, span = (key_values.shape[0], key_values.shape[1])
    kv_heads = key_values.reshape(batch_size, span, heads_count, NOPE + VDIM)
    key_all = jnp.concatenate(
        [
            kv_heads[..., :NOPE],
            jnp.broadcast_to(rope_keys[:, :, None, :], (batch_size, span, heads_count, ROPE)),
        ],
        axis=-1,
    )
    return (kv_heads[..., NOPE:], key_all)


def masked_scores(queries, key_all, allowed):
    factor = (NOPE + ROPE) ** (-0.5)
    scores = (
        jnp.einsum("bihd,bjhd->bhij", queries, key_all, preferred_element_type=jnp.float32) * factor
    )
    return jnp.where(allowed[:, None], scores, -1e30)


def attend_forward(queries, key_all, value_part, allowed):
    masked = masked_scores(queries, key_all, allowed)
    row_max = jnp.max(masked, axis=-1, keepdims=True)
    exponent = jnp.exp(masked - row_max)
    row_total = jnp.sum(exponent, axis=-1, keepdims=True)
    softmax_out = exponent / row_total
    mixed = jnp.einsum(
        "bhij,bjhd->bihd",
        softmax_out.astype(jnp.bfloat16),
        value_part,
        preferred_element_type=jnp.float32,
    ).astype(jnp.bfloat16)
    return (mixed, row_max + jnp.log(row_total))


def attend_backward(queries, key_all, value_part, allowed, log_total, mixed_grad):
    factor = (NOPE + ROPE) ** (-0.5)
    softmax_out = jnp.exp(masked_scores(queries, key_all, allowed) - log_total)
    soft_low = softmax_out.astype(jnp.bfloat16)
    soft_grad = jnp.einsum(
        "bihd,bjhd->bhij", mixed_grad, value_part, preferred_element_type=jnp.float32
    )
    inner_sum = jnp.sum(soft_grad * softmax_out, axis=-1, keepdims=True)
    score_grad = (softmax_out * (soft_grad - inner_sum) * factor).astype(jnp.bfloat16)
    query_grad = jnp.einsum(
        "bhij,bjhd->bihd", score_grad, key_all, preferred_element_type=jnp.float32
    )
    key_grad = jnp.einsum(
        "bhij,bihd->bjhd", score_grad, queries, preferred_element_type=jnp.float32
    )
    value_grad = jnp.einsum(
        "bhij,bihd->bjhd", soft_low, mixed_grad, preferred_element_type=jnp.float32
    )
    return (query_grad, key_grad, value_grad)


def whole_sequence(part_rows):
    return lax.all_gather(part_rows, "dp", axis=1, tiled=True)


def to_positions(partial_sum):
    return lax.psum_scatter(partial_sum, "dp", scatter_dimension=1, tiled=True)


def local(
    tokens,
    segments,
    routes,
    combine,
    input_gain,
    query_weight,
    latent_weight,
    latent_gain,
    expand_weight,
    output_weight,
    middle_gain,
    shared_gate,
    shared_up,
    shared_down,
    expert_gate,
    expert_up,
    expert_down,
    cotangent,
):
    batch_size, length, model_width = tokens.shape
    seq_length = segments.shape[1]
    row_count = batch_size * length
    top_k = routes.shape[2]
    dp_count = lax.axis_size("dp")
    first_gain, latent_full, latent_norm, second_gain = (
        lax.all_gather(input_gain, ("dp", "expert"), axis=0, tiled=True),
        lax.all_gather(latent_weight, ("dp", "expert"), axis=0, tiled=True),
        lax.all_gather(latent_gain, ("dp", "expert"), axis=0, tiled=True),
        lax.all_gather(middle_gain, ("dp", "expert"), axis=0, tiled=True),
    )
    query_part, gate_part, up_part, output_part, down_part, expand_own = (
        lax.all_gather(query_weight, "expert", axis=0, tiled=True),
        lax.all_gather(shared_gate, "expert", axis=0, tiled=True),
        lax.all_gather(shared_up, "expert", axis=0, tiled=True),
        lax.all_gather(output_weight, "expert", axis=1, tiled=True),
        lax.all_gather(shared_down, "expert", axis=1, tiled=True),
        lax.all_gather(expand_weight, "expert", axis=1, tiled=True),
    )
    expert_gate_weight_all, expert_up_weight_all, expert_down_weight_all = (
        lax.all_gather(expert_gate, "dp", axis=1, tiled=True),
        lax.all_gather(expert_up, "dp", axis=1, tiled=True),
        lax.all_gather(expert_down, "dp", axis=2, tiled=True),
    )
    offset = lax.axis_index("dp") * length
    token_values = tokens.astype(jnp.float32).reshape(row_count, model_width)
    scale_one = lax.rsqrt(jnp.mean(token_values * token_values, axis=-1, keepdims=True) + epsilon)
    normed_one = token_values * scale_one
    normed_low = (normed_one * first_gain).astype(jnp.bfloat16)
    out_grad = cotangent.astype(jnp.float32).reshape(row_count, model_width)
    rows_block = query_part.shape[0]
    query_cols, gate_cols, up_cols, output_recv, down_recv = (
        lax.all_to_all(
            query_part.reshape(rows_block, dp_count, -1),
            "dp",
            split_axis=1,
            concat_axis=0,
            tiled=True,
        ),
        lax.all_to_all(
            gate_part.reshape(rows_block, dp_count, -1),
            "dp",
            split_axis=1,
            concat_axis=0,
            tiled=True,
        ),
        lax.all_to_all(
            up_part.reshape(rows_block, dp_count, -1), "dp", split_axis=1, concat_axis=0, tiled=True
        ),
        lax.all_to_all(
            output_part.reshape(1, dp_count, -1), "dp", split_axis=1, concat_axis=0, tiled=True
        ),
        lax.all_to_all(
            down_part.reshape(1, dp_count, -1), "dp", split_axis=1, concat_axis=0, tiled=True
        ),
    )
    query_cols = query_cols.reshape(model_width, -1)
    gate_cols = gate_cols.reshape(model_width, -1)
    up_cols = up_cols.reshape(model_width, -1)
    output_rows = (
        output_recv.reshape(dp_count, -1, rows_block).transpose(1, 0, 2).reshape(-1, model_width)
    )
    down_rows = (
        down_recv.reshape(dp_count, -1, rows_block).transpose(1, 0, 2).reshape(-1, model_width)
    )
    heads_count = query_cols.shape[1] // (NOPE + ROPE)
    full_pos = jnp.arange(seq_length, dtype=jnp.int32)
    cosine_full, sine_full = rotary_tables(full_pos)
    whole_flat = whole_sequence(normed_low.reshape(batch_size, length, model_width)).reshape(
        batch_size * seq_length, model_width
    )
    queries = project_queries(
        whole_flat, query_cols, cosine_full, sine_full, batch_size, seq_length
    )
    latent_linear = jnp.dot(whole_flat, latent_full, preferred_element_type=jnp.float32)
    latent_normed_full, latent_scale_full, latent_low_full, rope_full = latent_parts(
        latent_linear, latent_norm, cosine_full, sine_full, batch_size, seq_length
    )
    expanded = (
        jnp.dot(latent_low_full, expand_own, preferred_element_type=jnp.float32)
        .astype(jnp.bfloat16)
        .reshape(batch_size, seq_length, -1)
    )
    value_part, key_all = split_keys(expanded, rope_full, heads_count)
    allowed = (segments[:, :, None] == segments[:, None, :]) & (
        full_pos[:, None] >= full_pos[None, :]
    )[None]
    mixed_four, log_total = attend_forward(queries, key_all, value_part, allowed)
    mixed_heads = mixed_four.reshape(batch_size * seq_length, -1)
    attention = to_positions(
        jnp.dot(mixed_heads, output_rows, preferred_element_type=jnp.float32).reshape(
            batch_size, seq_length, model_width
        )
    ).reshape(row_count, model_width)
    middle = token_values + attention
    scale_two = lax.rsqrt(jnp.mean(middle * middle, axis=-1, keepdims=True) + epsilon)
    normed_two = middle * scale_two
    ffn_rows = (normed_two * second_gain).astype(jnp.bfloat16)
    whole_rows = whole_sequence(ffn_rows.reshape(batch_size, length, model_width)).reshape(
        batch_size * seq_length, model_width
    )
    gate_pre = jnp.dot(whole_rows, gate_cols, preferred_element_type=jnp.float32)
    up_pre = jnp.dot(whole_rows, up_cols, preferred_element_type=jnp.float32)
    shared_act = (jax.nn.silu(gate_pre) * up_pre).astype(jnp.bfloat16)
    shared_out = to_positions(
        jnp.dot(shared_act, down_rows, preferred_element_type=jnp.float32).reshape(
            batch_size, seq_length, model_width
        )
    ).reshape(row_count, model_width)
    experts_total = expert_gate.shape[0] * lax.axis_size("expert")
    slot_cap = batch_size * (length * top_k * 4 // (experts_total * 3))
    flat_routes = routes.reshape(row_count * top_k)
    one_hot = (flat_routes[:, None] == jnp.arange(experts_total, dtype=jnp.int32)[None, :]).astype(
        jnp.int32
    )
    earlier = jnp.cumsum(one_hot, axis=0) - one_hot
    slot_pos = jnp.sum(earlier * one_hot, axis=1)
    target = flat_routes * slot_cap + slot_pos
    source_route = (
        jnp.full((experts_total * slot_cap,), row_count * top_k, jnp.int32)
        .at[target]
        .set(jnp.arange(row_count * top_k, dtype=jnp.int32))
    )
    source_token = source_route // top_k
    padding = jnp.zeros((1, model_width), jnp.bfloat16)
    send_rows = jnp.concatenate([ffn_rows, padding], axis=0)[source_token].reshape(
        experts_total, slot_cap, model_width
    )
    received_rows = lax.all_to_all(send_rows, "expert", split_axis=0, concat_axis=1, tiled=True)
    gate_exp = jnp.einsum(
        "zti,ziq->ztq", received_rows, expert_gate_weight_all, preferred_element_type=jnp.float32
    )
    expert_up_projected = jnp.einsum(
        "zti,ziq->ztq", received_rows, expert_up_weight_all, preferred_element_type=jnp.float32
    )
    act_exp = (jax.nn.silu(gate_exp) * expert_up_projected).astype(jnp.bfloat16)
    out_exp = jnp.einsum(
        "erf,efd->erd", act_exp, expert_down_weight_all, preferred_element_type=jnp.float32
    ).astype(jnp.bfloat16)
    returned = lax.all_to_all(out_exp, "expert", split_axis=1, concat_axis=0, tiled=True).reshape(
        experts_total * slot_cap, model_width
    )
    weights_route = combine.reshape(row_count, top_k)
    routed = jnp.sum(
        weights_route[:, :, None]
        * returned[target].reshape(row_count, top_k, model_width).astype(jnp.float32),
        axis=1,
    )
    outputs = (
        (middle + shared_out + routed).astype(jnp.bfloat16).reshape(batch_size, length, model_width)
    )
    route_grads = (
        (weights_route[:, :, None] * out_grad[:, None, :])
        .astype(jnp.bfloat16)
        .reshape(row_count * top_k, model_width)
    )
    send_grads = jnp.concatenate([route_grads, padding], axis=0)[source_route].reshape(
        experts_total, slot_cap, model_width
    )
    arrived_grads = lax.all_to_all(send_grads, "expert", split_axis=0, concat_axis=1, tiled=True)
    grad_edown = jnp.einsum(
        "erf,erd->efd", act_exp, arrived_grads, preferred_element_type=jnp.float32
    )
    act_exp_grad = jnp.einsum(
        "erd,efd->erf", arrived_grads, expert_down_weight_all, preferred_element_type=jnp.float32
    )
    silu_exp, slope_exp = silu_parts(gate_exp)
    gate_exp_grad = (act_exp_grad * expert_up_projected * slope_exp).astype(jnp.bfloat16)
    expert_up_projected_gradient = (act_exp_grad * silu_exp).astype(jnp.bfloat16)
    grad_egate = jnp.einsum(
        "quk,quj->qkj", received_rows, gate_exp_grad, preferred_element_type=jnp.float32
    )
    expert_up_weight_gradient = jnp.einsum(
        "quk,quj->qkj",
        received_rows,
        expert_up_projected_gradient,
        preferred_element_type=jnp.float32,
    )
    input_exp_grad = (
        jnp.einsum(
            "pcw,pnw->pcn",
            gate_exp_grad,
            expert_gate_weight_all,
            preferred_element_type=jnp.float32,
        )
        + jnp.einsum(
            "pcw,pnw->pcn",
            expert_up_projected_gradient,
            expert_up_weight_all,
            preferred_element_type=jnp.float32,
        )
    ).astype(jnp.bfloat16)
    sent_back = lax.all_to_all(
        input_exp_grad, "expert", split_axis=1, concat_axis=0, tiled=True
    ).reshape(experts_total * slot_cap, model_width)
    routed_rows_grad = jnp.sum(
        sent_back[target].reshape(row_count, top_k, model_width).astype(jnp.float32), axis=1
    )
    expert_grads = (
        lax.psum_scatter(
            grad_egate.astype(jnp.bfloat16), "dp", scatter_dimension=1, tiled=True
        ).astype(jnp.float32),
        lax.psum_scatter(
            expert_up_weight_gradient.astype(jnp.bfloat16), "dp", scatter_dimension=1, tiled=True
        ).astype(jnp.float32),
        lax.psum_scatter(
            grad_edown.astype(jnp.bfloat16), "dp", scatter_dimension=2, tiled=True
        ).astype(jnp.float32),
    )
    whole_grad = whole_sequence(cotangent).reshape(batch_size * seq_length, model_width)
    grad_sdown_t = jnp.einsum(
        "rd,rf->df", whole_grad, shared_act, preferred_element_type=jnp.float32
    )
    act_grad = jnp.einsum("rd,fd->rf", whole_grad, down_rows, preferred_element_type=jnp.float32)
    silu_val, silu_slope = silu_parts(gate_pre)
    gate_grad = (act_grad * up_pre * silu_slope).astype(jnp.bfloat16)
    up_grad = (act_grad * silu_val).astype(jnp.bfloat16)
    grad_sgate = jnp.einsum("rd,rf->df", whole_rows, gate_grad, preferred_element_type=jnp.float32)
    grad_sup = jnp.einsum("rd,rf->df", whole_rows, up_grad, preferred_element_type=jnp.float32)
    shared_partial = jnp.einsum(
        "rf,df->rd", gate_grad, gate_cols, preferred_element_type=jnp.float32
    ) + jnp.einsum("rf,df->rd", up_grad, up_cols, preferred_element_type=jnp.float32)
    shared_rows_grad = to_positions(
        shared_partial.reshape(batch_size, seq_length, model_width)
    ).reshape(row_count, model_width)
    rows_grad = shared_rows_grad + routed_rows_grad
    middle_part, second_gain_grad = norm_back(rows_grad, normed_two, scale_two, second_gain)
    middle_grad = out_grad + middle_part
    attn_grad = middle_grad.astype(jnp.bfloat16)
    whole_attn = whole_sequence(attn_grad.reshape(batch_size, length, model_width)).reshape(
        batch_size * seq_length, model_width
    )
    grad_out_t = jnp.einsum(
        "rd,rv->dv", whole_attn, mixed_heads, preferred_element_type=jnp.float32
    )
    mixed_grad = (
        jnp.einsum("rd,vd->rv", whole_attn, output_rows, preferred_element_type=jnp.float32)
        .astype(jnp.bfloat16)
        .reshape(batch_size, seq_length, heads_count, VDIM)
    )
    query_grad, key_grad, value_grad = attend_backward(
        queries, key_all, value_part, allowed, log_total, mixed_grad
    )
    expand_low = (
        jnp.concatenate([key_grad[..., :NOPE], value_grad], axis=-1)
        .astype(jnp.bfloat16)
        .reshape(batch_size * seq_length, -1)
    )
    grad_expand = jnp.einsum(
        "rc,rk->ck", latent_low_full, expand_low, preferred_element_type=jnp.float32
    )
    latent_partial = jnp.einsum(
        "rk,ck->rc", expand_low, expand_own, preferred_element_type=jnp.float32
    )
    rope_partial = jnp.sum(key_grad[..., NOPE:], axis=2).reshape(batch_size * seq_length, ROPE)
    query_linear_grad = (
        jnp.concatenate(
            [
                query_grad[..., :NOPE],
                rotate_back(
                    query_grad[..., NOPE:],
                    cosine_full[None, :, None, :],
                    sine_full[None, :, None, :],
                ),
            ],
            axis=-1,
        )
        .astype(jnp.bfloat16)
        .reshape(batch_size * seq_length, -1)
    )
    grad_query = jnp.einsum(
        "rd,rk->dk", whole_flat, query_linear_grad, preferred_element_type=jnp.float32
    )
    query_partial = jnp.einsum(
        "rk,dk->rd", query_linear_grad, query_cols, preferred_element_type=jnp.float32
    )
    combined = to_positions(
        jnp.concatenate([latent_partial, rope_partial, query_partial], axis=-1).reshape(
            batch_size, seq_length, -1
        )
    ).reshape(row_count, -1)
    latent_grad_in = combined[:, :RANK]
    rope_grad = combined[:, RANK : RANK + ROPE].reshape(batch_size, length, ROPE)
    query_normed_grad = combined[:, RANK + ROPE :]
    own_normed = lax.dynamic_slice_in_dim(
        latent_normed_full.reshape(batch_size, seq_length, RANK), offset, length, 1
    ).reshape(row_count, RANK)
    own_scale = lax.dynamic_slice_in_dim(
        latent_scale_full.reshape(batch_size, seq_length, 1), offset, length, 1
    ).reshape(row_count, 1)
    latent_grad, latent_gain_grad = norm_back(latent_grad_in, own_normed, own_scale, latent_norm)
    own_cos = lax.dynamic_slice_in_dim(cosine_full, offset, length, 0)
    own_sin = lax.dynamic_slice_in_dim(sine_full, offset, length, 0)
    rope_linear_grad = rotate_back(rope_grad, own_cos[None], own_sin[None]).reshape(row_count, ROPE)
    latent_linear_grad = jnp.concatenate([latent_grad, rope_linear_grad], axis=-1).astype(
        jnp.bfloat16
    )
    grad_latent = jnp.einsum(
        "rd,rk->dk", normed_low, latent_linear_grad, preferred_element_type=jnp.float32
    )
    normed_grad = query_normed_grad + jnp.einsum(
        "rk,dk->rd", latent_linear_grad, latent_full, preferred_element_type=jnp.float32
    )
    parts_back = (
        lax.all_to_all(
            grad_query.reshape(dp_count, -1, 1, grad_query.shape[1]).astype(jnp.bfloat16),
            "dp",
            split_axis=0,
            concat_axis=2,
            tiled=True,
        ).astype(jnp.float32),
        lax.all_to_all(
            grad_sgate.reshape(dp_count, -1, 1, grad_sgate.shape[1]).astype(jnp.bfloat16),
            "dp",
            split_axis=0,
            concat_axis=2,
            tiled=True,
        ).astype(jnp.float32),
        lax.all_to_all(
            grad_sup.reshape(dp_count, -1, 1, grad_sup.shape[1]).astype(jnp.bfloat16),
            "dp",
            split_axis=0,
            concat_axis=2,
            tiled=True,
        ).astype(jnp.float32),
        lax.all_to_all(
            grad_out_t.reshape(dp_count, -1, 1, grad_out_t.shape[1]).astype(jnp.bfloat16),
            "dp",
            split_axis=0,
            concat_axis=2,
            tiled=True,
        ).astype(jnp.float32),
        lax.all_to_all(
            grad_sdown_t.reshape(dp_count, -1, 1, grad_sdown_t.shape[1]).astype(jnp.bfloat16),
            "dp",
            split_axis=0,
            concat_axis=2,
            tiled=True,
        ).astype(jnp.float32),
    )
    query_back, gate_back, up_back, out_back, down_back = (
        piece.reshape(piece.shape[1], -1) for piece in parts_back
    )
    summed = (
        lax.psum_scatter(
            query_back.astype(jnp.bfloat16), "expert", scatter_dimension=0, tiled=True
        ).astype(jnp.float32),
        lax.psum_scatter(
            gate_back.astype(jnp.bfloat16), "expert", scatter_dimension=0, tiled=True
        ).astype(jnp.float32),
        lax.psum_scatter(
            up_back.astype(jnp.bfloat16), "expert", scatter_dimension=0, tiled=True
        ).astype(jnp.float32),
        lax.psum_scatter(
            out_back.astype(jnp.bfloat16), "expert", scatter_dimension=0, tiled=True
        ).astype(jnp.float32),
        lax.psum_scatter(
            down_back.astype(jnp.bfloat16), "expert", scatter_dimension=0, tiled=True
        ).astype(jnp.float32),
        lax.psum_scatter(
            grad_expand.astype(jnp.bfloat16), "expert", scatter_dimension=1, tiled=True
        ).astype(jnp.float32),
    )
    query_weight_grad = summed[0]
    shared_gate_grad = summed[1]
    shared_up_grad = summed[2]
    output_weight_grad = summed[3].T
    shared_down_grad = summed[4].T
    expand_weight_grad = summed[5]
    input_part, first_gain_grad = norm_back(normed_grad, normed_one, scale_one, first_gain)
    small_grads = (
        lax.psum_scatter(first_gain_grad, ("dp", "expert"), scatter_dimension=0, tiled=True),
        lax.psum_scatter(grad_latent, ("dp", "expert"), scatter_dimension=0, tiled=True),
        lax.psum_scatter(latent_gain_grad, ("dp", "expert"), scatter_dimension=0, tiled=True),
        lax.psum_scatter(second_gain_grad, ("dp", "expert"), scatter_dimension=0, tiled=True),
    )
    input_gain_grad, latent_weight_grad, latent_gain_grad_out, middle_gain_grad = small_grads
    tokens_grad = (middle_grad + input_part).reshape(batch_size, length, model_width)
    return (
        outputs,
        tokens_grad,
        input_gain_grad,
        query_weight_grad,
        latent_weight_grad,
        latent_gain_grad_out,
        expand_weight_grad,
        output_weight_grad,
        middle_gain_grad,
        shared_gate_grad,
        shared_up_grad,
        shared_down_grad,
        expert_grads[0],
        expert_grads[1],
        expert_grads[2],
    )


def solution(mesh):
    placed = (
        P("expert", "dp", None),
        P("expert", None),
        P("expert", "dp", None),
        P("expert", "dp", None),
        P(("dp", "expert")),
        P(("dp", "expert"), None),
        P(("dp", "expert"), None),
        P(("dp", "expert")),
        P(None, ("dp", "expert")),
        P(None, ("dp", "expert")),
        P(("dp", "expert")),
        P(("dp", "expert"), None),
        P(("dp", "expert"), None),
        P(None, ("dp", "expert")),
        P("expert", "dp", None),
        P("expert", "dp", None),
        P("expert", None, "dp"),
        P("expert", "dp", None),
    )
    return jax.shard_map(
        local,
        mesh=mesh,
        in_specs=placed,
        out_specs=(
            P("expert", "dp", None),
            P("expert", "dp", None),
            P(("dp", "expert")),
            P(("dp", "expert"), None),
            P(("dp", "expert"), None),
            P(("dp", "expert")),
            P(None, ("dp", "expert")),
            P(None, ("dp", "expert")),
            P(("dp", "expert")),
            P(("dp", "expert"), None),
            P(("dp", "expert"), None),
            P(None, ("dp", "expert")),
            P("expert", "dp", None),
            P("expert", "dp", None),
            P("expert", None, "dp"),
        ),
        check_vma=False,
    )
```

profile of v0, /device:TPU:0, one launch (start us, length us, event | category | flops | bytes accessed | tf_op | source)
XLA Modules:
  0.0 4097.8 jit_solution(5347069562872782185)
XLA Ops:
  11.3 43.2 %all-reduce.9 = (bf16[2048]{0:T(1024)(128)(2,1)S(1)}, bf16[2048]{0:T(1024)(128)(2,1)}, bf16[512]{0:T(512)(128)(2,1)S(1)}) all-reduce(bf16[2048]{0:T(1024)(128)(2,1)S(1)} %dynamic-update-slice, bf16[2048]{0:T(1024)(128)(2,1)S(1)} %dynamic-update-slice.2, ...), channel_id=1, replica_groups=mesh['dp'=2,'expert'=16] {'dp','expert'}, use_global_device_ids=true, to_apply=%add.2 | all-reduce | flops 4608 | bytes 18432
  144.9 58.4 %all-to-all-done.1 = bf16[2,2,524288]{2,1,0:T(2,128)(2,1)} async-done(((bf16[2,2,524288]{2,1,0:T(2,128)(2,1)}), bf16[2,2,524288]{2,1,0:T(2,128)(2,1)}, u32[]{:S(2)}, u32[]{:S(2)}) %all-to-all-start.1) | async-done | bytes 4194336 | tf_op jit(solution)/shard_map/all_to_all | solution.py:217
  221.0 65.6 %all-gather.17.cloned.1.call-done = bf16[2048,576]{1,0:T(8,128)(2,1)} async-done(((bf16[64,576]{1,0:T(8,128)(2,1)}), bf16[2048,576]{1,0:T(8,128)(2,1)}) %all-gather.17.cloned.1.call-update) | async-done | bytes 2359312 | tf_op jit(solution)/shard_map/all_gather | solution.py:175
  294.4 34.3 all-gather.19.cloned.1.call-done
  491.1 79.3 %reduce-scatter.25.cloned.1.call-done = f32[1,512,2048]{1,2,0:T(8,128)} async-done(((f32[1,1024,2048]{1,2,0:T(8,128)}), f32[1,512,2048]{1,2,0:T(8,128)}) %reduce-scatter.25.cloned.1.call-update) | async-done | bytes 4194320 | tf_op jit(solution)/shard_map/reduce_scatter | solution.py:145
  680.4 37.6 gather_fusion.2
  718.0 255.2 %all-to-all-done.5 = bf16[16,256,2048]{2,1,0:T(8,128)(2,1)} async-done(((bf16[16,256,2048]{2,1,0:T(8,128)(2,1)}), bf16[16,256,2048]{2,1,0:T(8,128)(2,1)}, u32[]{:S(2)}, u32[]{:S(2)}) %all-to-all-start.5) | async-done | bytes 16777248 | tf_op jit(solution)/shard_map/all_to_all | solution.py:296
  973.2 106.4 %all-to-all-start.7 = ((bf16[16,256,2048]{2,1,0:T(8,128)(2,1)}), bf16[16,256,2048]{2,1,0:T(8,128)(2,1)}, u32[]{:S(2)}, u32[]{:S(2)}) async-start(bf16[16,256,2048]{2,1,0:T(8,128)(2,1)} %bitcast.419), calls=%async_computation.10 | async-start | bytes 33554432 | tf_op jit(solution)/shard_map/all_to_all | solution.py:327
  1103.5 42.9 %reduce.14 = bf16[2,1441792]{1,0:T(2,128)(2,1)} reduce(bf16[2,1,1441792]{2,1,0:T(2,128)(2,1)} %bitcast.421, bf16[]{:T(256)} %broadcast.421), dimensions={1}, to_apply=%bitcast.345.reduce_sub_computation | reduce | bytes 11534338
  1265.7 110.7 %all-to-all-done.7 = bf16[16,256,2048]{2,1,0:T(8,128)(2,1)} async-done(((bf16[16,256,2048]{2,1,0:T(8,128)(2,1)}), bf16[16,256,2048]{2,1,0:T(8,128)(2,1)}, u32[]{:S(2)}, u32[]{:S(2)}) %all-to-all-start.7) | async-done | bytes 16777248 | tf_op jit(solution)/shard_map/all_to_all | solution.py:327
  1382.6 44.1 %multiply_convert_fusion.2 = (bf16[4096,1408]{1,0:T(8,128)(2,1)}, bf16[4096,1408]{1,0:T(8,128)(2,1)}, bf16[4096,1408]{1,0:T(8,128)(2,1)}) fusion(f32[4096,1408]{1,0:T(8,128)} %fusion.38, f32[4096,1408]{1,0:T(8,128)} %fusion.34, bf16[4096,2048]{1,0:T(8,128)(2,1)} %bitcast.54, bf16[1,1408,2048]{2,1,0:T(8,128)(2,1)} %all-gather.37.cloned.1.call-done), kind=kOutput, calls=%fused_computation.17 | convolution fusion | flops 23708827648 | bytes 103284736 | tf_op jit(solution)/shard_map/erd,efd->erf/dot_general | solution.py:331
  1524.9 34.9 fusion.18
  1589.0 99.8 %reduce.15 = bf16[4096,2048]{1,0:T(8,128)(2,1)} reduce(bf16[4096,1,2048]{2,1,0:T(2,128)(2,1)} %bitcast.416, bf16[]{:T(256)} %broadcast.421), dimensions={1}, to_apply=%bitcast.409.reduce_sub_computation | reduce | bytes 33554432
  1709.9 69.5 %all-to-all-start.8 = ((bf16[16,2,262144]{2,1,0:T(2,128)(2,1)}), bf16[16,2,262144]{2,1,0:T(2,128)(2,1)}, u32[]{:S(2)}, u32[]{:S(2)}) async-start(bf16[16,2,262144]{2,1,0:T(2,128)(2,1)} %reshape.1005), calls=%async_computation.11 | async-start | bytes 33554432 | tf_op jit(solution)/shard_map/all_to_all | solution.py:360
  1798.4 43.7 %bitcast_reduce_fusion = bf16[2,1441792]{1,0:T(2,128)(2,1)} fusion(bf16[2,1,1441792]{2,1,0:T(2,128)(2,1)} %reshape.1004), kind=kLoop, calls=%fused_computation.233 | loop fusion | bytes 11534336 | tf_op jit(solution)/shard_map/all_to_all | solution.py:220
  1985.9 99.7 %reduce.16 = bf16[4096,2048]{1,0:T(8,128)(2,1)} reduce(bf16[4096,1,2048]{2,1,0:T(2,128)(2,1)} %bitcast.415, bf16[]{:T(256)} %broadcast.421), dimensions={1}, to_apply=%bitcast.410.reduce_sub_computation | reduce | bytes 33554432
  2106.8 39.6 all-to-all-start.6
  2222.7 220.5 %all-to-all-done.6 = bf16[16,2,262144]{2,1,0:T(2,128)(2,1)} async-done(((bf16[16,2,262144]{2,1,0:T(2,128)(2,1)}), bf16[16,2,262144]{2,1,0:T(2,128)(2,1)}, u32[]{:S(2)}, u32[]{:S(2)}) %all-to-all-start.6) | async-done | bytes 16777248 | tf_op jit(solution)/shard_map/all_to_all | solution.py:307
  2665.6 122.6 %all-gather.41.cloned.1.call-done = bf16[1,1024,2048]{1,2,0:T(8,128)(2,1)} async-done(((bf16[1,512,2048]{1,2,0:T(8,128)(2,1)}), bf16[1,1024,2048]{1,2,0:T(8,128)(2,1)}) %all-gather.41.cloned.1.call-update) | async-done | bytes 4194320 | tf_op jit(solution)/shard_map/all_gather | solution.py:141
  2825.6 47.0 %fusion.72 = f32[1,1024,8,192]{1,3,2,0:T(8,128)} fusion(f32[8,1024,1024]{1,2,0:T(8,128)} %fusion.93, f32[8,1024]{1,0:T(8,128)S(1)} %log_add_fusion, f32[8,1024,1024]{1,2,0:T(8,128)} %get-tuple-element.138, pred[1024,1024]{0,1:T(8,128)(4,1)S(1)} %copy-done.10, bf16[1024,8,32]{0,2,1:T(8,128)(2,1)} %get-tuple-element.126, ...), kind=kOutput, calls=%fused_computation.129 | convolution fusion | flops 3322946560 | bytes 77627392 | tf_op jit(solution)/shard_map/bhij,bihd->bjhd/dot_general | solution.py:131
  2872.6 48.1 %fusion.75 = f32[1,1024,8,192]{1,3,2,0:T(8,128)} fusion(f32[8,1024,1024]{1,2,0:T(8,128)} %fusion.93, f32[8,1024]{1,0:T(8,128)S(1)} %log_add_fusion, f32[8,1024,1024]{1,2,0:T(8,128)} %get-tuple-element.138, pred[1024,1024]{0,1:T(8,128)(4,1)S(1)} %copy-done.10, bf16[1,1024,8,64]{1,3,2,0:T(8,128)(2,1)} %broadcast_in_dim.25, ...), kind=kOutput, calls=%fused_computation.130 | convolution fusion | flops 3319800832 | bytes 77627392 | tf_op jit(solution)/shard_map/bhij,bjhd->bihd/dot_general | solution.py:128
  2964.9 131.0 %all_to_all.189 = bf16[2,1024,1,1408]{3,1,2,0:T(8,128)(2,1)} all-to-all(bf16[2,1024,1,1408]{3,1,2,0:T(8,128)(2,1)S(1)} %convert_bitcast_fusion.3), channel_id=1, replica_groups=mesh['dp'=2,'expert'=16] {'dp'}, dimensions={0} | all-to-all | bytes 11534336 | tf_op jit(solution)/shard_map/all_to_all | solution.py:486
  3123.8 76.9 %all_to_all.190 = bf16[2,1024,1,1408]{3,1,2,0:T(8,128)(2,1)} all-to-all(bf16[2,1024,1,1408]{3,1,2,0:T(8,128)(2,1)S(1)} %convert_bitcast_fusion.4), channel_id=1, replica_groups=mesh['dp'=2,'expert'=16] {'dp'}, dimensions={0} | all-to-all | bytes 11534336 | tf_op jit(solution)/shard_map/all_to_all | solution.py:479
  3245.1 68.2 %all_to_all.191 = bf16[2,1024,1,1408]{1,3,2,0:T(8,128)(2,1)} all-to-all(bf16[2,1024,1,1408]{1,3,2,0:T(8,128)(2,1)S(1)} %copy.315), channel_id=1, replica_groups=mesh['dp'=2,'expert'=16] {'dp'}, dimensions={0} | all-to-all | bytes 11534336 | tf_op jit(solution)/shard_map/all_to_all | solution.py:500
  3353.6 34.4 fusion.22
  3441.2 83.4 %all_to_all.192 = bf16[2,1024,1,1024]{3,1,2,0:T(8,128)(2,1)} all-to-all(bf16[2,1024,1,1024]{3,1,2,0:T(8,128)(2,1)S(1)} %convert_bitcast_fusion.6), channel_id=1, replica_groups=mesh['dp'=2,'expert'=16] {'dp'}, dimensions={0} | all-to-all | bytes 8388608 | tf_op jit(solution)/shard_map/all_to_all | solution.py:493
  3547.1 129.3 %all_to_all.193 = bf16[2,1024,1,1536]{3,1,2,0:T(8,128)(2,1)} all-to-all(bf16[2,1024,1,1536]{3,1,2,0:T(8,128)(2,1)S(1)} %convert_bitcast_fusion.1), channel_id=1, replica_groups=mesh['dp'=2,'expert'=16] {'dp'}, dimensions={0} | all-to-all | bytes 12582912 | tf_op jit(solution)/shard_map/all_to_all | solution.py:472
  3729.8 51.7 %reduce-scatter.45.cloned.1.call-done = bf16[128,512]{1,0:T(8,128)(2,1)} async-done(((bf16[2048,512]{1,0:T(8,128)(2,1)}), bf16[128,512]{1,0:T(8,128)(2,1)}) %reduce-scatter.45.cloned.1.call-update) | async-done | bytes 131088
  3783.3 74.0 %reduce-scatter.47.cloned.1.call-done = bf16[64,2048]{1,0:T(8,128)(2,1)} async-done(((bf16[1024,2048]{1,0:T(8,128)(2,1)}), bf16[64,2048]{1,0:T(8,128)(2,1)}) %reduce-scatter.47.cloned.1.call-update) | async-done | bytes 262160
  3861.4 83.8 %reduce-scatter.43.cloned.1.call-done = bf16[64,3072]{1,0:T(8,128)(2,1)} async-done(((bf16[1024,3072]{1,0:T(8,128)(2,1)}), bf16[64,3072]{1,0:T(8,128)(2,1)}) %reduce-scatter.43.cloned.1.call-update) | async-done | bytes 393232
  3955.5 41.1 %all-reduce.8 = (f32[2048]{0:T(1024)S(1)}, f32[512]{0:T(512)S(1)}, f32[2048]{0:T(1024)S(1)}) all-reduce(f32[2048]{0:T(1024)S(1)} %get-tuple-element.109, f32[512]{0:T(512)S(1)} %get-tuple-element.107, f32[2048]{0:T(1024)S(1)} %copy-done.44), channel_id=6, replica_groups=mesh['dp'=2,'expert'=16] {'dp','expert'}, use_global_device_ids=true, to_apply=%region_21.22.clone | all-reduce | flops 4608 | bytes 36864
  4013.4 77.3 %reduce-scatter.33.cloned.1.call-done = f32[64,576]{1,0:T(8,128)} async-done(((f32[2048,576]{1,0:T(8,128)}), f32[64,576]{1,0:T(8,128)}) %reduce-scatter.33.cloned.1.call-update) | async-done | bytes 147472 | tf_op jit(solution)/shard_map/reduce_scatter | solution.py:540
  (412 shorter events, 1527.7 us)
Async XLA Ops:
  7.9 119.3 %all-gather.21.cloned.1.call-start = ((), (), s32[]{:S(2)}) async-start(), calls=%async_computation.31 | async-start | bytes 6684672 | tf_op jit(solution)/shard_map/all_gather | solution.py:180
  8.7 212.3 %all-gather.15.cloned.1.call-start = ((), (), s32[]{:S(2)}) async-start(), calls=%async_computation.28 | async-start | bytes 6291456 | tf_op jit(solution)/shard_map/all_gather | solution.py:141
  60.5 226.1 %all-gather.17.cloned.1.call-start = ((), (), s32[]{:S(2)}) async-start(), calls=%async_computation.29 | async-start | bytes 2703360 | tf_op jit(solution)/shard_map/all_gather | solution.py:175
  61.1 267.6 %all-gather.19.cloned.1.call-start = ((), (), s32[]{:S(2)}) async-start(), calls=%async_computation.30 | async-start | bytes 2228224 | tf_op jit(solution)/shard_map/all_gather | solution.py:185
  203.3 188.7 %all-to-all-start = ((bf16[1024,2,1536]{2,0,1:T(8,128)(2,1)}), bf16[1024,2,1536]{2,0,1:T(8,128)(2,1)}, u32[]{:S(2)}, u32[]{:S(2)}) async-start(bf16[1024,2,1536]{2,0,1:T(8,128)(2,1)} %copy.266), calls=%async_computation | async-start | bytes 12582912 | tf_op jit(solution)/shard_map/all_to_all | solution.py:200
  209.7 360.8 %reduce-scatter.25.cloned.1.call-start = ((), (), s32[]{:S(2)}) async-start(), calls=%async_computation.33 | async-start | bytes 12582912 | tf_op jit(solution)/shard_map/reduce_scatter | solution.py:145
  602.4 370.8 %all-to-all-start.5 = ((bf16[16,256,2048]{2,1,0:T(8,128)(2,1)}), bf16[16,256,2048]{2,1,0:T(8,128)(2,1)}, u32[]{:S(2)}, u32[]{:S(2)}) async-start(bf16[16,256,2048]{2,1,0:T(8,128)(2,1)} %bitcast.420), calls=%async_computation.7 | async-start | bytes 33554432 | tf_op jit(solution)/shard_map/all_to_all | solution.py:296
  608.1 473.4 %all-gather.31.cloned.1.call-start = ((), (), s32[]{:S(2)}) async-start(), calls=%async_computation.37 | async-start | bytes 6127616 | tf_op jit(solution)/shard_map/all_gather | solution.py:184
  608.9 546.9 %all-gather.27.cloned.1.call-start = ((), (), s32[]{:S(2)}) async-start(), calls=%async_computation.35 | async-start | bytes 6127616 | tf_op jit(solution)/shard_map/all_gather | solution.py:181
  609.6 554.5 %all-gather.29.cloned.1.call-start = ((), (), s32[]{:S(2)}) async-start(), calls=%async_computation.36 | async-start | bytes 6127616 | tf_op jit(solution)/shard_map/all_gather | solution.py:182
  973.2 403.2 %all-to-all-start.7 = ((bf16[16,256,2048]{2,1,0:T(8,128)(2,1)}), bf16[16,256,2048]{2,1,0:T(8,128)(2,1)}, u32[]{:S(2)}, u32[]{:S(2)}) async-start(bf16[16,256,2048]{2,1,0:T(8,128)(2,1)} %bitcast.419), calls=%async_computation.10 | async-start | bytes 33554432 | tf_op jit(solution)/shard_map/all_to_all | solution.py:327
  1080.2 152.5 %all-gather.33.cloned.1.call-start = ((), (), s32[]{:S(2)}) async-start(), calls=%async_computation.39 | async-start | bytes 8650752 | tf_op jit(solution)/shard_map/all_gather | solution.py:188
  1080.9 301.7 %all-gather.37.cloned.1.call-start = ((), (), s32[]{:S(2)}) async-start(), calls=%async_computation.41 | async-start | bytes 8650752 | tf_op jit(solution)/shard_map/all_gather | solution.py:190
  1518.7 191.2 %all-to-all-start.4 = ((bf16[2,2,720896]{2,1,0:T(2,128)(2,1)}), bf16[2,2,720896]{2,1,0:T(2,128)(2,1)}, u32[]{:S(2)}, u32[]{:S(2)}) async-start(bf16[2,2,720896]{2,1,0:T(2,128)(2,1)} %reshape.1003), calls=%async_computation.5 | async-start | bytes 11534336 | tf_op jit(solution)/shard_map/all_to_all | solution.py:220
  1709.9 396.9 %all-to-all-start.8 = ((bf16[16,2,262144]{2,1,0:T(2,128)(2,1)}), bf16[16,2,262144]{2,1,0:T(2,128)(2,1)}, u32[]{:S(2)}, u32[]{:S(2)}) async-start(bf16[16,2,262144]{2,1,0:T(2,128)(2,1)} %reshape.1005), calls=%async_computation.11 | async-start | bytes 33554432 | tf_op jit(solution)/shard_map/all_to_all | solution.py:360
  1779.4 95.2 %all-gather.25.cloned.1.call-start = ((), (), s32[]{:S(2)}) async-start(), calls=%async_computation.34 | async-start | bytes 6291456 | tf_op jit(solution)/shard_map/all_gather | solution.py:141
  1783.7 116.9 %all-gather.39.cloned.1.call-start = ((), (), s32[]{:S(2)}) async-start(), calls=%async_computation.42 | async-start | bytes 6291456 | tf_op jit(solution)/shard_map/all_gather | solution.py:141
  2106.8 336.4 %all-to-all-start.6 = ((bf16[16,2,262144]{2,1,0:T(2,128)(2,1)}), bf16[16,2,262144]{2,1,0:T(2,128)(2,1)}, u32[]{:S(2)}, u32[]{:S(2)}) async-start(bf16[16,2,262144]{2,1,0:T(2,128)(2,1)} %reshape.1007), calls=%async_computation.8 | async-start | bytes 33554432 | tf_op jit(solution)/shard_map/all_to_all | solution.py:307
  2146.4 502.1 %reduce-scatter.29.cloned.1.call-start = ((), (), s32[]{:S(2)}) async-start(), calls=%async_computation.43 | async-start | bytes 12582912 | tf_op jit(solution)/shard_map/reduce_scatter | solution.py:145
  2159.5 495.1 %reduce-scatter.27.cloned.1.call-start = ((), (), s32[]{:S(2)}) async-start(), calls=%async_computation.38 | async-start | bytes 12582912 | tf_op jit(solution)/shard_map/reduce_scatter | solution.py:145
  2172.0 616.2 %all-gather.41.cloned.1.call-start = ((), (), s32[]{:S(2)}) async-start(), calls=%async_computation.44 | async-start | bytes 6291456 | tf_op jit(solution)/shard_map/all_gather | solution.py:141
  2665.3 1029.4 %reduce-scatter.31.cloned.1.call-start = ((), (), s32[]{:S(2)}) async-start(), calls=%async_computation.45 | async-start | bytes 16121856 | tf_op jit(solution)/shard_map/reduce_scatter | solution.py:145
  2953.7 750.8 %reduce-scatter.51.cloned.1.call-start = ((), (), s32[]{:S(2)}) async-start(), calls=%async_computation.55 | async-start | bytes 6127616
  3112.7 594.3 %reduce-scatter.49.cloned.1.call-start = ((), (), s32[]{:S(2)}) async-start(), calls=%async_computation.54 | async-start | bytes 6127616
  3217.4 492.0 %reduce-scatter.35.cloned.1.call-start = ((), (), s32[]{:S(2)}) async-start(), calls=%async_computation.47 | async-start | bytes 6127616 | tf_op jit(solution)/shard_map/reduce_scatter | solution.py:524
  3321.7 389.6 %reduce-scatter.41.cloned.1.call-start = ((), (), s32[]{:S(2)}) async-start(), calls=%async_computation.50 | async-start | bytes 8650752 | tf_op jit(solution)/shard_map/reduce_scatter | solution.py:373
  3353.5 362.9 %reduce-scatter.39.cloned.1.call-start = ((), (), s32[]{:S(2)}) async-start(), calls=%async_computation.49 | async-start | bytes 8650752 | tf_op jit(solution)/shard_map/reduce_scatter | solution.py:370
  3388.0 333.1 %reduce-scatter.37.cloned.1.call-start = ((), (), s32[]{:S(2)}) async-start(), calls=%async_computation.48 | async-start | bytes 8650752 | tf_op jit(solution)/shard_map/reduce_scatter | solution.py:367
  3422.4 359.1 %reduce-scatter.45.cloned.1.call-start = ((), (), s32[]{:S(2)}) async-start(), calls=%async_computation.52 | async-start | bytes 2228224
  3434.0 423.2 %reduce-scatter.47.cloned.1.call-start = ((), (), s32[]{:S(2)}) async-start(), calls=%async_computation.53 | async-start | bytes 4456448
  3537.5 407.7 %reduce-scatter.43.cloned.1.call-start = ((), (), s32[]{:S(2)}) async-start(), calls=%async_computation.51 | async-start | bytes 6684672
  3694.0 396.8 %reduce-scatter.33.cloned.1.call-start = ((), (), s32[]{:S(2)}) async-start(), calls=%async_computation.46 | async-start | bytes 5406720 | tf_op jit(solution)/shard_map/reduce_scatter | solution.py:540
  (75 other events, 2314.6 us)
Sparse Core Ops, SparseCore 0:
  10.2 54.3 all-gather.22
  66.9 60.3 all-gather.20
  129.4 91.5 all-gather.14
  223.7 62.8 all-gather.16
  288.6 40.0 all-gather.18
  472.2 98.2 reduce-scatter.24
  611.5 262.5 all-gather.30
  876.7 100.0 all-gather.26
  979.3 72.8 all-gather.28
  1081.7 74.8 all-gather.34
  1158.2 74.4 all-gather.32
  1234.2 74.4 all-gather.36
  1783.8 58.4 all-gather.24
  1843.8 56.7 all-gather.38
  2159.6 100.9 reduce-scatter.28
  2262.8 99.2 reduce-scatter.26
  2665.5 122.7 all-gather.40
  2953.8 195.1 reduce-scatter.30
  3154.0 81.9 reduce-scatter.50
  3240.9 80.6 reduce-scatter.48
  3326.6 80.7 reduce-scatter.34
  3409.7 102.1 reduce-scatter.40
  3514.3 104.9 reduce-scatter.38
  3621.5 94.6 reduce-scatter.36
  3719.9 61.5 reduce-scatter.44
  3785.7 71.4 reduce-scatter.46
  3861.0 84.1 reduce-scatter.42
  3948.2 142.5 reduce-scatter.32
where the time goes:
time: 4120 us; the launch traced here: 4100 us
  waiting for transfers between devices  1340 us (33%)
  local copies, waits for them, and re-layouts  841 us (20%)
  matrix products  653 us (16%)
  blocking collectives  573 us (14%)
  other arithmetic  421 us (10%)
  starting transfers between devices  253 us (6%)
    unnamed x182, local copies, waits for them, and re-layouts  281 us
    unnamed x6, other arithmetic  274 us
    all_to_all x1, waiting for transfers between devices, local(): lax.all_to_all(send_rows, 'expert', split_axis=0, concat_axis=1, tiled=True)  255 us
    all_to_all x1, waiting for transfers between devices, local(): lax.all_to_all(out_exp, 'expert', split_axis=1, concat_axis=0, tiled=True)  221 us
    unnamed x33, waiting for transfers between devices  217 us
    all_gather x4, waiting for transfers between devices, whole_sequence(): return lax.all_gather(part_rows, 'dp', axis=1, tiled=True)  139 us
    all_to_all x1, blocking collectives, local(): lax.all_to_all(grad_sup.reshape(dp_count, -1, 1, grad_sup.shape[1]).astyp...  131 us
    all_to_all x1, blocking collectives, local(): lax.all_to_all(grad_query.reshape(dp_count, -1, 1, grad_query.shape[1]).a...  129 us
  transfers between devices with their start and end apart: 37, of which 19 were waited for; matrix products, arithmetic and copies ran while one was open for 39% of the time, Pallas kernels for 0%

commit v1 on v0

v1 whole, which is shorter than its diff:
```python
import functools

import jax
import jax.numpy as jnp
from jax import lax
from jax.experimental import pallas as pl
from jax.experimental.pallas import tpu as pltpu
from jax.sharding import PartitionSpec as P

NOPE = 128
ROPE = 64
VDIM = 128
RANK = 512
DOC = 512
epsilon = 1e-06
f32 = jnp.float32
bf16 = jnp.bfloat16
MIB = 1 << 20


def mm(spec, a, b):
    return jnp.einsum(spec, a, b, preferred_element_type=f32)


def dot(a, b, ca, cb):
    return lax.dot_general(a, b, (((ca,), (cb,)), ((), ())), preferred_element_type=f32)


def after(values, earlier):
    return lax.optimization_barrier((values, earlier))[0]


def rotate(values, cosine, sine):
    half = values.shape[-1] // 2
    a, b = values[..., :half], values[..., half:]
    return jnp.concatenate([a * cosine - b * sine, b * cosine + a * sine], axis=-1)


def rotate_back(values, cosine, sine):
    return rotate(values, cosine, -sine)


def norm_back(gradient, normed, scale_vec, gain_vec):
    scaled = gradient * gain_vec
    inner = jnp.mean(scaled * normed, axis=-1, keepdims=True)
    return scale_vec * (scaled - normed * inner), jnp.sum(gradient * normed, axis=0)


def silu_parts(gate_in):
    sig = jax.nn.sigmoid(gate_in)
    return gate_in * sig, sig * (1.0 + gate_in * (1.0 - sig))


def rotary_tables(positions):
    frequency = jnp.power(10000.0, -jnp.arange(ROPE // 2).astype(f32) * 2.0 / ROPE)
    angles = positions.astype(f32)[:, None] * frequency[None, :]
    return jnp.cos(angles), jnp.sin(angles)


def window_start(block, rows, length, seq, reach):
    first = lax.axis_index("dp") * length + block * rows - DOC
    return jnp.clip(first, 0, seq - reach)


def swap_halves(values):
    lane = lax.broadcasted_iota(jnp.int32, values.shape, 1)
    up = pltpu.roll(values, ROPE // 2, 1)
    down = pltpu.roll(values, 2 * ROPE - ROPE // 2, 1)
    return jnp.where(lane % ROPE < ROPE // 2, down, up)


def head_lanes(shape, head):
    lane = lax.broadcasted_iota(jnp.int32, shape, 1)
    return (lane // ROPE) == head


def probabilities(q, qr, k, kr, bias):
    scores = (dot(q, k, 1, 1) + dot(qr, kr, 1, 1)) * (NOPE + ROPE) ** (-0.5) + bias
    exponent = jnp.exp(scores - jnp.max(scores, axis=-1, keepdims=True))
    return exponent / jnp.sum(exponent, axis=-1, keepdims=True)


def attend_kernel(sizes, nope_ref, rope_ref, cos_ref, sin_ref, kv_ref, kr_ref, bias_ref, out_ref):
    blocks, rows, length, seq, reach = sizes
    for block in range(blocks):
        at = pl.ds(block * rows, rows)
        rope = rope_ref[at, :]
        rope = (rope * cos_ref[at, :] + swap_halves(rope) * sin_ref[at, :]).astype(bf16)
        start = pl.multiple_of(window_start(block, rows, length, seq, reach), 128)
        span = pl.ds(start, reach)
        kr = kr_ref[span, :]
        for head in range(2):
            qr = jnp.where(head_lanes(rope.shape, head), rope, jnp.zeros_like(rope))
            q = nope_ref[at, head * NOPE : (head + 1) * NOPE].astype(bf16)
            k = kv_ref[span, head * 256 : head * 256 + NOPE]
            v = kv_ref[span, head * 256 + NOPE : (head + 1) * 256]
            probs = probabilities(q, qr, k, kr, bias_ref[block])
            out_ref[at, head * VDIM : (head + 1) * VDIM] = dot(
                probs.astype(bf16), v, 1, 0
            ).astype(bf16)


def attend_back_kernel(
    sizes,
    nope_ref,
    rope_ref,
    cos_ref,
    sin_ref,
    kv_ref,
    kr_ref,
    bias_ref,
    grad_ref,
    dnope_ref,
    drope_ref,
    dkv_ref,
    dkr_ref,
    dk_acc,
    dv_acc,
):
    blocks, rows, length, seq, reach = sizes
    factor = (NOPE + ROPE) ** (-0.5)

    @pl.when(pl.program_id(0) == 0)
    def _():
        dkr_ref[...] = jnp.zeros_like(dkr_ref)

    dk_acc[...] = jnp.zeros_like(dk_acc)
    dv_acc[...] = jnp.zeros_like(dv_acc)
    for block in range(blocks):
        at = pl.ds(block * rows, rows)
        rope = rope_ref[at, :]
        rope = (rope * cos_ref[at, :] + swap_halves(rope) * sin_ref[at, :]).astype(bf16)
        start = pl.multiple_of(window_start(block, rows, length, seq, reach), 128)
        span = pl.ds(start, reach)
        kr = kr_ref[span, :]
        rope_grad = jnp.zeros((rows, 2 * ROPE), f32)
        for head in range(2):
            mine = head_lanes(rope.shape, head)
            qr = jnp.where(mine, rope, jnp.zeros_like(rope))
            q = nope_ref[at, head * NOPE : (head + 1) * NOPE].astype(bf16)
            k = kv_ref[span, head * 256 : head * 256 + NOPE]
            v = kv_ref[span, head * 256 + NOPE : (head + 1) * 256]
            grad = grad_ref[at, head * VDIM : (head + 1) * VDIM]
            probs = probabilities(q, qr, k, kr, bias_ref[block])
            dprobs = dot(grad, v, 1, 1)
            inner = jnp.sum(dprobs * probs, axis=-1, keepdims=True)
            dscores = (probs * (dprobs - inner) * factor).astype(bf16)
            dnope_ref[at, head * NOPE : (head + 1) * NOPE] = dot(dscores, k, 1, 0).astype(bf16)
            rope_grad += jnp.where(mine, dot(dscores, kr, 1, 0), 0.0)
            dk_acc[head, span, :] += dot(dscores, q, 0, 0)
            dv_acc[head, span, :] += dot(probs.astype(bf16), grad, 0, 0)
            dkr_ref[span, :] += dot(dscores, qr, 0, 0)
        rope_grad = rope_grad * cos_ref[at, :] - swap_halves(rope_grad) * sin_ref[at, :]
        drope_ref[at, :] = rope_grad.astype(bf16)
    for head in range(2):
        dkv_ref[:, head * 256 : head * 256 + NOPE] = dk_acc[head].astype(bf16)
        dkv_ref[:, head * 256 + NOPE : (head + 1) * 256] = dv_acc[head].astype(bf16)


def attention_sizes(length, seq):
    rows = min(256, length)
    return length // rows, rows, length, seq, min(seq, rows + DOC)


def attention_specs(length, seq, heads, sizes):
    first_rope = heads * NOPE // (2 * ROPE)
    whole = lambda shape: pl.BlockSpec(shape, lambda p: (0,) * len(shape))
    return [
        pl.BlockSpec((length, 2 * NOPE), lambda p: (0, p)),
        pl.BlockSpec((length, 2 * ROPE), lambda p: (0, first_rope + p)),
        whole((length, 2 * ROPE)),
        whole((length, 2 * ROPE)),
        pl.BlockSpec((seq, 2 * (NOPE + VDIM)), lambda p: (0, p)),
        whole((seq, 2 * ROPE)),
        whole((sizes[0], sizes[1], sizes[4])),
    ]


def attend(linear, tables, kv, kr, bias, heads):
    length, seq = linear.shape[0], kv.shape[0]
    sizes = attention_sizes(length, seq)
    return pl.pallas_call(
        functools.partial(attend_kernel, sizes),
        grid=(heads // 2,),
        in_specs=attention_specs(length, seq, heads, sizes),
        out_specs=pl.BlockSpec((length, 2 * VDIM), lambda p: (0, p)),
        out_shape=jax.ShapeDtypeStruct((length, heads * VDIM), bf16),
        compiler_params=pltpu.CompilerParams(vmem_limit_bytes=48 * MIB),
        name="attend",
    )(linear, linear, *tables, kv, kr, bias)


def attend_back(linear, tables, kv, kr, bias, grad, heads):
    length, seq = linear.shape[0], kv.shape[0]
    sizes = attention_sizes(length, seq)
    return pl.pallas_call(
        functools.partial(attend_back_kernel, sizes),
        grid=(heads // 2,),
        in_specs=attention_specs(length, seq, heads, sizes)
        + [pl.BlockSpec((length, 2 * VDIM), lambda p: (0, p))],
        out_specs=[
            pl.BlockSpec((length, 2 * NOPE), lambda p: (0, p)),
            pl.BlockSpec((length, 2 * ROPE), lambda p: (0, p)),
            pl.BlockSpec((seq, 2 * (NOPE + VDIM)), lambda p: (0, p)),
            pl.BlockSpec((seq, 2 * ROPE), lambda p: (0, 0)),
        ],
        out_shape=[
            jax.ShapeDtypeStruct((length, heads * NOPE), bf16),
            jax.ShapeDtypeStruct((length, heads * ROPE), bf16),
            jax.ShapeDtypeStruct((seq, heads * (NOPE + VDIM)), bf16),
            jax.ShapeDtypeStruct((seq, 2 * ROPE), f32),
        ],
        scratch_shapes=[pltpu.VMEM((2, seq, NOPE), f32), pltpu.VMEM((2, seq, VDIM), f32)],
        compiler_params=pltpu.CompilerParams(vmem_limit_bytes=48 * MIB),
        name="attend_back",
    )(linear, linear, *tables, kv, kr, bias, grad)


def one_hot(place_ref, slots):
    place = place_ref[0]
    slot = lax.broadcasted_iota(jnp.int32, (slots, place.shape[1]), 0)
    return slot == place


def width_parts(refs, width):
    step = width // len(refs)
    return [(ref, pl.ds(i * step, step)) for i, ref in enumerate(refs)]


def forward_kernel(n, slots, place_ref, rows_ref, *refs):
    weights, shared, outs = refs[:n], refs[n : 2 * n], refs[2 * n :]
    picked_ref, act_ref, up_slope_ref, silu_ref, act_s_ref, up_slope_s_ref, silu_s_ref = outs
    width = rows_ref.shape[-1]
    picks = one_hot(place_ref, slots).astype(f32).astype(bf16)
    picked_ref[0] = dot(picks, rows_ref[0], 1, 0).astype(bf16)
    both = total([dot(picked_ref[0, :, at], w[...], 1, 0) for w, at in width_parts(weights, width)])
    half = both.shape[1] // 2
    silu, slope = silu_parts(both[:, :half])
    up = both[:, half:]
    act_ref[0] = (silu * up).astype(bf16)
    up_slope_ref[0] = (up * slope).astype(bf16)
    silu_ref[0] = silu.astype(bf16)
    both = total([dot(rows_ref[0, :, at], w[...], 1, 0) for w, at in width_parts(shared, width)])
    half = both.shape[1] // 2
    silu, slope = silu_parts(both[:, :half])
    up = both[:, half:]
    act_s_ref[0] = (silu * up).astype(bf16)
    up_slope_s_ref[0] = (up * slope).astype(bf16)
    silu_s_ref[0] = silu.astype(bf16)


def backward_kernel(
    n, slots, place_ref, weight_ref, grads_ref, us_ref, silu_ref, us_s_ref, silu_s_ref, *refs
):
    gate_up, down, gate_up_s, down_s = (refs[i * n : (i + 1) * n] for i in range(4))
    picked_ref, d_gate_ref, d_up_ref, d_shared_ref, d_rows_ref = refs[4 * n :]
    width = grads_ref.shape[-1]
    hot = one_hot(place_ref, slots)
    slot_weight = jnp.sum(jnp.where(hot, weight_ref[0], 0.0), axis=1, keepdims=True)
    picks = hot.astype(f32).astype(bf16)
    picked_ref[0] = (dot(picks, grads_ref[0], 1, 0) * slot_weight).astype(bf16)
    d_act = total([dot(picked_ref[0, :, at], w[...], 1, 1) for w, at in width_parts(down, width)])
    d_gate = (d_act * us_ref[0].astype(f32)).astype(bf16)
    d_up = (d_act * silu_ref[0].astype(f32)).astype(bf16)
    d_gate_ref[0] = d_gate
    d_up_ref[0] = d_up
    d_both = jnp.concatenate([d_gate, d_up], axis=1)
    d_act = total([dot(grads_ref[0, :, at], w[...], 1, 0) for w, at in width_parts(down_s, width)])
    half = d_act.shape[1]
    d_shared_ref[0, :, :half] = (d_act * us_s_ref[0].astype(f32)).astype(bf16)
    d_shared_ref[0, :, half:] = (d_act * silu_s_ref[0].astype(f32)).astype(bf16)
    for (w, at), w_s in zip(width_parts(gate_up, width), gate_up_s):
        d_row = dot(d_both, w[...], 1, 1).astype(bf16)
        d_rows_ref[0, :, at] = (
            dot(picks, d_row, 0, 0) + dot(d_shared_ref[0], w_s[...], 1, 1)
        ).astype(bf16)


def output_kernel(n, slots, place_ref, weight_ref, act_ref, act_s_ref, *refs):
    down, down_s, out_ref = refs[:n], refs[n : 2 * n], refs[2 * n]
    width = out_ref.shape[-1]
    hot = one_hot(place_ref, slots)
    slot_weight = jnp.sum(jnp.where(hot, weight_ref[0], 0.0), axis=1, keepdims=True)
    picks = hot.astype(f32).astype(bf16)
    for (w, at), w_s in zip(width_parts(down, width), down_s):
        out = (dot(act_ref[0], w[...], 1, 0) * slot_weight).astype(bf16)
        out_ref[0, :, at] = (
            dot(picks, out, 0, 0) + dot(act_s_ref[0], w_s[...], 1, 1)
        ).astype(bf16)


def by_block(kernel, name, blocked, fixed, outs, flops):
    count = blocked[0].shape[0]
    block = lambda a: pl.BlockSpec((1, *a.shape[1:]), lambda b: (b, 0, 0))
    stay = lambda a: pl.BlockSpec(a.shape, lambda b: (0, 0), pipeline_mode=pl.Buffered(1))
    moved = sum(a.size * a.dtype.itemsize for a in (*blocked, *fixed, *outs))
    return pl.pallas_call(
        kernel,
        grid=(count,),
        in_specs=[block(a) for a in blocked] + [stay(a) for a in fixed],
        out_specs=[block(a) for a in outs],
        out_shape=outs,
        compiler_params=pltpu.CompilerParams(vmem_limit_bytes=60 * MIB),
        cost_estimate=pl.CostEstimate(flops=flops, bytes_accessed=moved, transcendentals=0),
        name=name,
    )(*blocked, *fixed)


def add_rows(into, left, right):
    step = 16
    lead = (slice(None),) * (len(into.shape) - 2)

    @pl.loop(0, into.shape[-2] // step)
    def _(i):
        at = (*lead, pl.ds(pl.multiple_of(i * step, step), step), slice(None))
        into[at] = (left[at].astype(f32) + right[at].astype(f32)).astype(into.dtype)


def grad_sum_kernel(chunks, n, *refs):
    ins, outs = refs[:n], refs[n : 2 * n]
    own, got, load_sem, send_sem, recv_sem = refs[2 * n], refs[2 * n + 1 : 2 * n + 6], *refs[2 * n + 6 :]
    dp, expert = lax.axis_index("dp"), lax.axis_index("expert")
    core, y = expert % 2, (expert // 2) % 2
    z_low, z_high = (expert // 4) % 2, expert // 8
    partners = [
        {"expert": expert + 1 - 2 * core},
        {"dp": 1 - dp},
        {"expert": expert + 2 - 4 * y},
        {"expert": expert + 4 - 8 * z_low},
        {"expert": expert + 8 - 16 * z_high},
    ]
    barrier = pltpu.get_barrier_semaphore()
    for partner in partners:
        pl.semaphore_signal(barrier, inc=1, device_id=partner, device_id_type=pl.DeviceIdType.MESH)
    pl.semaphore_wait(barrier, len(partners))
    count = len(chunks)

    def source(k, which):
        array, start, wide = chunks[k]
        return ins[array].at[:, :, :, :, which, :, pl.ds(start, wide)]

    def cut(ref, k):
        return ref.at[(slice(None),) * (len(ref.shape) - 1) + (pl.ds(0, chunks[k][2]),)]

    def send(stage, k, values):
        return pltpu.make_async_remote_copy(
            src_ref=values,
            dst_ref=cut(got[stage].at[k], k),
            send_sem=send_sem.at[stage, k],
            recv_sem=recv_sem.at[stage, k],
            device_id=partners[stage],
            device_id_type=pl.DeviceIdType.MESH,
        )

    def load(k):
        return pltpu.make_async_copy(source(k, core), cut(own.at[k % 2], k), load_sem.at[k % 2])

    copies = {}

    def start(stage, k, values):
        copies[stage, k] = send(stage, k, values)
        copies[stage, k].start()

    for k in range(count):
        start(0, k, source(k, 1 - core))
    for k in range(min(2, count)):
        load(k).start()
    for turn in range(count + 4):
        k = turn
        if k < count:
            load(k).wait()
            copies[0, k].wait_recv()
            held, mine = cut(got[0].at[k], k), cut(own.at[k % 2], k)
            add_rows(held.at[1 - dp], held.at[1 - dp], mine.at[1 - dp])
            start(1, k, held.at[1 - dp])
            add_rows(held.at[dp], held.at[dp], mine.at[dp])
            if k + 2 < count:
                load(k + 2).start()
        k = turn - 1
        if 0 <= k < count:
            copies[1, k].wait_recv()
            held = cut(got[1].at[k], k)
            add_rows(held, held, cut(got[0].at[k], k).at[dp])
            start(2, k, held.at[:, :, 1 - y])
        k = turn - 2
        if 0 <= k < count:
            copies[2, k].wait_recv()
            held = cut(got[2].at[k], k)
            add_rows(held, held, cut(got[1].at[k], k).at[:, :, y])
            start(3, k, held.at[:, 1 - z_low])
        k = turn - 3
        if 0 <= k < count:
            copies[3, k].wait_recv()
            held = cut(got[3].at[k], k)
            add_rows(held, held, cut(got[2].at[k], k).at[:, z_low])
            start(4, k, held.at[1 - z_high])
        k = turn - 4
        if 0 <= k < count:
            copies[4, k].wait_recv()
            array, first, wide = chunks[k]
            add_rows(
                outs[array].at[:, pl.ds(first, wide)],
                cut(got[4].at[k], k),
                cut(got[3].at[k], k).at[z_high],
            )
    for copy in copies.values():
        copy.wait_send()


def grad_sums(arrays):
    shards = 32
    rows, piece = arrays[0].shape[0] // shards, 1024
    chunks = [
        (i, at, min(piece, a.shape[1] - at))
        for i, a in enumerate(arrays)
        for at in range(0, a.shape[1], piece)
    ]
    dims = (2, 2, 2, 2)
    count = len(chunks)
    return pl.pallas_call(
        functools.partial(grad_sum_kernel, chunks, len(arrays)),
        in_specs=[pl.BlockSpec(memory_space=pl.ANY)] * len(arrays),
        out_specs=[pl.BlockSpec(memory_space=pltpu.VMEM)] * len(arrays),
        out_shape=[jax.ShapeDtypeStruct((rows, a.shape[1]), f32) for a in arrays],
        scratch_shapes=[
            pltpu.VMEM((2, *dims, rows, piece), bf16),
            *[pltpu.VMEM((count, *dims[i:], rows, piece), bf16) for i in range(5)],
            pltpu.SemaphoreType.DMA((2,)),
            pltpu.SemaphoreType.DMA((5, count)),
            pltpu.SemaphoreType.DMA((5, count)),
        ],
        compiler_params=pltpu.CompilerParams(
            collective_id=1, has_side_effects=True, vmem_limit_bytes=52 * MIB
        ),
        name="grad_sums",
    )(*[a.reshape(*dims, 2, rows, a.shape[1]) for a in arrays])


def swap(values):
    return lax.ppermute(values, "dp", [(0, 1), (1, 0)])


def turned(values, dp_count):
    if dp_count != 2:
        return values
    half = values.shape[-1] // 2
    a, b = values[..., :half], values[..., half:]
    first = lax.axis_index("dp") == 0
    return jnp.concatenate([jnp.where(first, a, b), jnp.where(first, b, a)], axis=-1)


def weight_parts(values, axis, dp_count):
    if dp_count != 2:
        return [lax.all_gather(values, "dp", axis=axis, tiled=True)]
    return [values, swap(values)]


def scatter_dp(results, axis):
    if len(results) == 1:
        return lax.psum_scatter(
            results[0]().astype(bf16), "dp", scatter_dimension=axis, tiled=True
        ).astype(f32)
    sent = swap(results[1]().astype(bf16))
    return results[0]() + sent.astype(f32)


def total(terms):
    return functools.reduce(jnp.add, terms)


def heads_apart(values, heads):
    by_head = values.reshape(-1, heads, NOPE + ROPE)
    rows = values.shape[0]
    return jnp.concatenate(
        [by_head[..., :NOPE].reshape(rows, -1), by_head[..., NOPE:].reshape(rows, -1)], axis=1
    )


def heads_together(values, heads):
    rows = values.shape[0]
    nope = values[:, : heads * NOPE].reshape(rows, heads, NOPE)
    rope = values[:, heads * NOPE :].reshape(rows, heads, ROPE)
    return jnp.concatenate([nope, rope], axis=-1).reshape(rows, -1)


def local(
    tokens,
    segments,
    routes,
    combine,
    input_gain,
    query_weight,
    latent_weight,
    latent_gain,
    expand_weight,
    output_weight,
    middle_gain,
    shared_gate,
    shared_up,
    shared_down,
    expert_gate,
    expert_up,
    expert_down,
    cotangent,
):
    _, length, width = tokens.shape
    seq = segments.shape[1]
    top_k = routes.shape[2]
    dp_count = lax.axis_size("dp")
    groups = lax.axis_size("expert")
    shards = dp_count * groups
    both = ("dp", "expert")
    hidden_s = shared_gate.shape[1]
    part_s = hidden_s // groups
    slots = length * top_k * 4 // (groups * 3)
    offset = lax.axis_index("dp") * length
    query_width = query_weight.shape[1]
    heads = query_width // (NOPE + ROPE)
    rows_w = query_weight.shape[0]

    g1 = input_gain.shape[0]
    gains = jnp.concatenate([input_gain, middle_gain, latent_gain])
    gains = lax.all_gather(gains, both, axis=0, tiled=False)
    first_gain = gains[:, :g1].reshape(-1).astype(f32)
    second_gain = gains[:, g1 : 2 * g1].reshape(-1).astype(f32)
    latent_norm = gains[:, 2 * g1 :].reshape(-1).astype(f32)

    hits = routes[0][:, None, :] == jnp.arange(groups, dtype=jnp.int32)[None, :, None]
    dense = jnp.sum(jnp.where(hits, combine[0][:, None, :], 0.0), axis=-1)
    dense = jnp.where(jnp.any(hits, axis=-1), dense, -1.0)
    my_weights = lax.all_to_all(dense.T, "expert", split_axis=0, concat_axis=0, tiled=True)
    chosen = my_weights >= 0.0
    before = jnp.arange(length)[:, None] < jnp.arange(length)[None, :]
    place = mm("bt,ts->bs", chosen.astype(bf16), before.astype(bf16)).astype(jnp.int32)
    place = jnp.where(chosen, place, -1)
    place = place[:, None, :]
    row_weights = my_weights[:, None, :]

    expand_rows = expand_weight.T.shape[0]
    split = expand_rows // rows_w
    expand_wide = jnp.concatenate(jnp.split(expand_weight.T, split, axis=0), axis=1)
    gathered = lax.all_gather(
        jnp.concatenate([heads_apart(query_weight, heads), latent_weight, expand_wide], axis=1),
        both,
        axis=0,
        tiled=True,
    )
    linear_width = query_width + RANK + ROPE
    query_latent = gathered[:, :linear_width]
    expand_t = (
        gathered[:, linear_width:]
        .reshape(shards, rows_w, split, RANK)
        .transpose(0, 2, 1, 3)
        .reshape(-1, RANK)
    )
    output_t = lax.all_gather(output_weight.T, both, axis=0, tiled=True)

    shared_own = jnp.stack(
        [
            shared_gate.reshape(rows_w, groups, part_s),
            shared_up.reshape(rows_w, groups, part_s),
            shared_down.T.reshape(rows_w, groups, part_s),
        ],
        axis=1,
    ).transpose(2, 0, 1, 3)
    shared_cols = lax.all_to_all(shared_own, "expert", split_axis=0, concat_axis=0, tiled=True)
    shared_cols = weight_parts(shared_cols.reshape(groups * rows_w, 3 * part_s), 0, dp_count)
    padded_s = -(-part_s // 128) * 128
    wide_s = [
        jnp.pad(c.reshape(-1, 3, part_s), ((0, 0), (0, 0), (0, padded_s - part_s)))
        for c in shared_cols
    ]
    gate_up_s = [c[:, :2].reshape(-1, 2 * padded_s) for c in wide_s]
    down_s_t = [c[:, 2] for c in wide_s]

    first_gain, my_weights, gate_up_s, down_s_t, query_latent = lax.optimization_barrier(
        (first_gain, my_weights, gate_up_s, down_s_t, query_latent)
    )
    own_e = after((expert_gate[0], expert_up[0], expert_down[0]), query_latent)
    gate_up_e = weight_parts(jnp.concatenate(own_e[:2], axis=1), 0, dp_count)
    down_e = weight_parts(own_e[2], 1, dp_count)

    token_values = tokens[0].astype(f32)
    scale_one = lax.rsqrt(jnp.mean(token_values * token_values, axis=-1, keepdims=True) + epsilon)
    normed_one = token_values * scale_one
    normed_low = (normed_one * first_gain).astype(bf16)
    own_pos = offset + jnp.arange(length, dtype=jnp.int32)
    cosine, sine = rotary_tables(own_pos)
    tables = (
        jnp.concatenate([cosine] * 4, axis=1),
        jnp.concatenate([-sine, sine, -sine, sine], axis=1),
    )
    linear = mm("rd,dk->rk", normed_low, query_latent)
    latent_raw = linear[:, query_width : query_width + RANK]
    latent_scale = lax.rsqrt(jnp.mean(latent_raw * latent_raw, axis=-1, keepdims=True) + epsilon)
    latent_normed = latent_raw * latent_scale
    latent_low = (latent_normed * latent_norm).astype(bf16)
    rope_low = rotate(linear[:, query_width + RANK :], cosine, sine).astype(bf16)
    latent_rope = jnp.concatenate([latent_low, rope_low], axis=-1)
    if dp_count == 2:
        other = swap(latent_rope)
        is_first = lax.axis_index("dp") == 0
        latent_rope = jnp.concatenate(
            [jnp.where(is_first, latent_rope, other), jnp.where(is_first, other, latent_rope)]
        )
    else:
        latent_rope = lax.all_gather(latent_rope, "dp", axis=0, tiled=True)
    latent_all = latent_rope[:, :RANK]
    rope_keys = jnp.concatenate([latent_rope[:, RANK:]] * 2, axis=1)
    expanded = mm("rc,kc->rk", latent_all, expand_t).astype(bf16)
    blocks, block_rows, _, _, reach = attention_sizes(length, seq)
    bias = []
    for block in range(blocks):
        start = window_start(block, block_rows, length, seq, reach)
        q_pos = offset + block * block_rows + jnp.arange(block_rows)
        q_seg = lax.dynamic_slice_in_dim(segments[0], offset + block * block_rows, block_rows)
        k_seg = lax.dynamic_slice_in_dim(segments[0], start, reach)
        seen = (q_seg[:, None] == k_seg[None, :]) & (
            q_pos[:, None] >= (start + jnp.arange(reach))[None, :]
        )
        bias.append(jnp.where(seen, 0.0, -1e30).astype(f32))
    bias = jnp.stack(bias)
    mixed = attend(linear, tables, expanded, rope_keys, bias, heads)
    middle = token_values + mm("rv,dv->rd", mixed, output_t)
    scale_two = lax.rsqrt(jnp.mean(middle * middle, axis=-1, keepdims=True) + epsilon)
    normed_two = middle * scale_two
    ffn_rows = (normed_two * second_gain).astype(bf16)

    def gather_rows(values):
        return lax.all_gather(values, "expert", axis=0, tiled=False)

    grads_all = gather_rows(turned(cotangent[0], dp_count))
    rows_all = gather_rows(turned(ffn_rows, dp_count))

    n = len(gate_up_e)
    hidden = expert_gate.shape[2]
    block_of = lambda rows, columns: jax.ShapeDtypeStruct((groups, rows, columns), bf16)
    wide = [block_of(slots, hidden)] * 3
    wide_shared = [block_of(length, padded_s)] * 3
    unit = 2 * groups * width
    picked, act_e, up_slope, silu, act_s, up_slope_s, silu_s = by_block(
        functools.partial(forward_kernel, n, slots),
        "experts_forward",
        [place, rows_all],
        [*gate_up_e, *gate_up_s],
        [block_of(slots, width), *wide, *wide_shared],
        unit * (slots * (length + 2 * hidden) + 2 * length * padded_s),
    )
    picked_grad, d_gate, d_up, d_shared, d_rows_part = by_block(
        functools.partial(backward_kernel, n, slots),
        "experts_backward",
        [place, row_weights, grads_all, up_slope, silu, up_slope_s, silu_s],
        [*gate_up_e, *down_e, *gate_up_s, *down_s_t],
        [
            block_of(slots, width),
            *wide[:2],
            block_of(length, 2 * padded_s),
            block_of(length, width),
        ],
        unit * (slots * (2 * length + 3 * hidden) + 3 * length * padded_s),
    )
    [out_part] = by_block(
        functools.partial(output_kernel, n, slots),
        "experts_output",
        [place, row_weights, act_e, act_s],
        [*down_e, *down_s_t],
        [block_of(length, width)],
        unit * (slots * (length + hidden) + length * padded_s),
    )

    def flat(values):
        return values.reshape(-1, values.shape[-1])

    def scatter_rows(values):
        return lax.psum_scatter(flat(values), "expert", scatter_dimension=0, tiled=True)

    d_rows = scatter_rows(d_rows_part)

    column_parts = lambda values: jnp.split(flat(values), n, axis=1)
    picked, picked_grad, rows_parts, grads_parts = map(
        column_parts, (picked, picked_grad, rows_all, grads_all)
    )
    act_e, act_s, d_gate, d_up, d_shared = map(flat, (act_e, act_s, d_gate, d_up, d_shared))
    grad_gate_e = scatter_dp([lambda p=p: mm("rd,rf->df", p, d_gate) for p in picked], 0)
    grad_up_e = scatter_dp([lambda p=p: mm("rd,rf->df", p, d_up) for p in picked], 0)
    grad_down_e = scatter_dp([lambda p=p: mm("rf,rd->fd", act_e, p) for p in picked_grad], 1)
    grad_s = scatter_dp(
        [
            lambda r=r, g=g: jnp.concatenate(
                [mm("rd,rf->df", r, d_shared), mm("rd,rf->df", g, act_s)], axis=1
            )
            for r, g in zip(rows_parts, grads_parts)
        ],
        0,
    )
    grad_s = grad_s.reshape(groups, rows_w, 3, padded_s)[..., :part_s].astype(bf16)
    grad_s = lax.all_to_all(grad_s, "expert", split_axis=0, concat_axis=0, tiled=True)
    grad_s = grad_s.transpose(2, 1, 0, 3).reshape(3, rows_w, hidden_s).astype(f32)
    d_rows, grad_gate_e, grad_up_e, grad_down_e, grad_s, out_part = lax.optimization_barrier(
        (d_rows, grad_gate_e, grad_up_e, grad_down_e, grad_s, out_part)
    )
    d_rows_own = turned(d_rows, dp_count).astype(f32)

    out_grad = cotangent[0].astype(f32)
    middle_part, second_gain_grad = norm_back(d_rows_own, normed_two, scale_two, second_gain)
    middle_grad = out_grad + middle_part
    attn_grad = middle_grad.astype(bf16)
    mixed_grad = mm("rd,dv->rv", attn_grad, output_t).astype(bf16)
    grad_out_t = mm("rd,rv->dv", attn_grad, mixed).astype(bf16)
    out_sum = scatter_rows(after(out_part, d_rows))
    d_nope, d_rope, d_expanded, d_keys_rope = attend_back(
        linear, tables, expanded, rope_keys, bias, mixed_grad, heads
    )
    latent_part = mm("rk,kc->rc", d_expanded, expand_t)
    rope_part = d_keys_rope[:, :ROPE] + d_keys_rope[:, ROPE:]
    latent_rope_part = jnp.concatenate([latent_part, rope_part], axis=-1)
    if dp_count == 2:
        first_half, second_half = latent_rope_part[:length], latent_rope_part[length:]
        is_first = lax.axis_index("dp") == 0
        sent = swap(jnp.where(is_first, second_half, first_half).astype(bf16))
        combined = jnp.where(is_first, first_half, second_half) + sent.astype(f32)
    else:
        combined = lax.psum_scatter(latent_rope_part, "dp", scatter_dimension=0, tiled=True)
    grad_expand_t = mm("rk,rc->kc", d_expanded, latent_all).astype(bf16)
    latent_grad, latent_gain_grad = norm_back(
        combined[:, :RANK], latent_normed, latent_scale, latent_norm
    )
    rope_grad = rotate_back(combined[:, RANK:], cosine, sine)
    linear_grad = jnp.concatenate(
        [d_nope, d_rope, latent_grad.astype(bf16), rope_grad.astype(bf16)], axis=-1
    )
    normed_grad = mm("rk,dk->rd", linear_grad, query_latent)
    linear_grad = jnp.pad(linear_grad, ((0, 0), (0, -linear_width % 128)))
    input_part, first_gain_grad = norm_back(normed_grad, normed_one, scale_one, first_gain)
    tokens_grad = (middle_grad + input_part)[None]
    small = jnp.stack(
        [
            first_gain_grad,
            second_gain_grad,
            jnp.pad(
                latent_gain_grad.reshape(shards, -1), ((0, 0), (0, g1 - RANK // shards))
            ).reshape(-1),
        ],
        axis=1,
    )
    small = jnp.pad(small, ((0, 0), (0, -small.shape[1] % 128))).astype(bf16)
    grad_linear = mm("rd,rk->dk", normed_low, linear_grad).astype(bf16)
    grad_expand = (
        grad_expand_t.reshape(shards, split, rows_w, RANK)
        .transpose(0, 2, 1, 3)
        .reshape(width, split * RANK)
    )
    sums = [grad_out_t, grad_expand, grad_linear, small]
    if dp_count == 2 and groups == 16:
        sums = grad_sums(sums)
    else:
        sums = [
            lax.psum_scatter(v, both, scatter_dimension=0, tiled=True).astype(f32) for v in sums
        ]
    grad_out_t, grad_expand, grad_linear, small = sums
    grad_expand_t = jnp.concatenate(jnp.split(grad_expand, split, axis=1), axis=0)
    out_sum = after(out_sum, grad_linear)
    outputs = (middle + turned(out_sum, dp_count).astype(f32)).astype(bf16)[None]
    return (
        outputs,
        tokens_grad,
        small[:, 0],
        heads_together(grad_linear[:, :query_width], heads),
        grad_linear[:, query_width:linear_width],
        small[: RANK // shards, 2],
        grad_expand_t.T,
        grad_out_t.T,
        small[:, 1],
        grad_s[0],
        grad_s[1],
        grad_s[2].T,
        grad_gate_e[None],
        grad_up_e[None],
        grad_down_e[None],
    )


def solution(mesh):
    rows = P("expert", "dp", None)
    first = P(("dp", "expert"), None)
    last = P(None, ("dp", "expert"))
    vector = P(("dp", "expert"))
    down = P("expert", None, "dp")
    return jax.shard_map(
        local,
        mesh=mesh,
        in_specs=(
            rows,
            P("expert", None),
            rows,
            rows,
            vector,
            first,
            first,
            vector,
            last,
            last,
            vector,
            first,
            first,
            last,
            rows,
            rows,
            down,
            rows,
        ),
        out_specs=(
            rows,
            rows,
            vector,
            first,
            first,
            vector,
            last,
            last,
            vector,
            first,
            first,
            last,
            rows,
            rows,
            down,
        ),
        check_vma=False,
    )
```

time: 4120 us -> 1530 us (0.37)
  waiting for transfers between devices: 1340 us -> 397 us
  local copies, waits for them, and re-layouts: 841 us -> 129 us
  Pallas kernels: 0 us -> 560 us
  blocking collectives: 573 us -> 96.3 us
  matrix products: 653 us -> 258 us
  other arithmetic: 421 us -> 44.2 us
  starting transfers between devices: 253 us -> 24 us
    all_to_all x9 -> x2, waiting for transfers between devices: 697 us -> 0.01 us  [the longest x1 0.01 us: local(): lax.all_to_all(grad_s, 'expert', split_axis=0, concat_axis=0, tiled=True)]
    pallas_call x0 -> x6, Pallas kernels: none -> 560 us  [the longest x3 270 us: by_block(): pl.pallas_call(kernel, grid=(count,), in_specs=[block(a) for a in blocked...]
    all_to_all x5 -> x1, blocking collectives: 489 us -> 10.5 us  [local(): lax.all_to_all(dense.T, 'expert', split_axis=0, concat_axis=0, tiled=True)]
    dot_general x36 -> x20, matrix products: 653 us -> 258 us  [mm(): return jnp.einsum(spec, a, b, preferred_element_type=f32)]
    unnamed x6 -> x3, other arithmetic: 274 us -> 0.01 us
    unnamed x182 -> x141, local copies, waits for them, and re-layouts: 281 us -> 18.8 us
    all_to_all x9 -> x2, starting transfers between devices: 252 us -> 12.2 us  [the longest x1 7.39 us: local(): lax.all_to_all(shared_own, 'expert', split_axis=0, concat_axis=0, tiled=T...]
    ppermute x0 -> x9, waiting for transfers between devices: none -> 225 us  [swap(): return lax.ppermute(values, 'dp', [(0, 1), (1, 0)])]
  transfers between devices with their start and end apart: 37 -> 17, of which waited for: 19 -> 10; matrix products, arithmetic and copies ran while one was open for 39% -> 26% of each run, Pallas kernels for 0% -> 28%
where the time goes in v1:
time: 1530 us; the launch traced here: 1520 us
  Pallas kernels  560 us (37%)
  waiting for transfers between devices  397 us (26%)
  matrix products  258 us (17%)
  local copies, waits for them, and re-layouts  129 us (8%)
  blocking collectives  96.3 us (6%)
  other arithmetic  44.2 us (3%)
  starting transfers between devices  24 us (2%)
  between operations  15.5 us (1%)
    pallas_call x3, Pallas kernels, by_block(): pl.pallas_call(kernel, grid=(count,), in_specs=[block(a) for a in blocked...  270 us
    dot_general x20, matrix products, mm(): return jnp.einsum(spec, a, b, preferred_element_type=f32)  258 us
    ppermute x9, waiting for transfers between devices, swap(): return lax.ppermute(values, 'dp', [(0, 1), (1, 0)])  225 us
    pallas_call x1, Pallas kernels, grad_sums(): pl.pallas_call(functools.partial(grad_sum_kernel, chunks, len(arrays)), i...  212 us
    all_gather x2, waiting for transfers between devices, gather_rows(): return lax.all_gather(values, 'expert', axis=0, tiled=False)  115 us
    unnamed x1, blocking collectives  85.7 us
    pallas_call x1, Pallas kernels, attend_back(): pl.pallas_call(functools.partial(attend_back_kernel, sizes), grid=(heads...  51 us
    reduce_scatter x2, waiting for transfers between devices, scatter_rows(): lax.psum_scatter(flat(values), 'expert', scatter_dimension=0, tiled=True)  37.6 us
  transfers between devices with their start and end apart: 17, of which 10 were waited for; matrix products, arithmetic and copies ran while one was open for 26% of the time, Pallas kernels for 28%

profile of v1, /device:TPU:0, one launch (start us, length us, event | category | flops | bytes accessed | tf_op | source)
XLA Modules:
  0.0 1524.2 jit_solution(10072610868091683097)
XLA Ops:
  26.1 85.7 %all-reduce.5 = bf16[4608]{0:T(1024)(128)(2,1)S(1)} all-reduce(bf16[4608]{0:T(1024)(128)(2,1)S(1)} %dynamic-update-slice), channel_id=2, replica_groups=mesh['dp'=2,'expert'=16] {'dp','expert'}, use_global_device_ids=true, to_apply=%add.5 | all-reduce | flops 4608 | bytes 18432
  125.6 41.3 %collective-permute-done = bf16[1024,528]{0,1:T(8,128)(2,1)} collective-permute-done((bf16[1024,528]{0,1:T(8,128)(2,1)}, bf16[1024,528]{0,1:T(8,128)(2,1)}, u32[]{:S(2)}, u32[]{:S(2)}) %collective-permute-start) | collective-permute-done | bytes 1081376 | tf_op jit(solution)/shard_map/ppermute | solution.py:440
  173.1 17.2 %all-gather.8.cloned.1.call-done = bf16[2048,4672]{1,0:T(8,128)(2,1)} async-done(((bf16[64,4672]{1,0:T(8,128)(2,1)}), bf16[2048,4672]{1,0:T(8,128)(2,1)}) %all-gather.8.cloned.1.call-update) | async-done | bytes 19136528 | tf_op jit(solution)/shard_map/all_gather | solution.py:542
  197.9 8.4 fusion.69.nope_ref.rope_ref
  243.8 27.4 %attend.1 = bf16[512,2048]{1,0:T(8,128)(2,1)S(1)} custom-call(f32[512,3648]{1,0:T(8,128)} %copy-done.8, f32[512,3648]{1,0:T(8,128)} %copy-done.8, f32[512,128]{1,0:T(8,128)S(1)} %pad_maximum_fusion.9.cos_ref, f32[512,128]{1,0:T(8,128)S(1)} %pad_maximum_fusion.10.sin_ref, bf16[1024,4096]{1,0:T(8,128)(2,1)} %convolution_convert_fusion.2.kv_ref, ...), custom_call_target="tpu_custom_call" | custom-call | tf_op jit(solution)/shard_map/attend/pallas_call | solution.py:182
  274.3 9.2 multiply_reduce_fusion
  297.7 10.5 all_to_all.22.weight_ref
  314.2 109.3 %collective-permute-done.2.refs_1_ = bf16[1024,2816]{1,0:T(8,128)(2,1)} collective-permute-done((bf16[1024,2816]{1,0:T(8,128)(2,1)}, bf16[1024,2816]{1,0:T(8,128)(2,1)}, u32[]{:S(2)}, u32[]{:S(2)}) %collective-permute-start.2) | collective-permute-done | bytes 5767200 | tf_op jit(solution)/shard_map/ppermute | solution.py:440
  423.5 30.9 %all-gather.14.cloned.1.call-done = bf16[8192,2048]{1,0:T(8,128)(2,1)} async-done(((bf16[512,2048]{1,0:T(8,128)(2,1)}), bf16[8192,2048]{1,0:T(8,128)(2,1)}) %all-gather.14.cloned.1.call-update) | async-done | bytes 33554448 | tf_op jit(solution)/shard_map/all_gather | solution.py:630
  454.4 85.9 %experts_forward.1 = (bf16[16,256,2048]{2,1,0:T(8,128)(2,1)}, bf16[16,256,1408]{2,1,0:T(8,128)(2,1)}, bf16[16,256,1408]{2,1,0:T(8,128)(2,1)}, bf16[16,256,1408]{...) custom-call(s32[16,1,512]{2,1,0:T(1,128)} %copy.245.place_ref, ...), custom_call_target="tpu_custom_call" | custom-call | flops 73014444032 | bytes 111181824 | tf_op jit(solution)/shard_map/experts_forward/pallas_call | solution.py:297
  540.2 83.7 %all-gather.12.cloned.1.call-done = bf16[8192,2048]{1,0:T(8,128)(2,1)} async-done(((bf16[512,2048]{1,0:T(8,128)(2,1)}), bf16[8192,2048]{1,0:T(8,128)(2,1)}) %all-gather.12.cloned.1.call-update) | async-done | bytes 33554448 | tf_op jit(solution)/shard_map/all_gather | solution.py:630
  623.9 132.0 %experts_backward.1 = (bf16[16,256,2048]{2,1,0:T(8,128)(2,1)}, bf16[16,256,1408]{2,1,0:T(8,128)(2,1)}, bf16[16,256,1408]{2,1,0:T(8,128)(2,1)}, bf16[16,512,512]{2,1,0:T(8,128)(2,1)}, bf16[16,512,2048]{2,1,0:T(8,128)(2,1)}) custom-call(s32[16,1,512]{2,1,0:T(1,128)} %copy.245.place_ref, f32[16,1,512]{2,1,0:T(1,128)} %copy-done.38, ...), custom_call_target="tpu_custom_call" | custom-call | flops 113816633344 | bytes 167313408 | tf_op jit(solution)/shard_map/experts_backward/pallas_call | solution.py:297
  756.0 19.5 %fusion.45 = bf16[1024,1408]{1,0:T(8,128)(2,1)} fusion(bf16[4096,1408]{1,0:T(8,128)(2,1)} %bitcast.174, bf16[4096,2048]{1,0:T(8,128)(2,1)} %bitcast.160), kind=kOutput, calls=%fused_computation.55 | convolution fusion | flops 11812601856 | bytes 22806528 | tf_op jit(solution)/shard_map/rd,rf->df/dot_general | solution.py:22
  777.0 21.6 %fusion.48 = bf16[1024,1408]{1,0:T(8,128)(2,1)} fusion(bf16[4096,1408]{1,0:T(8,128)(2,1)} %bitcast.172, bf16[4096,2048]{1,0:T(8,128)(2,1)} %bitcast.161), kind=kOutput, calls=%fused_computation.56 | convolution fusion | flops 11812601856 | bytes 22806528 | tf_op jit(solution)/shard_map/rd,rf->df/dot_general | solution.py:22
  799.2 18.0 %fusion.51 = bf16[1408,1024]{1,0:T(8,128)(2,1)} fusion(bf16[4096,1408]{1,0:T(8,128)(2,1)} %bitcast.170, bf16[4096,2048]{1,0:T(8,128)(2,1)S(1)} %bitcast.169), kind=kOutput, calls=%fused_computation.57 | convolution fusion | flops 11812601856 | bytes 22806528 | tf_op jit(solution)/shard_map/rf,rd->fd/dot_general | solution.py:22
  818.7 12.4 fusion.60
  831.1 15.0 fusion.56
  849.0 51.9 %experts_output.1 = bf16[16,512,2048]{2,1,0:T(8,128)(2,1)} custom-call(s32[16,1,512]{2,1,0:T(1,128)} %copy.245.place_ref, f32[16,1,512]{2,1,0:T(1,128)} %copy-done.38, bf16[16,256,1408]{2,1,0:T(8,128)(2,1)} %get-tuple-element.69.act_ref, bf16[16,512,256]{2,1,0:T(8,128)(2,1)} %get-tuple-element.72.act_s_ref, bf16[1408,1024]{1,0:T(8,128)(2,1)} %bitcast.159, ...), custom_call_target="tpu_custom_call" | custom-call | flops 40802189312 | bytes 56164352 | tf_op jit(solution)/shard_map/experts_output/pallas_call | solution.py:297
  900.9 16.1 %fusion.6 = f32[1024,512]{0,1:T(8,128)} fusion(bf16[8192,512]{1,0:T(8,128)(2,1)} %bitcast.177, bf16[8192,2048]{1,0:T(8,128)(2,1)} %all-gather.14.cloned.1.call-done), kind=kOutput, calls=%fused_computation.6 | convolution fusion | flops 8589934592 | bytes 27262976 | tf_op jit(solution)/shard_map/rd,rf->df/dot_general | solution.py:22
  917.0 10.0 fusion.4
  927.0 70.8 %collective-permute-done.7 = bf16[1024,768]{0,1:T(8,128)(2,1)} collective-permute-done((bf16[1024,768]{0,1:T(8,128)(2,1)}, bf16[1024,768]{0,1:T(8,128)(2,1)}, u32[]{:S(2)}, u32[]{:S(2)}) %collective-permute-start.7) | collective-permute-done | bytes 1572896 | tf_op jit(solution)/shard_map/ppermute | solution.py:440
  1016.8 20.2 %convert_add_fusion.3 = f32[1024,1408]{1,0:T(8,128)} fusion(bf16[1024,1408]{1,0:T(8,128)(2,1)} %collective-permute-done.4, bf16[4096,1408]{1,0:T(8,128)(2,1)} %bitcast.175, bf16[4096,2048]{1,0:T(8,128)(2,1)} %bitcast.162), kind=kOutput, calls=%fused_computation.33 | convolution fusion | flops 11814043648 | bytes 28573696 | tf_op jit(solution)/shard_map/rd,rf->df/dot_general | solution.py:22
  1037.0 20.1 %convert_add_fusion.1 = f32[1408,1024]{1,0:T(8,128)} fusion(bf16[1408,1024]{1,0:T(8,128)(2,1)} %collective-permute-done.6, bf16[4096,1408]{1,0:T(8,128)(2,1)} %bitcast.171, bf16[4096,2048]{1,0:T(8,128)(2,1)} %bitcast.166), kind=kOutput, calls=%fused_computation.31 | convolution fusion | flops 11814043648 | bytes 28573696 | tf_op jit(solution)/shard_map/rf,rd->fd/dot_general | solution.py:22
  1057.2 17.5 %convert_add_fusion.2 = f32[1024,1408]{1,0:T(8,128)} fusion(bf16[1024,1408]{1,0:T(8,128)(2,1)} %collective-permute-done.5, bf16[4096,1408]{1,0:T(8,128)(2,1)} %bitcast.173, bf16[4096,2048]{1,0:T(8,128)(2,1)S(1)} %bitcast.165), kind=kOutput, calls=%fused_computation.32 | convolution fusion | flops 11814043648 | bytes 28573696 | tf_op jit(solution)/shard_map/rd,rf->df/dot_general | solution.py:22
  1084.5 37.6 %reduce-scatter.3.cloned.1.call-done = bf16[512,2048]{1,0:T(8,128)(2,1)} async-done(((bf16[8192,2048]{1,0:T(8,128)(2,1)}), bf16[512,2048]{1,0:T(8,128)(2,1)}) %reduce-scatter.3.cloned.1.call-update) | async-done | bytes 2097168 | tf_op jit(solution)/shard_map/reduce_scatter | solution.py:675
  1134.5 51.0 %attend_back.1 = (bf16[512,2048]{1,0:T(8,128)(2,1)S(1)}, bf16[512,1024]{1,0:T(8,128)(2,1)S(1)}, bf16[1024,4096]{1,0:T(8,128)(2,1)}, f32[1024,128]{1,0:T(8,128)S(1)}) custom-call(f32[512,3648]{1,0:T(8,128)} %copy-done.8, f32[512,3648]{1,0:T(8,128)} %copy-done.8, f32[512,128]{1,0:T(8,128)S(1)} %pad_maximum_fusion.9.cos_ref, ...), custom_call_target="tpu_custom_call" | custom-call | tf_op jit(solution)/shard_map/attend_back/pallas_call | solution.py:196
  1185.6 9.7 convolution_convert_fusion.3
  1209.6 8.4 fusion.97
  1221.3 9.5 convolution_convert_fusion.1
  1252.0 15.5 %fusion.38 = (f32[512]{0:T(512)S(1)}, bf16[2048]{0:T(1024)(128)(2,1)S(1)}, f32[512,2048]{1,0:T(8,128)}) fusion(bf16[1,512,2048]{2,1,0:T(8,128)(2,1)} %param.18, f32[2048]{0:T(1024)S(1)} %copy-done.37, f32[512]{0:T(512)S(1)} %copy-done.49, bf16[512,3648]{1,0:T(8,128)(2,1)} %concatenate.75, bf16[2048,3648]{1,0:T(8,128)(2,1)} %copy-done.13), kind=kOutput, calls=%fused_computation.44 | convolution fusion | flops 7657747968 | bytes 24985600 | tf_op jit(solution)/shard_map/rk,dk->rd/dot_general | solution.py:22
  1268.0 13.9 convolution_convert_fusion
  1281.8 211.6 %grad_sums.1 = (f32[64,2048]{1,0:T(8,128)S(1)}, f32[64,1024]{1,0:T(8,128)S(1)}, f32[64,3712]{1,0:T(8,128)}, f32[64,128]{1,0:T(8,128)S(1)}) custom-call(bf16[2,2,2,2,2,64,2048]{6,5,4,3,2,1,0:T(8,128)(2,1)} %bitcast.132, bf16[2,2,2,2,2,64,1024]{6,5,4,3,2,1,0:T(8,128)(2,1)} %reshape_reshape.7.refs_1_, bf16[2,2,2,2,2,64,3712]{6,5,4,3,2,1,0:T(8,128)(2,1)} %bitcast.129, ...), custom_call_target="tpu_custom_call" | custom-call | tf_op jit(solution)/shard_map/grad_sums/pallas_call | solution.py:420
  (296 shorter events, 216.9 us)
Async XLA Ops:
  7.2 183.2 %all-gather.8.cloned.1.call-start = ((), (), s32[]{:S(2)}) async-start(), calls=%async_computation.5 | async-start | bytes 20004864 | tf_op jit(solution)/shard_map/all_gather | solution.py:542
  12.4 261.9 %all-gather.10.cloned.1.call-start = ((), (), s32[]{:S(2)}) async-start(), calls=%async_computation.6 | async-start | bytes 8650752 | tf_op jit(solution)/shard_map/all_gather | solution.py:556
  18.3 93.7 %all-to-all-start.1 = ((bf16[16,64,3,176]{3,1,2,0:T(8,128)(2,1)}), bf16[16,64,3,176]{3,1,2,0:T(8,128)(2,1)S(1)}, u32[]{:S(2)}, u32[]{:S(2)}) async-start(bf16[16,64,3,176]{3,1,2,0:T(8,128)(2,1)} %copy.224), calls=%async_computation.1 | async-start | bytes 3145728 | tf_op jit(solution)/shard_map/all_to_all | solution.py:566
  25.7 96.0 %copy-start.45 = (s32[1,1024]{1,0:T(1,128)S(1)}, s32[1,1024]{1,0:T(1,128)}, u32[]{:S(2)}) copy-start(s32[1,1024]{1,0:T(1,128)} %param.19) | copy-start | bytes 12292
  25.7 428.7 %all-gather.14.cloned.1.call-start = ((), (), s32[]{:S(2)}) async-start(), calls=%async_computation.10 | async-start | bytes 35651584 | tf_op jit(solution)/shard_map/all_gather | solution.py:630
  119.1 47.9 %collective-permute-start = (bf16[1024,528]{0,1:T(8,128)(2,1)}, bf16[1024,528]{0,1:T(8,128)(2,1)}, u32[]{:S(2)}, u32[]{:S(2)}) collective-permute-start(bf16[1024,528]{0,1:T(8,128)(2,1)} %reshape.424), channel_id=1, source_target_pairs={{0,16},{16,0},{1,17},{17,1},{2,18},{18,2},{3,19},{19,3},{4,20},{20... | collective-permute-start | bytes 3244040 | tf_op jit(solution)/shard_map/ppermute | solution.py:440
  121.4 85.0 %copy-start.50 = (f32[32]{0:T(128)}, f32[32]{0:T(128)S(1)}, u32[]{:S(2)}) copy-start(f32[32]{0:T(128)S(1)} %multiply_power_fusion) | copy-start | bytes 388
  121.5 76.4 %copy-start.36 = (f32[2048]{0:T(1024)}, f32[2048]{0:T(1024)S(1)}, u32[]{:S(2)}) copy-start(f32[2048]{0:T(1024)S(1)} %reshape.453) | copy-start | bytes 24580
  121.6 86.6 %copy-start.39 = (f32[512]{0:T(512)}, f32[512]{0:T(512)S(1)}, u32[]{:S(2)}) copy-start(f32[512]{0:T(512)S(1)} %reshape.454) | copy-start | bytes 6148
  121.7 161.9 %copy-start.32 = (f32[2048]{0:T(1024)}, f32[2048]{0:T(1024)S(1)}, u32[]{:S(2)}) copy-start(f32[2048]{0:T(1024)S(1)} %reshape.455) | copy-start | bytes 24580
  121.8 84.7 %copy-start.43 = (f32[512]{0:T(512)}, f32[512]{0:T(512)S(1)}, u32[]{:S(2)}) copy-start(f32[512]{0:T(512)S(1)} %add_convert_fusion.1) | copy-start | bytes 6148
  123.9 74.0 %copy-start.48 = (f32[512]{0:T(512)}, f32[512]{0:T(512)S(1)}, u32[]{:S(2)}) copy-start(f32[512]{0:T(512)S(1)} %add_rsqrt_fusion.2) | copy-start | bytes 6148
  210.6 22.3 %collective-permute-start.1 = (bf16[512,576]{0,1:T(8,128)(2,1)}, bf16[512,576]{0,1:T(8,128)(2,1)}, u32[]{:S(2)}, u32[]{:S(2)}) collective-permute-start(bf16[512,576]{0,1:T(8,128)(2,1)} %copy.236), channel_id=1, source_target_pairs={{0,16},{16,0},{1,17},{17,1},{2,18},{18,2},{3,19},{19,3},{4,20},{20... | collective-permute-start | bytes 1769480 | tf_op jit(solution)/shard_map/ppermute | solution.py:440
  287.0 336.9 %all-gather.12.cloned.1.call-start = ((), (), s32[]{:S(2)}) async-start(), calls=%async_computation.9 | async-start | bytes 35651584 | tf_op jit(solution)/shard_map/all_gather | solution.py:630
  290.2 831.8 %reduce-scatter.3.cloned.1.call-start = ((), (), s32[]{:S(2)}) async-start(), calls=%async_computation.7 | async-start | bytes 35651584 | tf_op jit(solution)/shard_map/reduce_scatter | solution.py:675
  296.1 127.4 %collective-permute-start.2 = (bf16[1024,2816]{1,0:T(8,128)(2,1)}, bf16[1024,2816]{1,0:T(8,128)(2,1)}, u32[]{:S(2)}, u32[]{:S(2)}) collective-permute-start(bf16[1024,2816]{1,0:T(8,128)(2,1)} %constant_dynamic-update-slice_fusion.refs_0_), channel_id=1, source_target_pairs={{0,16},{16,0},{1,17},{17,1},{2,18},{18,2},{3,19},{19,3},{4,20},{20... | collective-permute-start | bytes 17301512 | tf_op jit(solution)/shard_map/ppermute | solution.py:440
  308.2 232.0 %copy-start.38 = (f32[16,1,512]{2,1,0:T(1,128)}, f32[16,1,512]{2,1,0:T(1,128)S(1)}, u32[]{:S(2)}) copy-start(f32[16,1,512]{2,1,0:T(1,128)S(1)} %all_to_all.22.weight_ref) | copy-start | bytes 98308
  312.7 227.5 %collective-permute-start.3 = (bf16[1408,1024]{1,0:T(8,128)(2,1)}, bf16[1408,1024]{1,0:T(8,128)(2,1)}, u32[]{:S(2)}, u32[]{:S(2)}) collective-permute-start(bf16[1408,1024]{1,0:T(8,128)(2,1)} %bitcast.157), channel_id=1, source_target_pairs={{0,16},{16,0},{1,17},{17,1},{2,18},{18,2},{3,19},{19,3},{4,20},{20... | collective-permute-start | bytes 8650760 | tf_op jit(solution)/shard_map/ppermute | solution.py:440
  756.0 43.2 %slice-start.6 = ((s8[16777216]{0:T(1024)(128)(4,1)}), s8[4194304]{0:T(1024)(128)(4,1)S(1)}, s32[]{:S(2)}) async-start(s8[16777216]{0:T(1024)(128)(4,1)} %bitcast.167), calls=%async_computation.17 | async-start | bytes 8388608
  756.0 43.2 %slice-start.7 = ((s8[16777216]{0:T(1024)(128)(4,1)}), s8[4194304]{0:T(1024)(128)(4,1)S(1)}, s32[]{:S(2)}) async-start(s8[16777216]{0:T(1024)(128)(4,1)} %bitcast.167), calls=%async_computation.18 | async-start | bytes 8388608
  775.5 241.3 %collective-permute-start.4 = (bf16[1024,1408]{1,0:T(8,128)(2,1)}, bf16[1024,1408]{1,0:T(8,128)(2,1)}, u32[]{:S(2)}, u32[]{:S(2)}) collective-permute-start(bf16[1024,1408]{1,0:T(8,128)(2,1)} %fusion.45), channel_id=1, source_target_pairs={{0,16},{16,0},{1,17},{17,1},{2,18},{18,2},{3,19},{19,3},{4,20},{20... | collective-permute-start | bytes 8650760 | tf_op jit(solution)/shard_map/ppermute | solution.py:440
  798.6 258.5 %collective-permute-start.5 = (bf16[1024,1408]{1,0:T(8,128)(2,1)}, bf16[1024,1408]{1,0:T(8,128)(2,1)}, u32[]{:S(2)}, u32[]{:S(2)}) collective-permute-start(bf16[1024,1408]{1,0:T(8,128)(2,1)} %fusion.48), channel_id=1, source_target_pairs={{0,16},{16,0},{1,17},{17,1},{2,18},{18,2},{3,19},{19,3},{4,20},{20... | collective-permute-start | bytes 8650760 | tf_op jit(solution)/shard_map/ppermute | solution.py:440
  817.2 219.8 %collective-permute-start.6 = (bf16[1408,1024]{1,0:T(8,128)(2,1)}, bf16[1408,1024]{1,0:T(8,128)(2,1)}, u32[]{:S(2)}, u32[]{:S(2)}) collective-permute-start(bf16[1408,1024]{1,0:T(8,128)(2,1)} %fusion.51), channel_id=1, source_target_pairs={{0,16},{16,0},{1,17},{17,1},{2,18},{18,2},{3,19},{19,3},{4,20},{20... | collective-permute-start | bytes 8650760 | tf_op jit(solution)/shard_map/ppermute | solution.py:440
  848.4 149.4 %collective-permute-start.7 = (bf16[1024,768]{0,1:T(8,128)(2,1)}, bf16[1024,768]{0,1:T(8,128)(2,1)}, u32[]{:S(2)}, u32[]{:S(2)}) collective-permute-start(bf16[1024,768]{0,1:T(8,128)(2,1)} %pad_maximum_fusion.4), channel_id=1, source_target_pairs={{0,16},{16,0},{1,17},{17,1},{2,18},{18,2},{3,19},{19,3},{4,20},{20... | collective-permute-start | bytes 4718600 | tf_op jit(solution)/shard_map/ppermute | solution.py:440
  917.0 80.8 %copy-start.28 = (f32[1024,512]{0,1:T(8,128)S(1)}, f32[1024,512]{0,1:T(8,128)}, u32[]{:S(2)}) copy-start(f32[1024,512]{0,1:T(8,128)} %fusion.6) | copy-start | bytes 6291460
  1011.9 62.8 %all-to-all-start.2 = ((bf16[16,64,3,176]{3,1,2,0:T(8,128)(2,1)}), bf16[16,64,3,176]{3,1,2,0:T(8,128)(2,1)}, u32[]{:S(2)}, u32[]{:S(2)}) async-start(bf16[16,64,3,176]{3,1,2,0:T(8,128)(2,1)} %copy.249), calls=%async_computation.3 | async-start | bytes 3145728 | tf_op jit(solution)/shard_map/all_to_all | solution.py:697
  1016.7 494.7 %reduce-scatter.5.cloned.1.call-start = ((), (), s32[]{:S(2)}) async-start(), calls=%async_computation.8 | async-start | bytes 35651584 | tf_op jit(solution)/shard_map/reduce_scatter | solution.py:675
  1016.8 40.4 %slice-start.2 = ((s8[16777216]{0:T(1024)(128)(4,1)}), s8[4194304]{0:T(1024)(128)(4,1)S(1)}, s32[]{:S(2)}) async-start(s8[16777216]{0:T(1024)(128)(4,1)} %bitcast.163), calls=%async_computation.13 | async-start | bytes 8388608
  1016.8 40.4 %slice-start.3 = ((s8[16777216]{0:T(1024)(128)(4,1)}), s8[4194304]{0:T(1024)(128)(4,1)S(1)}, s32[]{:S(2)}) async-start(s8[16777216]{0:T(1024)(128)(4,1)} %bitcast.163), calls=%async_computation.14 | async-start | bytes 8388608
  1134.5 51.1 %copy-start.25 = (bf16[512,576]{1,0:T(8,128)(2,1)S(1)}, bf16[512,576]{1,0:T(8,128)(2,1)}, u32[]{:S(2)}) copy-start(bf16[512,576]{1,0:T(8,128)(2,1)} %copy-done.24) | copy-start | bytes 1769476
  1134.5 51.1 %copy-start.27 = (bf16[512,576]{1,0:T(8,128)(2,1)S(1)}, bf16[512,576]{1,0:T(8,128)(2,1)}, u32[]{:S(2)}) copy-start(bf16[512,576]{1,0:T(8,128)(2,1)} %copy-done.26) | copy-start | bytes 1769476
  1219.9 15.3 %collective-permute-start.8 = (bf16[512,576]{0,1:T(8,128)(2,1)S(1)}, bf16[512,576]{0,1:T(8,128)(2,1)S(1)}, u32[]{:S(2)}, u32[]{:S(2)}) collective-permute-start(bf16[512,576]{0,1:T(8,128)(2,1)S(1)} %copy.256), channel_id=1, source_target_pairs={{0,16},{16,0},{1,17},{17,1},{2,18},{18,2},{3,19},{19,3},{4,20},{20... | collective-permute-start | bytes 1769480 | tf_op jit(solution)/shard_map/ppermute | solution.py:440
  (50 other events, 391.6 us)
Sparse Core Ops, SparseCore 0:
  12.5 177.7 all-gather.7
  193.2 80.9 all-gather.9
  287.1 167.2 all-gather.13
  455.8 168.0 all-gather.11
  756.1 365.9 reduce-scatter.2
  1126.2 383.2 reduce-scatter.4

commit v2 on v1

--- a/solution.py
+++ b/solution.py
@@ -186,6 +186,7 @@
         out_specs=pl.BlockSpec((length, 2 * VDIM), lambda p: (0, p)),
         out_shape=jax.ShapeDtypeStruct((length, heads * VDIM), bf16),
         compiler_params=pltpu.CompilerParams(vmem_limit_bytes=48 * MIB),
+        cost_estimate=time_of(27),
         name="attend",
     )(linear, linear, *tables, kv, kr, bias)
 
@@ -212,6 +213,7 @@
         ],
         scratch_shapes=[pltpu.VMEM((2, seq, NOPE), f32), pltpu.VMEM((2, seq, VDIM), f32)],
         compiler_params=pltpu.CompilerParams(vmem_limit_bytes=48 * MIB),
+        cost_estimate=time_of(51),
         name="attend_back",
     )(linear, linear, *tables, kv, kr, bias, grad)
 
@@ -249,44 +251,50 @@
     silu_s_ref[0] = silu.astype(bf16)
 
 
-def backward_kernel(
+def hidden_kernel(
     n, slots, place_ref, weight_ref, grads_ref, us_ref, silu_ref, us_s_ref, silu_s_ref, *refs
 ):
-    gate_up, down, gate_up_s, down_s = (refs[i * n : (i + 1) * n] for i in range(4))
-    picked_ref, d_gate_ref, d_up_ref, d_shared_ref, d_rows_ref = refs[4 * n :]
+    down, down_s = refs[:n], refs[n : 2 * n]
+    picked_ref, d_gate_ref, d_up_ref, d_shared_ref = refs[2 * n :]
     width = grads_ref.shape[-1]
     hot = one_hot(place_ref, slots)
     slot_weight = jnp.sum(jnp.where(hot, weight_ref[0], 0.0), axis=1, keepdims=True)
     picks = hot.astype(f32).astype(bf16)
     picked_ref[0] = (dot(picks, grads_ref[0], 1, 0) * slot_weight).astype(bf16)
     d_act = total([dot(picked_ref[0, :, at], w[...], 1, 1) for w, at in width_parts(down, width)])
-    d_gate = (d_act * us_ref[0].astype(f32)).astype(bf16)
-    d_up = (d_act * silu_ref[0].astype(f32)).astype(bf16)
-    d_gate_ref[0] = d_gate
-    d_up_ref[0] = d_up
-    d_both = jnp.concatenate([d_gate, d_up], axis=1)
+    d_gate_ref[0] = (d_act * us_ref[0].astype(f32)).astype(bf16)
+    d_up_ref[0] = (d_act * silu_ref[0].astype(f32)).astype(bf16)
     d_act = total([dot(grads_ref[0, :, at], w[...], 1, 0) for w, at in width_parts(down_s, width)])
     half = d_act.shape[1]
     d_shared_ref[0, :, :half] = (d_act * us_s_ref[0].astype(f32)).astype(bf16)
     d_shared_ref[0, :, half:] = (d_act * silu_s_ref[0].astype(f32)).astype(bf16)
-    for (w, at), w_s in zip(width_parts(gate_up, width), gate_up_s):
-        d_row = dot(d_both, w[...], 1, 1).astype(bf16)
-        d_rows_ref[0, :, at] = (
-            dot(picks, d_row, 0, 0) + dot(d_shared_ref[0], w_s[...], 1, 1)
-        ).astype(bf16)
+
+
+def rows_kernel(
+    slots, place_ref, d_gate_ref, d_up_ref, d_shared_ref, gate_up_ref, gate_up_s_ref, d_rows_ref
+):
+    picks = one_hot(place_ref, slots).astype(f32).astype(bf16)
+    d_both = jnp.concatenate([d_gate_ref[0], d_up_ref[0]], axis=1)
+    d_row = dot(d_both, gate_up_ref[...], 1, 1).astype(bf16)
+    d_rows_ref[0] = (
+        dot(picks, d_row, 0, 0) + dot(d_shared_ref[0], gate_up_s_ref[...], 1, 1)
+    ).astype(bf16)
 
 
 def output_kernel(n, slots, place_ref, weight_ref, act_ref, act_s_ref, *refs):
-    down, down_s, out_ref = refs[:n], refs[n : 2 * n], refs[2 * n]
-    width = out_ref.shape[-1]
+    down, down_s, outs = refs[:n], refs[n : 2 * n], refs[2 * n :]
     hot = one_hot(place_ref, slots)
     slot_weight = jnp.sum(jnp.where(hot, weight_ref[0], 0.0), axis=1, keepdims=True)
     picks = hot.astype(f32).astype(bf16)
-    for (w, at), w_s in zip(width_parts(down, width), down_s):
+    bounds = [0, outs[0].shape[-1], outs[0].shape[-1] + outs[1].shape[-1]]
+    for i, (w, w_s) in enumerate(zip(down, down_s)):
         out = (dot(act_ref[0], w[...], 1, 0) * slot_weight).astype(bf16)
-        out_ref[0, :, at] = (
-            dot(picks, out, 0, 0) + dot(act_s_ref[0], w_s[...], 1, 1)
-        ).astype(bf16)
+        rows = (dot(picks, out, 0, 0) + dot(act_s_ref[0], w_s[...], 1, 1)).astype(bf16)
+        first = i * w.shape[1]
+        for out_ref, low, high in zip(outs, bounds, bounds[1:]):
+            low_in, high_in = max(low, first), min(high, first + w.shape[1])
+            if low_in < high_in:
+                out_ref[0, :, low_in - low : high_in - low] = rows[:, low_in - first : high_in - first]
 
 
 def by_block(kernel, name, blocked, fixed, outs, flops):
@@ -306,19 +314,7 @@
     )(*blocked, *fixed)
 
 
-def add_rows(into, left, right):
-    step = 16
-    lead = (slice(None),) * (len(into.shape) - 2)
-
-    @pl.loop(0, into.shape[-2] // step)
-    def _(i):
-        at = (*lead, pl.ds(pl.multiple_of(i * step, step), step), slice(None))
-        into[at] = (left[at].astype(f32) + right[at].astype(f32)).astype(into.dtype)
-
-
-def grad_sum_kernel(chunks, n, *refs):
-    ins, outs = refs[:n], refs[n : 2 * n]
-    own, got, load_sem, send_sem, recv_sem = refs[2 * n], refs[2 * n + 1 : 2 * n + 6], *refs[2 * n + 6 :]
+def neighbours():
     dp, expert = lax.axis_index("dp"), lax.axis_index("expert")
     core, y = expert % 2, (expert // 2) % 2
     z_low, z_high = (expert // 4) % 2, expert // 8
@@ -333,107 +329,221 @@
     for partner in partners:
         pl.semaphore_signal(barrier, inc=1, device_id=partner, device_id_type=pl.DeviceIdType.MESH)
     pl.semaphore_wait(barrier, len(partners))
+    return partners, (core, dp, y, z_low, z_high)
+
+
+PIECE = 64 * 1024
+
+
+def chunks_of(shapes):
+    chunks = []
+    for i, (rows, columns) in enumerate(shapes):
+        wide = min(columns, 1024)
+        tall = rows
+        while tall > 16 and tall * wide > PIECE:
+            tall //= 2
+        chunks += [
+            (i, top, tall, left, min(wide, columns - left))
+            for top in range(0, rows, tall)
+            for left in range(0, columns, wide)
+        ]
+    return chunks
+
+
+def piece_of(chunk):
+    _, top, tall, left, wide = chunk
+    return pl.ds(top, tall), pl.ds(left, wide)
+
+
+def time_of(microseconds):
+    return pl.CostEstimate(
+        flops=0, bytes_accessed=int(microseconds * 3.69e6), transcendentals=0
+    )
+
+
+def gather_kernel(chunks, n, *refs):
+    ins, outs = refs[:n], refs[n : 2 * n]
+    own_sem, send_sem, recv_sem = refs[2 * n :]
+    partners, (core, dp, y, z_low, z_high) = neighbours()
+    mine = (dp, z_high, z_low, y, core)
+    place = [4, 0, 3, 2, 1]
+    own = [pltpu.make_async_copy(ins[i], outs[i].at[mine], own_sem.at[i]) for i in range(n)]
+    for copy in own:
+        copy.start()
+    copies = {}
+    waited = set()
     count = len(chunks)
 
+    def order(k):
+        return [4, 2, 3, 1, 0] if k % 2 else [4, 3, 2, 1, 0]
+
+    for turn in range(count + 5):
+        for stage in range(5):
+            k = turn - stage
+            if not 0 <= k < count:
+                continue
+            array = chunks[k][0]
+            gathered = [place[axis] for axis in order(k)[:stage]]
+            held = [slice(None) if d in gathered else mine[d] for d in range(5)]
+            there = outs[array].at[(*held, *piece_of(chunks[k]))]
+            if stage == 0:
+                here = ins[array].at[piece_of(chunks[k])]
+            else:
+                here = there
+                copies[stage - 1, k].wait_recv()
+            if stage == 1 and array not in waited:
+                waited.add(array)
+                own[array].wait()
+            copies[stage, k] = pltpu.make_async_remote_copy(
+                src_ref=here,
+                dst_ref=there,
+                send_sem=send_sem.at[stage, k],
+                recv_sem=recv_sem.at[stage, k],
+                device_id=partners[order(k)[stage]],
+                device_id_type=pl.DeviceIdType.MESH,
+            )
+            copies[stage, k].start()
+    for k in range(count):
+        copies[4, k].wait_recv()
+    for copy in copies.values():
+        copy.wait_send()
+
+
+def gather_all(arrays):
+    chunks = chunks_of([a.shape for a in arrays])
+    dims = (2, 2, 2, 2, 2)
+    n = len(arrays)
+    gathered = pl.pallas_call(
+        functools.partial(gather_kernel, chunks, n),
+        in_specs=[pl.BlockSpec(memory_space=pl.ANY)] * n,
+        out_specs=[pl.BlockSpec(memory_space=pl.ANY)] * n,
+        out_shape=[jax.ShapeDtypeStruct((*dims, *a.shape), a.dtype) for a in arrays],
+        scratch_shapes=[
+            pltpu.SemaphoreType.DMA((n,)),
+            pltpu.SemaphoreType.DMA((5, len(chunks))),
+            pltpu.SemaphoreType.DMA((5, len(chunks))),
+        ],
+        compiler_params=pltpu.CompilerParams(collective_id=2, has_side_effects=True),
+        cost_estimate=time_of(180),
+        name="gather_all",
+    )(*arrays)
+    return [g.reshape(-1, a.shape[1]) for g, a in zip(gathered, arrays)]
+
+
+def add_rows(into, left, right):
+    step = 16
+    lead = (slice(None),) * (len(into.shape) - 2)
+
+    @pl.loop(0, into.shape[-2] // step)
+    def _(i):
+        at = (*lead, pl.ds(pl.multiple_of(i * step, step), step), slice(None))
+        into[at] = (left[at].astype(f32) + right[at].astype(f32)).astype(into.dtype)
+
+
+def grad_sum_kernel(chunks, n, *refs):
+    ins, outs = refs[:n], refs[n : 2 * n]
+    count = len(chunks)
+    own = refs[2 * n : 2 * n + count]
+    got = [refs[2 * n + (i + 1) * count :][:count] for i in range(5)]
+    load_sem, send_sem, recv_sem = refs[-3:]
+    partners, mine = neighbours()
+    core = mine[0]
+
     def source(k, which):
-        array, start, wide = chunks[k]
-        return ins[array].at[:, :, :, :, which, :, pl.ds(start, wide)]
-
-    def cut(ref, k):
-        return ref.at[(slice(None),) * (len(ref.shape) - 1) + (pl.ds(0, chunks[k][2]),)]
-
-    def send(stage, k, values):
-        return pltpu.make_async_remote_copy(
+        array = chunks[k][0]
+        lead = (slice(None),) * (len(ins[array].shape) - 3)
+        return ins[array].at[(*lead, which, *piece_of(chunks[k]))]
+
+    def pick(ref, stage, which):
+        lead = [0, 0, 2, 1, 0][stage]
+        return ref.at[(*(slice(None),) * lead, which)]
+
+    def stages(k):
+        return [0, 1, 2, 3, 4] if len(ins[chunks[k][0]].shape) == 7 else [0, 2, 3, 4]
+
+    copies = {}
+
+    def start(stage, k, values):
+        copies[stage, k] = pltpu.make_async_remote_copy(
             src_ref=values,
-            dst_ref=cut(got[stage].at[k], k),
+            dst_ref=got[stage][k],
             send_sem=send_sem.at[stage, k],
             recv_sem=recv_sem.at[stage, k],
             device_id=partners[stage],
             device_id_type=pl.DeviceIdType.MESH,
         )
-
-    def load(k):
-        return pltpu.make_async_copy(source(k, core), cut(own.at[k % 2], k), load_sem.at[k % 2])
-
-    copies = {}
-
-    def start(stage, k, values):
-        copies[stage, k] = send(stage, k, values)
         copies[stage, k].start()
 
+    loads = [pltpu.make_async_copy(source(k, core), own[k], load_sem.at[k]) for k in range(count)]
     for k in range(count):
         start(0, k, source(k, 1 - core))
-    for k in range(min(2, count)):
-        load(k).start()
+        loads[k].start()
     for turn in range(count + 4):
-        k = turn
-        if k < count:
-            load(k).wait()
-            copies[0, k].wait_recv()
-            held, mine = cut(got[0].at[k], k), cut(own.at[k % 2], k)
-            add_rows(held.at[1 - dp], held.at[1 - dp], mine.at[1 - dp])
-            start(1, k, held.at[1 - dp])
-            add_rows(held.at[dp], held.at[dp], mine.at[dp])
-            if k + 2 < count:
-                load(k + 2).start()
-        k = turn - 1
-        if 0 <= k < count:
-            copies[1, k].wait_recv()
-            held = cut(got[1].at[k], k)
-            add_rows(held, held, cut(got[0].at[k], k).at[dp])
-            start(2, k, held.at[:, :, 1 - y])
-        k = turn - 2
-        if 0 <= k < count:
-            copies[2, k].wait_recv()
-            held = cut(got[2].at[k], k)
-            add_rows(held, held, cut(got[1].at[k], k).at[:, :, y])
-            start(3, k, held.at[:, 1 - z_low])
-        k = turn - 3
-        if 0 <= k < count:
-            copies[3, k].wait_recv()
-            held = cut(got[3].at[k], k)
-            add_rows(held, held, cut(got[2].at[k], k).at[:, z_low])
-            start(4, k, held.at[1 - z_high])
-        k = turn - 4
-        if 0 <= k < count:
-            copies[4, k].wait_recv()
-            array, first, wide = chunks[k]
-            add_rows(
-                outs[array].at[:, pl.ds(first, wide)],
-                cut(got[4].at[k], k),
-                cut(got[3].at[k], k).at[z_high],
-            )
+        for step in range(5):
+            k = turn - step
+            if not 0 <= k < count or step >= len(stages(k)):
+                continue
+            stage = stages(k)[step]
+            later = stages(k)[step + 1] if step + 1 < len(stages(k)) else None
+            held = got[stage][k]
+            copies[stage, k].wait_recv()
+            if step == 0:
+                loads[k].wait()
+                sent, kept = 1 - mine[later], mine[later]
+                part = pick(held, later, sent)
+                add_rows(part, part, pick(own[k], later, sent))
+                start(later, k, part)
+                part = pick(held, later, kept)
+                add_rows(part, part, pick(own[k], later, kept))
+                continue
+            kept = pick(got[stages(k)[step - 1]][k], stage, mine[stage])
+            if later is None:
+                add_rows(outs[chunks[k][0]].at[piece_of(chunks[k])], held, kept)
+            else:
+                add_rows(held, held, kept)
+                start(later, k, pick(held, later, 1 - mine[later]))
     for copy in copies.values():
         copy.wait_send()
 
 
-def grad_sums(arrays):
-    shards = 32
-    rows, piece = arrays[0].shape[0] // shards, 1024
-    chunks = [
-        (i, at, min(piece, a.shape[1] - at))
-        for i, a in enumerate(arrays)
-        for at in range(0, a.shape[1], piece)
-    ]
-    dims = (2, 2, 2, 2)
-    count = len(chunks)
+def grad_sums(arrays, over_dp):
+    n = len(arrays)
+    dims = [(2,) * (5 if o else 4) for o in over_dp]
+    rows = [a.shape[0] // 2 ** len(d) for a, d in zip(arrays, dims)]
+    chunks = chunks_of([(r, a.shape[1]) for r, a in zip(rows, arrays)])
+    wider = [c for c in chunks if over_dp[c[0]]]
+    narrower = [c for c in chunks if not over_dp[c[0]]]
+    chunks = []
+    while wider or narrower:
+        chunks += wider[:1] + narrower[:1]
+        wider, narrower = wider[1:], narrower[1:]
+
+    def buffers(stage):
+        shapes = []
+        for i, _, tall, _, wide in chunks:
+            lead = dims[i][:-1] if stage == 0 else (2,) * (4 - stage)
+            unused = stage == 1 and not over_dp[i]
+            shapes.append(pltpu.VMEM((16, 128) if unused else (*lead, tall, wide), bf16))
+        return shapes
+
     return pl.pallas_call(
-        functools.partial(grad_sum_kernel, chunks, len(arrays)),
-        in_specs=[pl.BlockSpec(memory_space=pl.ANY)] * len(arrays),
-        out_specs=[pl.BlockSpec(memory_space=pltpu.VMEM)] * len(arrays),
-        out_shape=[jax.ShapeDtypeStruct((rows, a.shape[1]), f32) for a in arrays],
+        functools.partial(grad_sum_kernel, chunks, n),
+        in_specs=[pl.BlockSpec(memory_space=pl.ANY)] * n,
+        out_specs=[pl.BlockSpec(memory_space=pltpu.VMEM)] * n,
+        out_shape=[jax.ShapeDtypeStruct((r, a.shape[1]), f32) for r, a in zip(rows, arrays)],
         scratch_shapes=[
-            pltpu.VMEM((2, *dims, rows, piece), bf16),
-            *[pltpu.VMEM((count, *dims[i:], rows, piece), bf16) for i in range(5)],
-            pltpu.SemaphoreType.DMA((2,)),
-            pltpu.SemaphoreType.DMA((5, count)),
-            pltpu.SemaphoreType.DMA((5, count)),
+            *buffers(0),
+            *[buffer for stage in range(5) for buffer in buffers(stage)],
+            pltpu.SemaphoreType.DMA((len(chunks),)),
+            pltpu.SemaphoreType.DMA((5, len(chunks))),
+            pltpu.SemaphoreType.DMA((5, len(chunks))),
         ],
         compiler_params=pltpu.CompilerParams(
-            collective_id=1, has_side_effects=True, vmem_limit_bytes=52 * MIB
+            collective_id=1, has_side_effects=True, vmem_limit_bytes=56 * MIB
         ),
+        cost_estimate=time_of(170),
         name="grad_sums",
-    )(*[a.reshape(*dims, 2, rows, a.shape[1]) for a in arrays])
+    )(*[a.reshape(*d, r, a.shape[1]) for a, d, r in zip(arrays, dims, rows)])
 
 
 def swap(values):
@@ -519,12 +629,6 @@
     rows_w = query_weight.shape[0]
 
     g1 = input_gain.shape[0]
-    gains = jnp.concatenate([input_gain, middle_gain, latent_gain])
-    gains = lax.all_gather(gains, both, axis=0, tiled=False)
-    first_gain = gains[:, :g1].reshape(-1).astype(f32)
-    second_gain = gains[:, g1 : 2 * g1].reshape(-1).astype(f32)
-    latent_norm = gains[:, 2 * g1 :].reshape(-1).astype(f32)
-
     hits = routes[0][:, None, :] == jnp.arange(groups, dtype=jnp.int32)[None, :, None]
     dense = jnp.sum(jnp.where(hits, combine[0][:, None, :], 0.0), axis=-1)
     dense = jnp.where(jnp.any(hits, axis=-1), dense, -1.0)
@@ -536,24 +640,22 @@
     place = place[:, None, :]
     row_weights = my_weights[:, None, :]
 
-    expand_rows = expand_weight.T.shape[0]
-    split = expand_rows // rows_w
-    expand_wide = jnp.concatenate(jnp.split(expand_weight.T, split, axis=0), axis=1)
-    gathered = lax.all_gather(
-        jnp.concatenate([heads_apart(query_weight, heads), latent_weight, expand_wide], axis=1),
-        both,
-        axis=0,
-        tiled=True,
-    )
     linear_width = query_width + RANK + ROPE
-    query_latent = gathered[:, :linear_width]
-    expand_t = (
-        gathered[:, linear_width:]
-        .reshape(shards, rows_w, split, RANK)
-        .transpose(0, 2, 1, 3)
-        .reshape(-1, RANK)
-    )
-    output_t = lax.all_gather(output_weight.T, both, axis=0, tiled=True)
+    gains = jnp.stack([input_gain, middle_gain, jnp.pad(latent_gain, (0, g1 - latent_gain.size))])
+    gains = jnp.pad(gains, ((0, 13), (0, -g1 % 128)))
+    own_linear = jnp.concatenate([heads_apart(query_weight, heads), latent_weight], axis=1)
+    own_linear = jnp.pad(own_linear, ((0, 0), (0, -linear_width % 128)))
+    shares = [gains, own_linear, expand_weight.T, output_weight.T]
+    if dp_count == 2 and groups == 16:
+        gains, query_latent, expand_t, output_t = gather_all(shares)
+    else:
+        gains, query_latent, expand_t, output_t = [
+            lax.all_gather(v, both, axis=0, tiled=True) for v in shares
+        ]
+    gains = gains.reshape(shards, 16, -1)
+    first_gain = gains[:, 0, :g1].reshape(-1).astype(f32)
+    second_gain = gains[:, 1, :g1].reshape(-1).astype(f32)
+    latent_norm = gains[:, 2, : latent_gain.size].reshape(-1).astype(f32)
 
     shared_own = jnp.stack(
         [
@@ -563,7 +665,8 @@
         ],
         axis=1,
     ).transpose(2, 0, 1, 3)
-    shared_cols = lax.all_to_all(shared_own, "expert", split_axis=0, concat_axis=0, tiled=True)
+    shared_own = after(shared_own, expand_t)
+    shared_cols = shared_moved = lax.all_to_all(shared_own, "expert", split_axis=0, concat_axis=0, tiled=True)
     shared_cols = weight_parts(shared_cols.reshape(groups * rows_w, 3 * part_s), 0, dp_count)
     padded_s = -(-part_s // 128) * 128
     wide_s = [
@@ -573,9 +676,6 @@
     gate_up_s = [c[:, :2].reshape(-1, 2 * padded_s) for c in wide_s]
     down_s_t = [c[:, 2] for c in wide_s]
 
-    first_gain, my_weights, gate_up_s, down_s_t, query_latent = lax.optimization_barrier(
-        (first_gain, my_weights, gate_up_s, down_s_t, query_latent)
-    )
     own_e = after((expert_gate[0], expert_up[0], expert_down[0]), query_latent)
     gate_up_e = weight_parts(jnp.concatenate(own_e[:2], axis=1), 0, dp_count)
     down_e = weight_parts(own_e[2], 1, dp_count)
@@ -595,7 +695,7 @@
     latent_scale = lax.rsqrt(jnp.mean(latent_raw * latent_raw, axis=-1, keepdims=True) + epsilon)
     latent_normed = latent_raw * latent_scale
     latent_low = (latent_normed * latent_norm).astype(bf16)
-    rope_low = rotate(linear[:, query_width + RANK :], cosine, sine).astype(bf16)
+    rope_low = rotate(linear[:, query_width + RANK : linear_width], cosine, sine).astype(bf16)
     latent_rope = jnp.concatenate([latent_low, rope_low], axis=-1)
     if dp_count == 2:
         other = swap(latent_rope)
@@ -630,13 +730,22 @@
         return lax.all_gather(values, "expert", axis=0, tiled=False)
 
     grads_all = gather_rows(turned(cotangent[0], dp_count))
-    rows_all = gather_rows(turned(ffn_rows, dp_count))
+    rows_all = gather_rows(
+        after(turned(ffn_rows, dp_count), (grads_all, shared_moved, my_weights))
+    )
+
+    def flat(values):
+        return values.reshape(-1, values.shape[-1])
+
+    def scatter_rows(values):
+        return lax.psum_scatter(flat(values), "expert", scatter_dimension=0, tiled=True)
 
     n = len(gate_up_e)
     hidden = expert_gate.shape[2]
     block_of = lambda rows, columns: jax.ShapeDtypeStruct((groups, rows, columns), bf16)
     wide = [block_of(slots, hidden)] * 3
     wide_shared = [block_of(length, padded_s)] * 3
+    aside = 3 * width // 16
     unit = 2 * groups * width
     picked, act_e, up_slope, silu, act_s, up_slope_s, silu_s = by_block(
         functools.partial(forward_kernel, n, slots),
@@ -646,35 +755,33 @@
         [block_of(slots, width), *wide, *wide_shared],
         unit * (slots * (length + 2 * hidden) + 2 * length * padded_s),
     )
-    picked_grad, d_gate, d_up, d_shared, d_rows_part = by_block(
-        functools.partial(backward_kernel, n, slots),
-        "experts_backward",
+    picked_grad, d_gate, d_up, d_shared = by_block(
+        functools.partial(hidden_kernel, n, slots),
+        "experts_hidden",
         [place, row_weights, grads_all, up_slope, silu, up_slope_s, silu_s],
-        [*gate_up_e, *down_e, *gate_up_s, *down_s_t],
-        [
-            block_of(slots, width),
-            *wide[:2],
-            block_of(length, 2 * padded_s),
-            block_of(length, width),
-        ],
-        unit * (slots * (2 * length + 3 * hidden) + 3 * length * padded_s),
-    )
-    [out_part] = by_block(
+        [*down_e, *down_s_t],
+        [block_of(slots, width), *wide[:2], block_of(length, 2 * padded_s)],
+        unit * (slots * (length + hidden) + length * padded_s),
+    )
+    d_rows = []
+    for weights, weights_s in zip(gate_up_e, gate_up_s):
+        [part] = by_block(
+            functools.partial(rows_kernel, slots),
+            "experts_rows",
+            [place, d_gate, d_up, d_shared if not d_rows else after(d_shared, part)],
+            [weights, weights_s],
+            [block_of(length, width // n)],
+            unit // n * (slots * (length + 2 * hidden) + 2 * length * padded_s),
+        )
+        d_rows.append(scatter_rows(part))
+    out_parts = by_block(
         functools.partial(output_kernel, n, slots),
         "experts_output",
         [place, row_weights, act_e, act_s],
         [*down_e, *down_s_t],
-        [block_of(length, width)],
+        [block_of(length, width - aside), block_of(length, aside)],
         unit * (slots * (length + hidden) + length * padded_s),
     )
-
-    def flat(values):
-        return values.reshape(-1, values.shape[-1])
-
-    def scatter_rows(values):
-        return lax.psum_scatter(flat(values), "expert", scatter_dimension=0, tiled=True)
-
-    d_rows = scatter_rows(d_rows_part)
 
     column_parts = lambda values: jnp.split(flat(values), n, axis=1)
     picked, picked_grad, rows_parts, grads_parts = map(
@@ -694,23 +801,32 @@
         0,
     )
     grad_s = grad_s.reshape(groups, rows_w, 3, padded_s)[..., :part_s].astype(bf16)
+    d_rows, grad_gate_e, grad_up_e, grad_down_e, grad_s, out_parts = lax.optimization_barrier(
+        (d_rows, grad_gate_e, grad_up_e, grad_down_e, grad_s, out_parts)
+    )
     grad_s = lax.all_to_all(grad_s, "expert", split_axis=0, concat_axis=0, tiled=True)
     grad_s = grad_s.transpose(2, 1, 0, 3).reshape(3, rows_w, hidden_s).astype(f32)
-    d_rows, grad_gate_e, grad_up_e, grad_down_e, grad_s, out_part = lax.optimization_barrier(
-        (d_rows, grad_gate_e, grad_up_e, grad_down_e, grad_s, out_part)
-    )
-    d_rows_own = turned(d_rows, dp_count).astype(f32)
+    d_rows_own = turned(jnp.concatenate(d_rows, axis=1), dp_count).astype(f32)
 
     out_grad = cotangent[0].astype(f32)
     middle_part, second_gain_grad = norm_back(d_rows_own, normed_two, scale_two, second_gain)
     middle_grad = out_grad + middle_part
     attn_grad = middle_grad.astype(bf16)
     mixed_grad = mm("rd,dv->rv", attn_grad, output_t).astype(bf16)
-    grad_out_t = mm("rd,rv->dv", attn_grad, mixed).astype(bf16)
-    out_sum = scatter_rows(after(out_part, d_rows))
+    attn_parts = jnp.split(turned(attn_grad, dp_count), n, axis=1)
+    early = mixed.shape[1] // 2
+    grad_out_t = [lambda p=p: mm("rd,rv->dv", p, mixed[:, :early]) for p in attn_parts]
+    if dp_count == 2:
+        sent, mixed_grad = lax.optimization_barrier((grad_out_t[1]().astype(bf16), mixed_grad))
+        grad_out_t = grad_out_t[0]() + swap(sent).astype(f32)
+    else:
+        grad_out_t = scatter_dp(grad_out_t, 0)
+    grad_out_t = [grad_out_t.astype(bf16), mm("rd,rv->dv", attn_grad, mixed[:, early:]).astype(bf16)]
+    out_sum = scatter_rows(after(out_parts[0], d_rows))
     d_nope, d_rope, d_expanded, d_keys_rope = attend_back(
         linear, tables, expanded, rope_keys, bias, mixed_grad, heads
     )
+    d_expanded, grad_out_t[0] = lax.optimization_barrier((d_expanded, grad_out_t[0]))
     latent_part = mm("rk,kc->rc", d_expanded, expand_t)
     rope_part = d_keys_rope[:, :ROPE] + d_keys_rope[:, ROPE:]
     latent_rope_part = jnp.concatenate([latent_part, rope_part], axis=-1)
@@ -729,8 +845,8 @@
     linear_grad = jnp.concatenate(
         [d_nope, d_rope, latent_grad.astype(bf16), rope_grad.astype(bf16)], axis=-1
     )
+    linear_grad = jnp.pad(linear_grad, ((0, 0), (0, -linear_width % 128)))
     normed_grad = mm("rk,dk->rd", linear_grad, query_latent)
-    linear_grad = jnp.pad(linear_grad, ((0, 0), (0, -linear_width % 128)))
     input_part, first_gain_grad = norm_back(normed_grad, normed_one, scale_one, first_gain)
     tokens_grad = (middle_grad + input_part)[None]
     small = jnp.stack(
@@ -745,22 +861,20 @@
     )
     small = jnp.pad(small, ((0, 0), (0, -small.shape[1] % 128))).astype(bf16)
     grad_linear = mm("rd,rk->dk", normed_low, linear_grad).astype(bf16)
-    grad_expand = (
-        grad_expand_t.reshape(shards, split, rows_w, RANK)
-        .transpose(0, 2, 1, 3)
-        .reshape(width, split * RANK)
-    )
-    sums = [grad_out_t, grad_expand, grad_linear, small]
+    sums = [*grad_out_t, flat(out_parts[1]), grad_expand_t, grad_linear, small]
+    over_dp = [False, True, False, True, True, True]
     if dp_count == 2 and groups == 16:
-        sums = grad_sums(sums)
+        sums = grad_sums(sums, over_dp)
     else:
         sums = [
-            lax.psum_scatter(v, both, scatter_dimension=0, tiled=True).astype(f32) for v in sums
+            lax.psum_scatter(v, both if o else "expert", scatter_dimension=0, tiled=True)
+            for v, o in zip(sums, over_dp)
         ]
-    grad_out_t, grad_expand, grad_linear, small = sums
-    grad_expand_t = jnp.concatenate(jnp.split(grad_expand, split, axis=1), axis=0)
+        sums = [v.astype(f32) for v in sums]
+    *grad_out_t, out_aside, grad_expand_t, grad_linear, small = sums
     out_sum = after(out_sum, grad_linear)
-    outputs = (middle + turned(out_sum, dp_count).astype(f32)).astype(bf16)[None]
+    out_sum = jnp.concatenate([out_sum.astype(f32), out_aside], axis=1)
+    outputs = (middle + turned(out_sum, dp_count)).astype(bf16)[None]
     return (
         outputs,
         tokens_grad,
@@ -769,7 +883,7 @@
         grad_linear[:, query_width:linear_width],
         small[: RANK // shards, 2],
         grad_expand_t.T,
-        grad_out_t.T,
+        jnp.concatenate(grad_out_t, axis=1).T,
         small[:, 1],
         grad_s[0],
         grad_s[1],

time: 1530 us -> 1450 us (0.948)
  Pallas kernels: 560 us -> 773 us
  waiting for transfers between devices: 397 us -> 207 us
  blocking collectives: 96.3 us -> 0 us
  local copies, waits for them, and re-layouts: 129 us -> 101 us
    pallas_call x1 -> x2, Pallas kernels: 212 us -> 412 us  [the longest x1 218 us: gather_all(): pl.pallas_call(functools.partial(gather_kernel, chunks, n), in_specs=[pl....]
    all_gather x2, waiting for transfers between devices: 115 us -> 4.83 us  [gather_rows(): return lax.all_gather(values, 'expert', axis=0, tiled=False)]
    unnamed x1 -> x0, blocking collectives: 85.7 us -> none
    ppermute x9 -> x10, waiting for transfers between devices: 225 us -> 147 us  [swap(): return lax.ppermute(values, 'dp', [(0, 1), (1, 0)])]
    all_gather x2 -> x0, waiting for transfers between devices: 19 us -> none  [the longest x1 17.2 us: local(): lax.all_gather(jnp.concatenate([heads_apart(query_weight, heads), latent_...]
    pallas_call x3 -> x5, Pallas kernels: 270 us -> 283 us  [by_block(): pl.pallas_call(kernel, grid=(count,), in_specs=[block(a) for a in blocked...]
    reduce_scatter x2 -> x3, waiting for transfers between devices: 37.6 us -> 49.4 us  [scatter_rows(): lax.psum_scatter(flat(values), 'expert', scatter_dimension=0, tiled=True)]
    dot_general x20 -> x22, matrix products: 258 us -> 265 us  [mm(): return jnp.einsum(spec, a, b, preferred_element_type=f32)]
  transfers between devices with their start and end apart: 17 -> 18, of which waited for: 10 -> 6; matrix products, arithmetic and copies ran while one was open for 26% -> 27% of each run, Pallas kernels for 28% -> 47%
where the time goes in v2:
time: 1450 us; the launch traced here: 1440 us
  Pallas kernels  773 us (53%)
  matrix products  265 us (18%)
  waiting for transfers between devices  207 us (14%)
  local copies, waits for them, and re-layouts  101 us (7%)
  other arithmetic  43.4 us (3%)
  starting transfers between devices  31.1 us (2%)
  between operations  15.4 us (1%)
    pallas_call x5, Pallas kernels, by_block(): pl.pallas_call(kernel, grid=(count,), in_specs=[block(a) for a in blocked...  283 us
    dot_general x22, matrix products, mm(): return jnp.einsum(spec, a, b, preferred_element_type=f32)  265 us
    pallas_call x1, Pallas kernels, gather_all(): pl.pallas_call(functools.partial(gather_kernel, chunks, n), in_specs=[pl....  218 us
    pallas_call x1, Pallas kernels, grad_sums(): pl.pallas_call(functools.partial(grad_sum_kernel, chunks, n), in_specs=[p...  194 us
    ppermute x10, waiting for transfers between devices, swap(): return lax.ppermute(values, 'dp', [(0, 1), (1, 0)])  147 us
    pallas_call x1, Pallas kernels, attend_back(): pl.pallas_call(functools.partial(attend_back_kernel, sizes), grid=(heads...  50.7 us
    reduce_scatter x3, waiting for transfers between devices, scatter_rows(): lax.psum_scatter(flat(values), 'expert', scatter_dimension=0, tiled=True)  49.4 us
  transfers between devices with their start and end apart: 18, of which 6 were waited for; matrix products, arithmetic and copies ran while one was open for 27% of the time, Pallas kernels for 47%

profile of v2, /device:TPU:0, one launch (start us, length us, event | category | flops | bytes accessed | tf_op | source)
XLA Modules:
  0.0 1435.0 jit_solution(4693239175535814194)
XLA Ops:
  13.7 218.4 %gather_all.1 = (bf16[2,2,2,2,2,16,128]{6,5,4,3,2,1,0:T(8,128)(2,1)}, bf16[2,2,2,2,2,64,3712]{6,5,4,3,2,1,0:T(8,128)(2,1)}, bf16[2,2,2,2,2,128,512]{6,5,4,3,2,1,...) custom-call(bf16[16,128]{1,0:T(8,128)(2,1)} %fusion.131.refs_0_, bf16[64,3712]{1,0:T(8,128)(2,1)} %fusion.102.refs_1_, ...), custom_call_target="tpu_custom_call" | custom-call | bytes 664200000 | tf_op jit(solution)/shard_map/gather_all/pallas_call | solution.py:416
  234.7 12.0 fusion.65.nope_ref.rope_ref
  257.8 8.2 all-to-all-start.1
  271.2 7.2 convolution_convert_fusion.1.kv_ref
  278.5 26.8 %attend.1 = bf16[512,2048]{1,0:T(8,128)(2,1)S(1)} custom-call(f32[512,3712]{1,0:T(8,128)} %copy-done.7, f32[512,3712]{1,0:T(8,128)} %copy-done.7, f32[512,128]{1,0:T(8,128)S(1)} %get-tuple-element.253.cos_ref, f32[512,128]{1,0:T(8,128)S(1)} %get-tuple-element.254.sin_ref, bf16[1024,4096]{1,0:T(8,128)(2,1)} %convolution_convert_fusion.1.kv_ref, ...), custom_call_target="tpu_custom_call" | custom-call | bytes 99630000 | tf_op jit(solution)/shard_map/attend/pallas_call | solution.py:182
  330.5 7.3 all-to-all-start
  339.3 5.7 all-to-all-done.weight_ref
  352.6 117.2 %collective-permute-done.2 = bf16[1024,528]{0,1:T(8,128)(2,1)} collective-permute-done((bf16[1024,528]{0,1:T(8,128)(2,1)}, bf16[1024,528]{0,1:T(8,128)(2,1)}, u32[]{:S(2)}, u32[]{:S(2)}) %collective-permute-start.2) | collective-permute-done | bytes 1081376 | tf_op jit(solution)/shard_map/ppermute | solution.py:550
  484.8 85.9 %experts_forward.1 = (bf16[16,256,2048]{2,1,0:T(8,128)(2,1)}, bf16[16,256,1408]{2,1,0:T(8,128)(2,1)}, bf16[16,256,1408]{2,1,0:T(8,128)(2,1)}, bf16[16,256,1408]{...) custom-call(s32[16,1,512]{2,1,0:T(1,128)} %copy.209.place_ref, ...), custom_call_target="tpu_custom_call" | custom-call | flops 73014444032 | bytes 111181824 | tf_op jit(solution)/shard_map/experts_forward/pallas_call | solution.py:305
  570.7 54.4 %experts_hidden.1 = (bf16[16,256,2048]{2,1,0:T(8,128)(2,1)}, bf16[16,256,1408]{2,1,0:T(8,128)(2,1)}, bf16[16,256,1408]{2,1,0:T(8,128)(2,1)}, bf16[16,512,512]{2,1,0:T(8,128)(2,1)}) custom-call(s32[16,1,512]{2,1,0:T(1,128)} %copy.209.place_ref, f32[16,1,512]{2,1,0:T(1,128)} %copy-done.47, bf16[16,512,2048]{2,1,0:T(8,128)(2,1)} %bitcast.192, ...), custom_call_target="tpu_custom_call" | custom-call | flops 40802189312 | bytes 120127488 | tf_op jit(solution)/shard_map/experts_hidden/pallas_call | solution.py:305
  625.1 45.2 %experts_rows.2 = bf16[16,512,1024]{2,1,0:T(8,128)(2,1)} custom-call(s32[16,1,512]{2,1,0:T(1,128)} %copy.209.place_ref, bf16[16,256,1408]{2,1,0:T(8,128)(2,1)} %get-tuple-element.75.d_gate_ref, bf16[16,256,1408]{2,1,0:T(8,128)(2,1)} %get-tuple-element.76.d_up_ref, bf16[16,512,512]{2,1,0:T(8,128)(2,1)} %get-tuple-element.78.d_shared_ref, ...), custom_call_target="tpu_custom_call" | custom-call | flops 36507222016 | bytes 55083008 | tf_op jit(solution)/shard_map/experts_rows/pallas_call | solution.py:305
  670.4 19.4 %fusion.50 = bf16[1024,1408]{1,0:T(8,128)(2,1)} fusion(bf16[4096,1408]{1,0:T(8,128)(2,1)} %bitcast.217, bf16[4096,2048]{1,0:T(8,128)(2,1)} %bitcast.205), kind=kOutput, calls=%fused_computation.58 | convolution fusion | flops 11812601856 | bytes 22806528 | tf_op jit(solution)/shard_map/rd,rf->df/dot_general | solution.py:22
  691.2 21.2 %fusion.53 = bf16[1024,1408]{1,0:T(8,128)(2,1)} fusion(bf16[4096,1408]{1,0:T(8,128)(2,1)} %bitcast.215, bf16[4096,2048]{1,0:T(8,128)(2,1)} %bitcast.206), kind=kOutput, calls=%fused_computation.59 | convolution fusion | flops 11812601856 | bytes 22806528 | tf_op jit(solution)/shard_map/rd,rf->df/dot_general | solution.py:22
  713.2 45.2 %experts_rows.3 = bf16[16,512,1024]{2,1,0:T(8,128)(2,1)} custom-call(s32[16,1,512]{2,1,0:T(1,128)} %copy.209.place_ref, bf16[16,256,1408]{2,1,0:T(8,128)(2,1)} %get-tuple-element.75.d_gate_ref, bf16[16,256,1408]{2,1,0:T(8,128)(2,1)} %get-tuple-element.76.d_up_ref, bf16[16,512,512]{2,1,0:T(8,128)(2,1)} %get-tuple-element.78.d_shared_ref, ...), custom_call_target="tpu_custom_call" | custom-call | flops 36507222016 | bytes 55083008 | tf_op jit(solution)/shard_map/experts_rows/pallas_call | solution.py:305
  758.6 19.9 %fusion.56 = bf16[1408,1024]{1,0:T(8,128)(2,1)} fusion(bf16[4096,1408]{1,0:T(8,128)(2,1)} %bitcast.213, bf16[4096,2048]{1,0:T(8,128)(2,1)} %bitcast.209), kind=kOutput, calls=%fused_computation.60 | convolution fusion | flops 11812601856 | bytes 22806528 | tf_op jit(solution)/shard_map/rf,rd->fd/dot_general | solution.py:22
  779.7 9.1 fusion.76
  788.7 15.0 %fusion.72 = bf16[1024,512]{0,1:T(8,128)(2,1)S(1)} fusion(bf16[8192,512]{1,0:T(8,128)(2,1)} %bitcast.219, bf16[8192,2048]{1,0:T(8,128)(2,1)} %all-gather.7.cloned.1.call-done), kind=kOutput, calls=%fused_computation.88 | convolution fusion | flops 8590458880 | bytes 26214400 | tf_op jit(solution)/shard_map/rd,rf->df/dot_general | solution.py:22
  807.0 51.9 %experts_output.1 = (bf16[16,512,1664]{2,1,0:T(8,128)(2,1)}, bf16[16,512,384]{2,1,0:T(8,128)(2,1)}) custom-call(s32[16,1,512]{2,1,0:T(1,128)} %copy.209.place_ref, f32[16,1,512]{2,1,0:T(1,128)} %copy-done.47, bf16[16,256,1408]{2,1,0:T(8,128)(2,1)} %get-tuple-element.80.act_ref, bf16[16,512,256]{2,1,0:T(8,128)(2,1)} %get-tuple-element.82.act_s_ref, ...), custom_call_target="tpu_custom_call" | custom-call | flops 40802189312 | bytes 56164352 | tf_op jit(solution)/shard_map/experts_output/pallas_call | solution.py:305
  858.9 19.0 %fusion.6 = f32[1024,512]{0,1:T(8,128)} fusion(bf16[8192,512]{1,0:T(8,128)(2,1)} %bitcast.220, bf16[8192,2048]{1,0:T(8,128)(2,1)} %all-gather.7.cloned.1.call-done), kind=kOutput, calls=%fused_computation.6 | convolution fusion | flops 8589934592 | bytes 27262976 | tf_op jit(solution)/shard_map/rd,rf->df/dot_general | solution.py:22
  877.9 9.8 fusion.4
  887.7 24.3 %collective-permute-done.7 = bf16[1024,768]{0,1:T(8,128)(2,1)} collective-permute-done((bf16[1024,768]{0,1:T(8,128)(2,1)}, bf16[1024,768]{0,1:T(8,128)(2,1)}, u32[]{:S(2)}, u32[]{:S(2)}) %collective-permute-start.7) | collective-permute-done | bytes 1572896 | tf_op jit(solution)/shard_map/ppermute | solution.py:550
  923.2 20.6 %convert_add_fusion.2 = f32[1024,1408]{1,0:T(8,128)} fusion(bf16[1024,1408]{1,0:T(8,128)(2,1)} %collective-permute-done.4, bf16[4096,1408]{1,0:T(8,128)(2,1)} %bitcast.218, bf16[4096,2048]{1,0:T(8,128)(2,1)} %bitcast.207), kind=kOutput, calls=%fused_computation.25 | convolution fusion | flops 11814043648 | bytes 28573696 | tf_op jit(solution)/shard_map/rd,rf->df/dot_general | solution.py:22
  943.8 20.0 %convert_add_fusion.1 = f32[1024,1408]{1,0:T(8,128)} fusion(bf16[1024,1408]{1,0:T(8,128)(2,1)} %collective-permute-done.5, bf16[4096,1408]{1,0:T(8,128)(2,1)} %bitcast.216, bf16[4096,2048]{1,0:T(8,128)(2,1)} %bitcast.208), kind=kOutput, calls=%fused_computation.24 | convolution fusion | flops 11814043648 | bytes 28573696 | tf_op jit(solution)/shard_map/rd,rf->df/dot_general | solution.py:22
  963.9 17.2 %convert_add_fusion = f32[1408,1024]{1,0:T(8,128)} fusion(bf16[1408,1024]{1,0:T(8,128)(2,1)} %collective-permute-done.6, bf16[4096,1408]{1,0:T(8,128)(2,1)} %bitcast.214, bf16[4096,2048]{1,0:T(8,128)(2,1)S(1)} %bitcast.212), kind=kOutput, calls=%fused_computation.23 | convolution fusion | flops 11814043648 | bytes 28573696 | tf_op jit(solution)/shard_map/rf,rd->fd/dot_general | solution.py:22
  981.1 49.4 %reduce-scatter.6.cloned.1.call-done = bf16[512,1024]{1,0:T(8,128)(2,1)} async-done(((bf16[8192,1024]{1,0:T(8,128)(2,1)}), bf16[512,1024]{1,0:T(8,128)(2,1)}) %reduce-scatter.6.cloned.1.call-update) | async-done | bytes 1048592 | tf_op jit(solution)/shard_map/reduce_scatter | solution.py:741
  1045.3 11.8 convolution_convert_fusion.4.grad_ref
  1061.7 50.7 %attend_back.1 = (bf16[512,2048]{1,0:T(8,128)(2,1)S(1)}, bf16[512,1024]{1,0:T(8,128)(2,1)S(1)}, bf16[1024,4096]{1,0:T(8,128)(2,1)}, f32[1024,128]{1,0:T(8,128)S(1)}) custom-call(f32[512,3712]{1,0:T(8,128)} %copy-done.7, f32[512,3712]{1,0:T(8,128)} %copy-done.7, f32[512,128]{1,0:T(8,128)S(1)} %get-tuple-element.253.cos_ref, ...), custom_call_target="tpu_custom_call" | custom-call | bytes 188190000 | tf_op jit(solution)/shard_map/attend_back/pallas_call | solution.py:197
  1140.8 6.9 fusion.139
  1150.6 10.0 convolution_convert_fusion.2
  1182.5 15.0 %fusion.41 = (f32[512]{0:T(512)S(1)}, bf16[2048]{0:T(1024)(128)(2,1)S(1)}, f32[512,2048]{1,0:T(8,128)}) fusion(bf16[1,512,2048]{2,1,0:T(8,128)(2,1)} %param.18, f32[2048]{0:T(1024)S(1)} %copy-done.46, f32[512]{0:T(512)S(1)} %copy-done.58, bf16[2048,3712]{1,0:T(8,128)(2,1)} %bitcast.195, bf16[512,3648]{1,0:T(8,128)(2,1)} %concatenate.74), kind=kOutput, calls=%fused_computation.45 | convolution fusion | flops 7791965696 | bytes 25247744 | tf_op jit(solution)/shard_map/rk,dk->rd/dot_general | solution.py:22
  1198.8 14.1 convolution_convert_fusion
  1212.9 194.1 %grad_sums.1 = (f32[64,1024]{1,0:T(8,128)}, f32[64,1024]{1,0:T(8,128)}, f32[512,384]{1,0:T(8,128)}, f32[128,512]{1,0:T(8,128)}, f32[64,3712]{1,0:T(8,128)}, /*index=5*/f32[64,128]{1,0:T(8,128)}) custom-call(bf16[2,2,2,2,64,1024]{5,4,3,2,1,0:T(8,128)(2,1)} %bitcast.174, bf16[2,2,2,2,2,64,1024]{6,5,4,3,2,1,0:T(8,128)(2,1)} %bitcast.169, ...), custom_call_target="tpu_custom_call" | custom-call | bytes 627299968 | tf_op jit(solution)/shard_map/grad_sums/pallas_call | solution.py:529
  (307 shorter events, 186.8 us)
Async XLA Ops:
  7.2 306.4 %all-gather.5.cloned.1.call-start = ((), (), s32[]{:S(2)}) async-start(), calls=%async_computation.9 | async-start | bytes 35651584 | tf_op jit(solution)/shard_map/all_gather | solution.py:730
  10.5 223.7 %copy-start.19 = (bf16[1,512,2048]{2,1,0:T(8,128)(2,1)S(1)}, bf16[1,512,2048]{2,1,0:T(8,128)(2,1)}, u32[]{:S(2)}) copy-start(bf16[1,512,2048]{2,1,0:T(8,128)(2,1)} %param.18) | copy-start | bytes 6291460
  234.2 14.1 copy-start.48
  251.2 16.0 %collective-permute-start = (bf16[512,576]{0,1:T(8,128)(2,1)}, bf16[512,576]{0,1:T(8,128)(2,1)}, u32[]{:S(2)}, u32[]{:S(2)}) collective-permute-start(bf16[512,576]{0,1:T(8,128)(2,1)} %copy.196), channel_id=1, source_target_pairs={{0,16},{16,0},{1,17},{17,1},{2,18},{18,2},{3,19},{19,3},{4,20},{20... | collective-permute-start | bytes 1769480 | tf_op jit(solution)/shard_map/ppermute | solution.py:550
  257.8 55.8 %all-to-all-start.1 = ((bf16[16,64,3,176]{3,1,2,0:T(8,128)(2,1)}), bf16[16,64,3,176]{3,1,2,0:T(8,128)(2,1)}, u32[]{:S(2)}, u32[]{:S(2)}) async-start(bf16[16,64,3,176]{3,1,2,0:T(8,128)(2,1)} %copy.199), calls=%async_computation.1 | async-start | bytes 3145728 | tf_op jit(solution)/shard_map/all_to_all | solution.py:669
  266.0 218.8 %all-gather.7.cloned.1.call-start = ((), (), s32[]{:S(2)}) async-start(), calls=%async_computation.10 | async-start | bytes 35651584 | tf_op jit(solution)/shard_map/all_gather | solution.py:730
  266.2 43.9 %copy-start.38 = (f32[2048]{0:T(1024)}, f32[2048]{0:T(1024)S(1)}, u32[]{:S(2)}) copy-start(f32[2048]{0:T(1024)S(1)} %reshape.487) | copy-start | bytes 24580
  271.2 34.1 %slice-start = ((s8[8388608]{0:T(1024)(128)(4,1)}), s8[4194304]{0:T(1024)(128)(4,1)S(1)}, s32[]{:S(2)}) async-start(s8[8388608]{0:T(1024)(128)(4,1)} %bitcast.197), calls=%async_computation.11 | async-start | bytes 8388608
  278.5 26.9 %copy-start.20 = (bf16[1,512,2048]{2,1,0:T(8,128)(2,1)S(1)}, bf16[1,512,2048]{2,1,0:T(8,128)(2,1)}, u32[]{:S(2)}) copy-start(bf16[1,512,2048]{2,1,0:T(8,128)(2,1)} %param.18) | copy-start | bytes 6291460
  278.5 26.9 %slice-start.1 = ((s8[8388608]{0:T(1024)(128)(4,1)}), s8[4194304]{0:T(1024)(128)(4,1)S(1)}, s32[]{:S(2)}) async-start(s8[8388608]{0:T(1024)(128)(4,1)} %bitcast.197), calls=%async_computation.12 | async-start | bytes 8388608
  319.2 160.8 %collective-permute-start.1 = (bf16[1024,2816]{1,0:T(8,128)(2,1)}, bf16[1024,2816]{1,0:T(8,128)(2,1)}, u32[]{:S(2)}, u32[]{:S(2)}) collective-permute-start(bf16[1024,2816]{1,0:T(8,128)(2,1)} %constant_dynamic-update-slice_fusion.refs_0_.gate_up_ref), channel_id=1, source_target_pairs={{0,16},{16,0},{1,17},{17,1},{2,18},{18,2},{3,19},{19,3},{4,20},{20... | collective-permute-start | bytes 17301512 | tf_op jit(solution)/shard_map/ppermute | solution.py:550
  328.3 141.5 %collective-permute-start.2 = (bf16[1024,528]{0,1:T(8,128)(2,1)}, bf16[1024,528]{0,1:T(8,128)(2,1)}, u32[]{:S(2)}, u32[]{:S(2)}) collective-permute-start(bf16[1024,528]{0,1:T(8,128)(2,1)} %reshape.459), channel_id=1, source_target_pairs={{0,16},{16,0},{1,17},{17,1},{2,18},{18,2},{3,19},{19,3},{4,20},{20... | collective-permute-start | bytes 3244040 | tf_op jit(solution)/shard_map/ppermute | solution.py:550
  330.5 14.5 %all-to-all-start = ((f32[16,1,512]{2,1,0:T(1,128)}), f32[16,1,512]{2,1,0:T(1,128)S(1)}, u32[]{:S(2)}, u32[]{:S(2)}) async-start(f32[16,1,512]{2,1,0:T(1,128)} %all_to_all.14), calls=%async_computation | async-start | bytes 65536 | tf_op jit(solution)/shard_map/all_to_all | solution.py:635
  337.7 643.4 %reduce-scatter.4.cloned.1.call-start = ((), (), s32[]{:S(2)}) async-start(), calls=%async_computation.6 | async-start | bytes 17825792 | tf_op jit(solution)/shard_map/reduce_scatter | solution.py:741
  337.8 232.9 %collective-permute-start.3 = (bf16[1408,1024]{1,0:T(8,128)(2,1)}, bf16[1408,1024]{1,0:T(8,128)(2,1)}, u32[]{:S(2)}, u32[]{:S(2)}) collective-permute-start(bf16[1408,1024]{1,0:T(8,128)(2,1)} %bitcast.202), channel_id=1, source_target_pairs={{0,16},{16,0},{1,17},{17,1},{2,18},{18,2},{3,19},{19,3},{4,20},{20... | collective-permute-start | bytes 8650760 | tf_op jit(solution)/shard_map/ppermute | solution.py:550
  670.3 360.2 %reduce-scatter.6.cloned.1.call-start = ((), (), s32[]{:S(2)}) async-start(), calls=%async_computation.7 | async-start | bytes 17825792 | tf_op jit(solution)/shard_map/reduce_scatter | solution.py:741
  689.8 233.4 %collective-permute-start.4 = (bf16[1024,1408]{1,0:T(8,128)(2,1)}, bf16[1024,1408]{1,0:T(8,128)(2,1)}, u32[]{:S(2)}, u32[]{:S(2)}) collective-permute-start(bf16[1024,1408]{1,0:T(8,128)(2,1)} %fusion.50), channel_id=1, source_target_pairs={{0,16},{16,0},{1,17},{17,1},{2,18},{18,2},{3,19},{19,3},{4,20},{20... | collective-permute-start | bytes 8650760 | tf_op jit(solution)/shard_map/ppermute | solution.py:550
  712.4 231.4 %collective-permute-start.5 = (bf16[1024,1408]{1,0:T(8,128)(2,1)}, bf16[1024,1408]{1,0:T(8,128)(2,1)}, u32[]{:S(2)}, u32[]{:S(2)}) collective-permute-start(bf16[1024,1408]{1,0:T(8,128)(2,1)} %fusion.53), channel_id=1, source_target_pairs={{0,16},{16,0},{1,17},{17,1},{2,18},{18,2},{3,19},{19,3},{4,20},{20... | collective-permute-start | bytes 8650760 | tf_op jit(solution)/shard_map/ppermute | solution.py:550
  758.5 659.7 %reduce-scatter.8.cloned.1.call-start = ((), (), s32[]{:S(2)}) async-start(), calls=%async_computation.8 | async-start | bytes 28966912 | tf_op jit(solution)/shard_map/reduce_scatter | solution.py:741
  758.6 21.1 %copy-start.66 = (bf16[16,512,256]{2,1,0:T(8,128)(2,1)S(1)}, bf16[16,512,256]{2,1,0:T(8,128)(2,1)}, u32[]{:S(2)}) copy-start(bf16[16,512,256]{2,1,0:T(8,128)(2,1)} %get-tuple-element.82.act_s_ref) | copy-start | bytes 12582916
  778.4 185.4 %collective-permute-start.6 = (bf16[1408,1024]{1,0:T(8,128)(2,1)}, bf16[1408,1024]{1,0:T(8,128)(2,1)}, u32[]{:S(2)}, u32[]{:S(2)}) collective-permute-start(bf16[1408,1024]{1,0:T(8,128)(2,1)} %fusion.56), channel_id=1, source_target_pairs={{0,16},{16,0},{1,17},{17,1},{2,18},{18,2},{3,19},{19,3},{4,20},{20... | collective-permute-start | bytes 8650760 | tf_op jit(solution)/shard_map/ppermute | solution.py:550
  806.1 106.0 %collective-permute-start.7 = (bf16[1024,768]{0,1:T(8,128)(2,1)}, bf16[1024,768]{0,1:T(8,128)(2,1)}, u32[]{:S(2)}, u32[]{:S(2)}) collective-permute-start(bf16[1024,768]{0,1:T(8,128)(2,1)} %pad_maximum_fusion.5), channel_id=1, source_target_pairs={{0,16},{16,0},{1,17},{17,1},{2,18},{18,2},{3,19},{19,3},{4,20},{20... | collective-permute-start | bytes 4718600 | tf_op jit(solution)/shard_map/ppermute | solution.py:550
  877.9 34.1 %copy-start.30 = (f32[1024,512]{0,1:T(8,128)S(1)}, f32[1024,512]{0,1:T(8,128)}, u32[]{:S(2)}) copy-start(f32[1024,512]{0,1:T(8,128)} %fusion.6) | copy-start | bytes 6291460
  923.2 40.7 %slice-start.2 = ((s8[16777216]{0:T(1024)(128)(4,1)}), s8[4194304]{0:T(1024)(128)(4,1)S(1)}, s32[]{:S(2)}) async-start(s8[16777216]{0:T(1024)(128)(4,1)} %bitcast.210), calls=%async_computation.13 | async-start | bytes 8388608
  923.2 40.7 %slice-start.3 = ((s8[16777216]{0:T(1024)(128)(4,1)}), s8[4194304]{0:T(1024)(128)(4,1)S(1)}, s32[]{:S(2)}) async-start(s8[16777216]{0:T(1024)(128)(4,1)} %bitcast.210), calls=%async_computation.14 | async-start | bytes 8388608
  943.8 20.1 %slice-start.4 = ((s8[16777216]{0:T(1024)(128)(4,1)}), s8[4194304]{0:T(1024)(128)(4,1)S(1)}, s32[]{:S(2)}) async-start(s8[16777216]{0:T(1024)(128)(4,1)} %bitcast.210), calls=%async_computation.15 | async-start | bytes 8388608
  943.8 20.1 %slice-start.5 = ((s8[16777216]{0:T(1024)(128)(4,1)}), s8[4194304]{0:T(1024)(128)(4,1)S(1)}, s32[]{:S(2)}) async-start(s8[16777216]{0:T(1024)(128)(4,1)} %bitcast.210), calls=%async_computation.16 | async-start | bytes 8388608
  1033.7 85.3 %all-to-all-start.2 = ((bf16[16,64,3,176]{3,1,2,0:T(8,128)(2,1)}), bf16[16,64,3,176]{3,1,2,0:T(8,128)(2,1)}, u32[]{:S(2)}, u32[]{:S(2)}) async-start(bf16[16,64,3,176]{3,1,2,0:T(8,128)(2,1)} %copy.219), calls=%async_computation.5 | async-start | bytes 3145728 | tf_op jit(solution)/shard_map/all_to_all | solution.py:807
  1045.3 69.4 %copy-start.31 = (bf16[512,2048]{1,0:T(8,128)(2,1)}, bf16[512,2048]{1,0:T(8,128)(2,1)S(1)}, u32[]{:S(2)}) copy-start(bf16[512,2048]{1,0:T(8,128)(2,1)S(1)} %fusion.137) | copy-start | bytes 6291460
  1059.8 76.0 %collective-permute-start.8 = (bf16[1024,1024]{1,0:T(8,128)(2,1)}, bf16[1024,1024]{1,0:T(8,128)(2,1)}, u32[]{:S(2)}, u32[]{:S(2)}) collective-permute-start(bf16[1024,1024]{1,0:T(8,128)(2,1)} %convolution_convert_fusion.5), channel_id=1, source_target_pairs={{0,16},{16,0},{1,17},{17,1},{2,18},{18,2},{3,19},{19,3},{4,20},{20... | collective-permute-start | bytes 6291464 | tf_op jit(solution)/shard_map/ppermute | solution.py:550
  1150.4 15.3 %collective-permute-start.9 = (bf16[512,576]{0,1:T(8,128)(2,1)}, bf16[512,576]{0,1:T(8,128)(2,1)S(1)}, u32[]{:S(2)}, u32[]{:S(2)}) collective-permute-start(bf16[512,576]{0,1:T(8,128)(2,1)} %copy.216), channel_id=1, source_target_pairs={{0,16},{16,0},{1,17},{17,1},{2,18},{18,2},{3,19},{19,3},{4,20},{20... | collective-permute-start | bytes 1769480 | tf_op jit(solution)/shard_map/ppermute | solution.py:550
  1182.5 16.3 %copy-start.21 = (bf16[1,512,2048]{2,1,0:T(8,128)(2,1)S(1)}, bf16[1,512,2048]{2,1,0:T(8,128)(2,1)}, u32[]{:S(2)}) copy-start(bf16[1,512,2048]{2,1,0:T(8,128)(2,1)} %param.18) | copy-start | bytes 6291460
  (59 other events, 358.2 us)
Sparse Core Ops, SparseCore 0:
  10.6 248.2 all-gather.4
  313.7 171.0 all-gather.6
  670.4 178.6 reduce-scatter.3
  853.1 177.4 reduce-scatter.5
  1034.5 289.5 reduce-scatter.7

commit v3 on v2

--- a/solution.py
+++ b/solution.py
@@ -16,6 +16,7 @@
 f32 = jnp.float32
 bf16 = jnp.bfloat16
 MIB = 1 << 20
+TILE = 256
 
 
 def mm(spec, a, b):
@@ -229,45 +230,42 @@
     return [(ref, pl.ds(i * step, step)) for i, ref in enumerate(refs)]
 
 
-def forward_kernel(n, slots, place_ref, rows_ref, *refs):
-    weights, shared, outs = refs[:n], refs[n : 2 * n], refs[2 * n :]
-    picked_ref, act_ref, up_slope_ref, silu_ref, act_s_ref, up_slope_s_ref, silu_s_ref = outs
-    width = rows_ref.shape[-1]
-    picks = one_hot(place_ref, slots).astype(f32).astype(bf16)
-    picked_ref[0] = dot(picks, rows_ref[0], 1, 0).astype(bf16)
-    both = total([dot(picked_ref[0, :, at], w[...], 1, 0) for w, at in width_parts(weights, width)])
-    half = both.shape[1] // 2
-    silu, slope = silu_parts(both[:, :half])
-    up = both[:, half:]
-    act_ref[0] = (silu * up).astype(bf16)
-    up_slope_ref[0] = (up * slope).astype(bf16)
-    silu_ref[0] = silu.astype(bf16)
-    both = total([dot(rows_ref[0, :, at], w[...], 1, 0) for w, at in width_parts(shared, width)])
-    half = both.shape[1] // 2
-    silu, slope = silu_parts(both[:, :half])
-    up = both[:, half:]
-    act_s_ref[0] = (silu * up).astype(bf16)
-    up_slope_s_ref[0] = (up * slope).astype(bf16)
-    silu_s_ref[0] = silu.astype(bf16)
-
-
-def hidden_kernel(
-    n, slots, place_ref, weight_ref, grads_ref, us_ref, silu_ref, us_s_ref, silu_s_ref, *refs
-):
-    down, down_s = refs[:n], refs[n : 2 * n]
-    picked_ref, d_gate_ref, d_up_ref, d_shared_ref = refs[2 * n :]
+def hidden_kernel(n, slots, place_ref, weight_ref, grads_ref, *refs):
+    down, (picked_ref, d_act_ref) = refs[:n], refs[n:]
     width = grads_ref.shape[-1]
     hot = one_hot(place_ref, slots)
     slot_weight = jnp.sum(jnp.where(hot, weight_ref[0], 0.0), axis=1, keepdims=True)
     picks = hot.astype(f32).astype(bf16)
     picked_ref[0] = (dot(picks, grads_ref[0], 1, 0) * slot_weight).astype(bf16)
     d_act = total([dot(picked_ref[0, :, at], w[...], 1, 1) for w, at in width_parts(down, width)])
-    d_gate_ref[0] = (d_act * us_ref[0].astype(f32)).astype(bf16)
-    d_up_ref[0] = (d_act * silu_ref[0].astype(f32)).astype(bf16)
-    d_act = total([dot(grads_ref[0, :, at], w[...], 1, 0) for w, at in width_parts(down_s, width)])
-    half = d_act.shape[1]
-    d_shared_ref[0, :, :half] = (d_act * us_s_ref[0].astype(f32)).astype(bf16)
-    d_shared_ref[0, :, half:] = (d_act * silu_s_ref[0].astype(f32)).astype(bf16)
+    d_act_ref[0] = d_act.astype(bf16)
+
+
+def gated_tiles(values_ref, weights, d_act, act_ref, d_gate_ref, d_up_ref, up_first):
+    width, hidden = values_ref.shape[-1], act_ref.shape[-1]
+    for left in range(0, hidden, TILE):
+        wide = min(TILE, hidden - left)
+        here, above = pl.ds(left, wide), pl.ds(hidden + left, wide)
+        parts = width_parts(weights, width)
+        gate = total([dot(values_ref[0, :, at], w[:, here], 1, 0) for w, at in parts])
+        up = total([dot(values_ref[0, :, at], w[:, above], 1, 0) for w, at in parts])
+        silu, slope = silu_parts(gate)
+        d_tile = d_act[:, left : left + wide].astype(f32)
+        act_ref[0, :, here] = (silu * up).astype(bf16)
+        d_gate_ref[0, :, here] = (d_tile * up * slope).astype(bf16)
+        d_up_ref[0, :, pl.ds(up_first + left, wide)] = (d_tile * silu).astype(bf16)
+
+
+def forward_kernel(n, slots, place_ref, rows_ref, grads_ref, d_act_ref, *refs):
+    weights, shared, down_s, outs = refs[:n], refs[n : 2 * n], refs[2 * n : 3 * n], refs[3 * n :]
+    picked_ref, act_ref, d_gate_ref, d_up_ref, act_s_ref, d_shared_ref = outs
+    picks = one_hot(place_ref, slots).astype(f32).astype(bf16)
+    picked_ref[0] = dot(picks, rows_ref[0], 1, 0).astype(bf16)
+    gated_tiles(picked_ref, weights, d_act_ref.at[0], act_ref, d_gate_ref, d_up_ref, 0)
+    half = act_s_ref.shape[-1]
+    parts = width_parts(down_s, rows_ref.shape[-1])
+    d_act_s = total([dot(grads_ref[0, :, at], w[...], 1, 0) for w, at in parts])
+    gated_tiles(rows_ref, shared, d_act_s, act_s_ref, d_shared_ref, d_shared_ref, half)
 
 
 def rows_kernel(
@@ -362,9 +360,18 @@
 
 
 def gather_kernel(chunks, n, *refs):
-    ins, outs = refs[:n], refs[n : 2 * n]
-    own_sem, send_sem, recv_sem = refs[2 * n :]
+    ins, outs = refs[:n], refs[n + 1 : 2 * n + 1]
+    own_sem, send_sem, recv_sem, cross_sem = refs[2 * n + 2 :]
     partners, (core, dp, y, z_low, z_high) = neighbours()
+    crossing = pltpu.make_async_remote_copy(
+        src_ref=refs[n],
+        dst_ref=refs[2 * n + 1],
+        send_sem=cross_sem.at[0],
+        recv_sem=cross_sem.at[1],
+        device_id=partners[1],
+        device_id_type=pl.DeviceIdType.MESH,
+    )
+    crossing.start()
     mine = (dp, z_high, z_low, y, core)
     place = [4, 0, 3, 2, 1]
     own = [pltpu.make_async_copy(ins[i], outs[i].at[mine], own_sem.at[i]) for i in range(n)]
@@ -407,27 +414,32 @@
         copies[4, k].wait_recv()
     for copy in copies.values():
         copy.wait_send()
-
-
-def gather_all(arrays):
+    crossing.wait()
+
+
+def gather_all(arrays, crossed):
     chunks = chunks_of([a.shape for a in arrays])
     dims = (2, 2, 2, 2, 2)
     n = len(arrays)
-    gathered = pl.pallas_call(
+    *gathered, crossed = pl.pallas_call(
         functools.partial(gather_kernel, chunks, n),
-        in_specs=[pl.BlockSpec(memory_space=pl.ANY)] * n,
-        out_specs=[pl.BlockSpec(memory_space=pl.ANY)] * n,
-        out_shape=[jax.ShapeDtypeStruct((*dims, *a.shape), a.dtype) for a in arrays],
+        in_specs=[pl.BlockSpec(memory_space=pl.ANY)] * (n + 1),
+        out_specs=[pl.BlockSpec(memory_space=pl.ANY)] * (n + 1),
+        out_shape=[
+            *[jax.ShapeDtypeStruct((*dims, *a.shape), a.dtype) for a in arrays],
+            jax.ShapeDtypeStruct(crossed.shape, crossed.dtype),
+        ],
         scratch_shapes=[
             pltpu.SemaphoreType.DMA((n,)),
             pltpu.SemaphoreType.DMA((5, len(chunks))),
             pltpu.SemaphoreType.DMA((5, len(chunks))),
+            pltpu.SemaphoreType.DMA((2,)),
         ],
         compiler_params=pltpu.CompilerParams(collective_id=2, has_side_effects=True),
         cost_estimate=time_of(180),
         name="gather_all",
-    )(*arrays)
-    return [g.reshape(-1, a.shape[1]) for g, a in zip(gathered, arrays)]
+    )(*arrays, crossed)
+    return [g.reshape(-1, a.shape[1]) for g, a in zip(gathered, arrays)], crossed
 
 
 def add_rows(into, left, right):
@@ -645,13 +657,15 @@
     gains = jnp.pad(gains, ((0, 13), (0, -g1 % 128)))
     own_linear = jnp.concatenate([heads_apart(query_weight, heads), latent_weight], axis=1)
     own_linear = jnp.pad(own_linear, ((0, 0), (0, -linear_width % 128)))
-    shares = [gains, own_linear, expand_weight.T, output_weight.T]
+    shares = [gains, own_linear, expand_weight.T]
     if dp_count == 2 and groups == 16:
-        gains, query_latent, expand_t, output_t = gather_all(shares)
+        shares, down_other = gather_all(shares, expert_down[0])
+        down_e = [expert_down[0], down_other]
     else:
-        gains, query_latent, expand_t, output_t = [
-            lax.all_gather(v, both, axis=0, tiled=True) for v in shares
-        ]
+        shares = [lax.all_gather(v, both, axis=0, tiled=True) for v in shares]
+        down_e = weight_parts(expert_down[0], 1, dp_count)
+    gains, query_latent, expand_t = shares
+    output_t = lax.all_gather(output_weight.T, both, axis=0, tiled=True)
     gains = gains.reshape(shards, 16, -1)
     first_gain = gains[:, 0, :g1].reshape(-1).astype(f32)
     second_gain = gains[:, 1, :g1].reshape(-1).astype(f32)
@@ -676,9 +690,8 @@
     gate_up_s = [c[:, :2].reshape(-1, 2 * padded_s) for c in wide_s]
     down_s_t = [c[:, 2] for c in wide_s]
 
-    own_e = after((expert_gate[0], expert_up[0], expert_down[0]), query_latent)
-    gate_up_e = weight_parts(jnp.concatenate(own_e[:2], axis=1), 0, dp_count)
-    down_e = weight_parts(own_e[2], 1, dp_count)
+    own_e = after((expert_gate[0], expert_up[0]), shared_cols)
+    gate_up_e = weight_parts(jnp.concatenate(own_e, axis=1), 0, dp_count)
 
     token_values = tokens[0].astype(f32)
     scale_one = lax.rsqrt(jnp.mean(token_values * token_values, axis=-1, keepdims=True) + epsilon)
@@ -743,25 +756,25 @@
     n = len(gate_up_e)
     hidden = expert_gate.shape[2]
     block_of = lambda rows, columns: jax.ShapeDtypeStruct((groups, rows, columns), bf16)
-    wide = [block_of(slots, hidden)] * 3
-    wide_shared = [block_of(length, padded_s)] * 3
+    wide = block_of(slots, hidden)
+    wide_shared = block_of(length, padded_s)
     aside = 3 * width // 16
     unit = 2 * groups * width
-    picked, act_e, up_slope, silu, act_s, up_slope_s, silu_s = by_block(
+    picked_grad, d_act = by_block(
+        functools.partial(hidden_kernel, n, slots),
+        "experts_hidden",
+        [place, row_weights, grads_all],
+        down_e,
+        [block_of(slots, width), wide],
+        unit * slots * (length + hidden),
+    )
+    picked, act_e, d_gate, d_up, act_s, d_shared = by_block(
         functools.partial(forward_kernel, n, slots),
         "experts_forward",
-        [place, rows_all],
-        [*gate_up_e, *gate_up_s],
-        [block_of(slots, width), *wide, *wide_shared],
-        unit * (slots * (length + 2 * hidden) + 2 * length * padded_s),
-    )
-    picked_grad, d_gate, d_up, d_shared = by_block(
-        functools.partial(hidden_kernel, n, slots),
-        "experts_hidden",
-        [place, row_weights, grads_all, up_slope, silu, up_slope_s, silu_s],
-        [*down_e, *down_s_t],
-        [block_of(slots, width), *wide[:2], block_of(length, 2 * padded_s)],
-        unit * (slots * (length + hidden) + length * padded_s),
+        [place, rows_all, grads_all, d_act],
+        [*gate_up_e, *gate_up_s, *down_s_t],
+        [block_of(slots, width), wide, wide, wide, wide_shared, block_of(length, 2 * padded_s)],
+        unit * (slots * (length + 2 * hidden) + 3 * length * padded_s),
     )
     d_rows = []
     for weights, weights_s in zip(gate_up_e, gate_up_s):
@@ -801,12 +814,13 @@
         0,
     )
     grad_s = grad_s.reshape(groups, rows_w, 3, padded_s)[..., :part_s].astype(bf16)
+    d_rows[0] = d_rows[0].astype(f32)
     d_rows, grad_gate_e, grad_up_e, grad_down_e, grad_s, out_parts = lax.optimization_barrier(
         (d_rows, grad_gate_e, grad_up_e, grad_down_e, grad_s, out_parts)
     )
     grad_s = lax.all_to_all(grad_s, "expert", split_axis=0, concat_axis=0, tiled=True)
     grad_s = grad_s.transpose(2, 1, 0, 3).reshape(3, rows_w, hidden_s).astype(f32)
-    d_rows_own = turned(jnp.concatenate(d_rows, axis=1), dp_count).astype(f32)
+    d_rows_own = turned(jnp.concatenate([d.astype(f32) for d in d_rows], axis=1), dp_count)
 
     out_grad = cotangent[0].astype(f32)
     middle_part, second_gain_grad = norm_back(d_rows_own, normed_two, scale_two, second_gain)

time: 1450 us -> 1440 us (level)
    ppermute x10 -> x9, waiting for transfers between devices: 147 us -> 112 us  [swap(): return lax.ppermute(values, 'dp', [(0, 1), (1, 0)])]
    all_gather x2, waiting for transfers between devices: 4.83 us -> 31.3 us  [gather_rows(): return lax.all_gather(values, 'expert', axis=0, tiled=False)]
    pallas_call x1, Pallas kernels: 218 us -> 202 us  [gather_all(): pl.pallas_call(functools.partial(gather_kernel, chunks, n), in_specs=[pl....]
  transfers between devices with their start and end apart: 18 -> 17, of which waited for: 6 -> 8; matrix products, arithmetic and copies ran while one was open for 27% -> 28% of each run, Pallas kernels for 47% -> 43%
where the time goes in v3:
time: 1440 us; the launch traced here: 1430 us
  Pallas kernels  759 us (53%)
  matrix products  271 us (19%)
  waiting for transfers between devices  196 us (14%)
  local copies, waits for them, and re-layouts  101 us (7%)
  other arithmetic  54.2 us (4%)
  starting transfers between devices  20.7 us (1%)
  between operations  15.4 us (1%)
    pallas_call x5, Pallas kernels, by_block(): pl.pallas_call(kernel, grid=(count,), in_specs=[block(a) for a in blocked...  288 us
    dot_general x22, matrix products, mm(): return jnp.einsum(spec, a, b, preferred_element_type=f32)  271 us
    pallas_call x1, Pallas kernels, gather_all(): pl.pallas_call(functools.partial(gather_kernel, chunks, n), in_specs=[pl....  202 us
    pallas_call x1, Pallas kernels, grad_sums(): pl.pallas_call(functools.partial(grad_sum_kernel, chunks, n), in_specs=[p...  191 us
    ppermute x9, waiting for transfers between devices, swap(): return lax.ppermute(values, 'dp', [(0, 1), (1, 0)])  112 us
    reduce_scatter x3, waiting for transfers between devices, scatter_rows(): lax.psum_scatter(flat(values), 'expert', scatter_dimension=0, tiled=True)  51.1 us
    pallas_call x1, Pallas kernels, attend_back(): pl.pallas_call(functools.partial(attend_back_kernel, sizes), grid=(heads...  50.7 us
    all_gather x2, waiting for transfers between devices, gather_rows(): return lax.all_gather(values, 'expert', axis=0, tiled=False)  31.3 us
  transfers between devices with their start and end apart: 17, of which 8 were waited for; matrix products, arithmetic and copies ran while one was open for 28% of the time, Pallas kernels for 43%

profile of v3, /device:TPU:0, one launch (start us, length us, event | category | flops | bytes accessed | tf_op | source)
XLA Modules:
  0.0 1429.3 jit_solution(8399833404826048197)
XLA Ops:
  18.3 201.7 %gather_all.1 = (bf16[2,2,2,2,2,16,128]{6,5,4,3,2,1,0:T(8,128)(2,1)}, bf16[2,2,2,2,2,64,3712]{6,5,4,3,2,1,0:T(8,128)(2,1)}, bf16[2,2,2,2,2,128,512]{6,5,4,3,2,1,0:T(8,128)(2,1)}, bf16[1408,1024]{1,0:T(8,128)(2,1)}) custom-call(bf16[16,128]{1,0:T(8,128)(2,1)} %fusion.125.refs_0_, bf16[64,3712]{1,0:T(8,128)(2,1)} %fusion.96.refs_1_, ...), custom_call_target="tpu_custom_call" | custom-call | bytes 664200000 | tf_op jit(solution)/shard_map/gather_all/pallas_call | solution.py:424
  230.8 12.0 fusion.59.nope_ref.rope_ref
  249.9 13.2 collective-permute-done
  273.9 27.4 %attend.1 = bf16[512,2048]{1,0:T(8,128)(2,1)S(1)} custom-call(f32[512,3712]{1,0:T(8,128)} %copy-done.7, f32[512,3712]{1,0:T(8,128)} %copy-done.7, f32[512,128]{1,0:T(8,128)S(1)} %get-tuple-element.245.cos_ref, f32[512,128]{1,0:T(8,128)S(1)} %get-tuple-element.246.sin_ref, bf16[1024,4096]{1,0:T(8,128)(2,1)} %convolution_convert_fusion.1.kv_ref, ...), custom_call_target="tpu_custom_call" | custom-call | bytes 99630000 | tf_op jit(solution)/shard_map/attend/pallas_call | solution.py:183
  302.6 9.3 multiply_reduce_fusion.2
  315.4 26.8 %all-gather.8.cloned.1.call-done = bf16[8192,2048]{1,0:T(8,128)(2,1)} async-done(((bf16[512,2048]{1,0:T(8,128)(2,1)}), bf16[8192,2048]{1,0:T(8,128)(2,1)}) %all-gather.8.cloned.1.call-update) | async-done | bytes 33554448 | tf_op jit(solution)/shard_map/all_gather | solution.py:743
  351.5 24.6 %collective-permute-done.1 = bf16[1024,528]{0,1:T(8,128)(2,1)S(1)} collective-permute-done((bf16[1024,528]{0,1:T(8,128)(2,1)S(1)}, bf16[1024,528]{0,1:T(8,128)(2,1)S(1)}, u32[]{:S(2)}, u32[]{:S(2)}) %collective-permute-start.1) | collective-permute-done | bytes 1081376 | tf_op jit(solution)/shard_map/ppermute | solution.py:562
  384.1 11.8 all_to_all.22.weight_ref
  413.5 42.6 %experts_hidden.1 = (bf16[16,256,2048]{2,1,0:T(8,128)(2,1)}, bf16[16,256,1408]{2,1,0:T(8,128)(2,1)}) custom-call(s32[16,1,512]{2,1,0:T(1,128)} %copy.209.place_ref, f32[16,1,512]{2,1,0:T(1,128)} %copy-done.40, bf16[16,512,2048]{2,1,0:T(8,128)(2,1)} %bitcast.192, bf16[1408,1024]{1,0:T(8,128)(2,1)} %bitcast.170, bf16[1408,1024]{1,0:T(8,128)(2,1)} %get-tuple-element.63.refs_1_), custom_call_target="tpu_custom_call" | custom-call | flops 32212254720 | bytes 67698688 | tf_op jit(solution)/shard_map/experts_hidden/pallas_call | solution.py:303
  456.1 52.4 %collective-permute-done.2.refs_1_.gate_up_ref = bf16[1024,2816]{1,0:T(8,128)(2,1)} collective-permute-done((bf16[1024,2816]{1,0:T(8,128)(2,1)}, bf16[1024,2816]{1,0:T(8,128)(2,1)}, u32[]{:S(2)}, u32[]{:S(2)}) %collective-permute-start.2) | collective-permute-done | bytes 5767200 | tf_op jit(solution)/shard_map/ppermute | solution.py:562
  513.0 101.7 %experts_forward.1 = (bf16[16,256,2048]{2,1,0:T(8,128)(2,1)}, bf16[16,256,1408]{2,1,0:T(8,128)(2,1)}, bf16[16,256,1408]{2,1,0:T(8,128)(2,1)}, bf16[16,256,1408]{...) custom-call(s32[16,1,512]{2,1,0:T(1,128)} %copy.209.place_ref, ...), custom_call_target="tpu_custom_call" | custom-call | flops 81604378624 | bytes 157319168 | tf_op jit(solution)/shard_map/experts_forward/pallas_call | solution.py:303
  614.8 45.3 %experts_rows.2 = bf16[16,512,1024]{2,1,0:T(8,128)(2,1)} custom-call(s32[16,1,512]{2,1,0:T(1,128)} %copy.209.place_ref, bf16[16,256,1408]{2,1,0:T(8,128)(2,1)} %get-tuple-element.67.d_gate_ref, bf16[16,256,1408]{2,1,0:T(8,128)(2,1)} %get-tuple-element.68.d_up_ref, bf16[16,512,512]{2,1,0:T(8,128)(2,1)} %get-tuple-element.70.d_shared_ref, ...), custom_call_target="tpu_custom_call" | custom-call | flops 36507222016 | bytes 55083008 | tf_op jit(solution)/shard_map/experts_rows/pallas_call | solution.py:303
  660.3 13.0 fusion.70
  673.3 17.9 %fusion.66 = bf16[1024,512]{0,1:T(8,128)(2,1)S(1)} fusion(bf16[8192,512]{1,0:T(8,128)(2,1)} %bitcast.215, bf16[8192,2048]{1,0:T(8,128)(2,1)} %all-gather.10.cloned.1.call-done), kind=kOutput, calls=%fused_computation.85 | convolution fusion | flops 8590458880 | bytes 26214400 | tf_op jit(solution)/shard_map/rd,rf->df/dot_general | solution.py:23
  694.9 45.9 %experts_rows.3 = bf16[16,512,1024]{2,1,0:T(8,128)(2,1)} custom-call(s32[16,1,512]{2,1,0:T(1,128)} %copy.209.place_ref, bf16[16,256,1408]{2,1,0:T(8,128)(2,1)} %get-tuple-element.67.d_gate_ref, bf16[16,256,1408]{2,1,0:T(8,128)(2,1)} %get-tuple-element.68.d_up_ref, bf16[16,512,512]{2,1,0:T(8,128)(2,1)} %get-tuple-element.70.d_shared_ref, ...), custom_call_target="tpu_custom_call" | custom-call | flops 36507222016 | bytes 55083008 | tf_op jit(solution)/shard_map/experts_rows/pallas_call | solution.py:303
  741.4 19.4 %fusion.44 = bf16[1024,1408]{1,0:T(8,128)(2,1)} fusion(bf16[4096,1408]{1,0:T(8,128)(2,1)} %bitcast.213, bf16[4096,2048]{1,0:T(8,128)(2,1)} %bitcast.205), kind=kOutput, calls=%fused_computation.54 | convolution fusion | flops 11812601856 | bytes 22806528 | tf_op jit(solution)/shard_map/rd,rf->df/dot_general | solution.py:23
  761.3 19.4 %fusion.47 = bf16[1024,1408]{1,0:T(8,128)(2,1)} fusion(bf16[4096,1408]{1,0:T(8,128)(2,1)} %bitcast.211, bf16[4096,2048]{1,0:T(8,128)(2,1)} %bitcast.206), kind=kOutput, calls=%fused_computation.55 | convolution fusion | flops 11812601856 | bytes 22806528 | tf_op jit(solution)/shard_map/rd,rf->df/dot_general | solution.py:23
  782.2 16.8 %fusion.50 = bf16[1408,1024]{1,0:T(8,128)(2,1)} fusion(bf16[4096,1408]{1,0:T(8,128)(2,1)} %bitcast.209, bf16[4096,2048]{1,0:T(8,128)(2,1)S(1)} %bitcast.201), kind=kOutput, calls=%fused_computation.56 | convolution fusion | flops 11812601856 | bytes 22806528 | tf_op jit(solution)/shard_map/rf,rd->fd/dot_general | solution.py:23
  799.5 52.6 %experts_output.1 = (bf16[16,512,1664]{2,1,0:T(8,128)(2,1)}, bf16[16,512,384]{2,1,0:T(8,128)(2,1)}) custom-call(s32[16,1,512]{2,1,0:T(1,128)} %copy.209.place_ref, f32[16,1,512]{2,1,0:T(1,128)} %copy-done.40, bf16[16,256,1408]{2,1,0:T(8,128)(2,1)} %get-tuple-element.72.act_ref, bf16[16,512,256]{2,1,0:T(8,128)(2,1)} %get-tuple-element.74.act_s_ref, ...), custom_call_target="tpu_custom_call" | custom-call | flops 40802189312 | bytes 56164352 | tf_op jit(solution)/shard_map/experts_output/pallas_call | solution.py:303
  852.1 18.9 %fusion.6 = f32[1024,512]{0,1:T(8,128)} fusion(bf16[8192,512]{1,0:T(8,128)(2,1)} %bitcast.216, bf16[8192,2048]{1,0:T(8,128)(2,1)} %all-gather.10.cloned.1.call-done), kind=kOutput, calls=%fused_computation.6 | convolution fusion | flops 8589934592 | bytes 27262976 | tf_op jit(solution)/shard_map/rd,rf->df/dot_general | solution.py:23
  871.0 9.5 fusion.4
  891.6 20.2 %convert_add_fusion.2 = f32[1024,1408]{1,0:T(8,128)} fusion(bf16[1024,1408]{1,0:T(8,128)(2,1)} %collective-permute-done.3, bf16[4096,1408]{1,0:T(8,128)(2,1)} %bitcast.214, bf16[4096,2048]{1,0:T(8,128)(2,1)} %bitcast.207), kind=kOutput, calls=%fused_computation.25 | convolution fusion | flops 11814043648 | bytes 28573696 | tf_op jit(solution)/shard_map/rd,rf->df/dot_general | solution.py:23
  911.8 20.1 %convert_add_fusion.1 = f32[1024,1408]{1,0:T(8,128)} fusion(bf16[1024,1408]{1,0:T(8,128)(2,1)} %collective-permute-done.4, bf16[4096,1408]{1,0:T(8,128)(2,1)} %bitcast.212, bf16[4096,2048]{1,0:T(8,128)(2,1)} %bitcast.208), kind=kOutput, calls=%fused_computation.24 | convolution fusion | flops 11814043648 | bytes 28573696 | tf_op jit(solution)/shard_map/rd,rf->df/dot_general | solution.py:23
  932.0 17.1 %collective-permute-done.5 = bf16[1408,1024]{1,0:T(8,128)(2,1)} collective-permute-done((bf16[1408,1024]{1,0:T(8,128)(2,1)}, bf16[1408,1024]{1,0:T(8,128)(2,1)}, u32[]{:S(2)}, u32[]{:S(2)}) %collective-permute-start.5) | collective-permute-done | bytes 2883616 | tf_op jit(solution)/shard_map/ppermute | solution.py:562
  949.0 17.3 %convert_add_fusion = f32[1408,1024]{1,0:T(8,128)} fusion(bf16[1408,1024]{1,0:T(8,128)(2,1)} %collective-permute-done.5, bf16[4096,1408]{1,0:T(8,128)(2,1)} %bitcast.210, bf16[4096,2048]{1,0:T(8,128)(2,1)S(1)} %bitcast.204), kind=kOutput, calls=%fused_computation.23 | convolution fusion | flops 11814043648 | bytes 28573696 | tf_op jit(solution)/shard_map/rf,rd->fd/dot_general | solution.py:23
  969.2 51.1 %reduce-scatter.6.cloned.1.call-done = bf16[512,1024]{1,0:T(8,128)(2,1)} async-done(((bf16[8192,1024]{1,0:T(8,128)(2,1)}), bf16[512,1024]{1,0:T(8,128)(2,1)}) %reduce-scatter.6.cloned.1.call-update) | async-done | bytes 1048592 | tf_op jit(solution)/shard_map/reduce_scatter | solution.py:754
  1037.3 11.8 convolution_convert_fusion.4.grad_ref
  1053.6 50.7 %attend_back.1 = (bf16[512,2048]{1,0:T(8,128)(2,1)S(1)}, bf16[512,1024]{1,0:T(8,128)(2,1)S(1)}, bf16[1024,4096]{1,0:T(8,128)(2,1)}, f32[1024,128]{1,0:T(8,128)S(1)}) custom-call(f32[512,3712]{1,0:T(8,128)} %copy-done.7, f32[512,3712]{1,0:T(8,128)} %copy-done.7, f32[512,128]{1,0:T(8,128)S(1)} %get-tuple-element.245.cos_ref, ...), custom_call_target="tpu_custom_call" | custom-call | bytes 188190000 | tf_op jit(solution)/shard_map/attend_back/pallas_call | solution.py:198
  1142.8 10.0 convolution_convert_fusion.2
  1174.8 14.9 %fusion.35 = (f32[512]{0:T(512)S(1)}, bf16[2048]{0:T(1024)(128)(2,1)S(1)}, f32[512,2048]{1,0:T(8,128)}) fusion(bf16[1,512,2048]{2,1,0:T(8,128)(2,1)} %param.18, f32[2048]{0:T(1024)S(1)} %copy-done.39, f32[512]{0:T(512)S(1)} %copy-done.53, bf16[2048,3712]{1,0:T(8,128)(2,1)} %bitcast.196, bf16[512,3648]{1,0:T(8,128)(2,1)} %concatenate.74), kind=kOutput, calls=%fused_computation.37 | convolution fusion | flops 7791965696 | bytes 25247744 | tf_op jit(solution)/shard_map/rk,dk->rd/dot_general | solution.py:23
  1191.0 14.2 convolution_convert_fusion
  1205.2 191.5 %grad_sums.1 = (f32[64,1024]{1,0:T(8,128)}, f32[64,1024]{1,0:T(8,128)}, f32[512,384]{1,0:T(8,128)}, f32[128,512]{1,0:T(8,128)}, f32[64,3712]{1,0:T(8,128)}, /*index=5*/f32[64,128]{1,0:T(8,128)}) custom-call(bf16[2,2,2,2,64,1024]{5,4,3,2,1,0:T(8,128)(2,1)} %bitcast.173, bf16[2,2,2,2,2,64,1024]{6,5,4,3,2,1,0:T(8,128)(2,1)} %bitcast.165, ...), custom_call_target="tpu_custom_call" | custom-call | bytes 627299968 | tf_op jit(solution)/shard_map/grad_sums/pallas_call | solution.py:541
  (301 shorter events, 212.7 us)
Async XLA Ops:
  7.2 295.5 %all-gather.6.cloned.1.call-start = ((), (), s32[]{:S(2)}) async-start(), calls=%async_computation.6 | async-start | bytes 8650752 | tf_op jit(solution)/shard_map/all_gather | solution.py:668
  7.9 334.3 %all-gather.8.cloned.1.call-start = ((), (), s32[]{:S(2)}) async-start(), calls=%async_computation.10 | async-start | bytes 35651584 | tf_op jit(solution)/shard_map/all_gather | solution.py:743
  223.3 92.1 %all-to-all-start.1 = ((bf16[16,64,3,176]{3,1,2,0:T(8,128)(2,1)}), bf16[16,64,3,176]{3,1,2,0:T(8,128)(2,1)}, u32[]{:S(2)}, u32[]{:S(2)}) async-start(bf16[16,64,3,176]{3,1,2,0:T(8,128)(2,1)} %copy.199), calls=%async_computation.1 | async-start | bytes 3145728 | tf_op jit(solution)/shard_map/all_to_all | solution.py:683
  227.9 285.1 %all-gather.10.cloned.1.call-start = ((), (), s32[]{:S(2)}) async-start(), calls=%async_computation.11 | async-start | bytes 35651584 | tf_op jit(solution)/shard_map/all_gather | solution.py:743
  229.2 15.2 %copy-start.41 = (f32[512]{0:T(512)}, f32[512]{0:T(512)S(1)}, u32[]{:S(2)}) copy-start(f32[512]{0:T(512)S(1)} %reshape.482) | copy-start | bytes 6148
  230.3 12.8 copy-start.54
  230.3 12.8 copy-start.47
  247.3 15.8 %collective-permute-start = (bf16[512,576]{0,1:T(8,128)(2,1)}, bf16[512,576]{0,1:T(8,128)(2,1)}, u32[]{:S(2)}, u32[]{:S(2)}) collective-permute-start(bf16[512,576]{0,1:T(8,128)(2,1)} %copy.196), channel_id=1, source_target_pairs={{0,16},{16,0},{1,17},{17,1},{2,18},{18,2},{3,19},{19,3},{4,20},{20... | collective-permute-start | bytes 1769480 | tf_op jit(solution)/shard_map/ppermute | solution.py:562
  248.9 63.1 %copy-start.35 = (f32[2048]{0:T(1024)}, f32[2048]{0:T(1024)S(1)}, u32[]{:S(2)}) copy-start(f32[2048]{0:T(1024)S(1)} %reshape.483) | copy-start | bytes 24580
  342.3 624.1 %reduce-scatter.4.cloned.1.call-start = ((), (), s32[]{:S(2)}) async-start(), calls=%async_computation.7 | async-start | bytes 17825792 | tf_op jit(solution)/shard_map/reduce_scatter | solution.py:754
  349.9 30.8 %copy-start.18 = (bf16[1,1024,1408]{2,1,0:T(8,128)(2,1)S(1)}, bf16[1,1024,1408]{2,1,0:T(8,128)(2,1)}, u32[]{:S(2)}) copy-start(bf16[1,1024,1408]{2,1,0:T(8,128)(2,1)} %param.33) | copy-start | bytes 8650756
  349.9 26.1 %collective-permute-start.1 = (bf16[1024,528]{0,1:T(8,128)(2,1)S(1)}, bf16[1024,528]{0,1:T(8,128)(2,1)S(1)}, u32[]{:S(2)}, u32[]{:S(2)}) collective-permute-start(bf16[1024,528]{0,1:T(8,128)(2,1)S(1)} %reshape.454), channel_id=1, source_target_pairs={{0,16},{16,0},{1,17},{17,1},{2,18},{18,2},{3,19},{19,3},{4,20},{20... | collective-permute-start | bytes 3244040 | tf_op jit(solution)/shard_map/ppermute | solution.py:562
  382.5 126.0 %collective-permute-start.2 = (bf16[1024,2816]{1,0:T(8,128)(2,1)}, bf16[1024,2816]{1,0:T(8,128)(2,1)}, u32[]{:S(2)}, u32[]{:S(2)}) collective-permute-start(bf16[1024,2816]{1,0:T(8,128)(2,1)} %constant_dynamic-update-slice_fusion.refs_0_.gate_up_ref), channel_id=1, source_target_pairs={{0,16},{16,0},{1,17},{17,1},{2,18},{18,2},{3,19},{19,3},{4,20},{20... | collective-permute-start | bytes 17301512 | tf_op jit(solution)/shard_map/ppermute | solution.py:562
  660.0 360.3 %reduce-scatter.6.cloned.1.call-start = ((), (), s32[]{:S(2)}) async-start(), calls=%async_computation.8 | async-start | bytes 17825792 | tf_op jit(solution)/shard_map/reduce_scatter | solution.py:754
  693.6 187.0 %collective-permute-start.6 = (bf16[1024,768]{0,1:T(8,128)(2,1)}, bf16[1024,768]{0,1:T(8,128)(2,1)}, u32[]{:S(2)}, u32[]{:S(2)}) collective-permute-start(bf16[1024,768]{0,1:T(8,128)(2,1)} %pad_maximum_fusion.5), channel_id=1, source_target_pairs={{0,16},{16,0},{1,17},{17,1},{2,18},{18,2},{3,19},{19,3},{4,20},{20... | collective-permute-start | bytes 4718600 | tf_op jit(solution)/shard_map/ppermute | solution.py:562
  740.9 675.4 %reduce-scatter.8.cloned.1.call-start = ((), (), s32[]{:S(2)}) async-start(), calls=%async_computation.9 | async-start | bytes 28966912 | tf_op jit(solution)/shard_map/reduce_scatter | solution.py:754
  741.3 40.9 %slice-start = ((s8[16777216]{0:T(1024)(128)(4,1)}), s8[4194304]{0:T(1024)(128)(4,1)S(1)}, s32[]{:S(2)}) async-start(s8[16777216]{0:T(1024)(128)(4,1)} %bitcast.199), calls=%async_computation.12 | async-start | bytes 8388608
  741.4 40.9 %slice-start.1 = ((s8[16777216]{0:T(1024)(128)(4,1)}), s8[4194304]{0:T(1024)(128)(4,1)S(1)}, s32[]{:S(2)}) async-start(s8[16777216]{0:T(1024)(128)(4,1)} %bitcast.199), calls=%async_computation.13 | async-start | bytes 8388608
  760.7 130.9 %collective-permute-start.3 = (bf16[1024,1408]{1,0:T(8,128)(2,1)}, bf16[1024,1408]{1,0:T(8,128)(2,1)}, u32[]{:S(2)}, u32[]{:S(2)}) collective-permute-start(bf16[1024,1408]{1,0:T(8,128)(2,1)} %fusion.44), channel_id=1, source_target_pairs={{0,16},{16,0},{1,17},{17,1},{2,18},{18,2},{3,19},{19,3},{4,20},{20... | collective-permute-start | bytes 8650760 | tf_op jit(solution)/shard_map/ppermute | solution.py:562
  761.3 20.9 %slice-start.2 = ((s8[16777216]{0:T(1024)(128)(4,1)}), s8[4194304]{0:T(1024)(128)(4,1)S(1)}, s32[]{:S(2)}) async-start(s8[16777216]{0:T(1024)(128)(4,1)} %bitcast.199), calls=%async_computation.14 | async-start | bytes 8388608
  761.3 20.9 %slice-start.3 = ((s8[16777216]{0:T(1024)(128)(4,1)}), s8[4194304]{0:T(1024)(128)(4,1)S(1)}, s32[]{:S(2)}) async-start(s8[16777216]{0:T(1024)(128)(4,1)} %bitcast.199), calls=%async_computation.15 | async-start | bytes 8388608
  780.7 131.1 %collective-permute-start.4 = (bf16[1024,1408]{1,0:T(8,128)(2,1)}, bf16[1024,1408]{1,0:T(8,128)(2,1)}, u32[]{:S(2)}, u32[]{:S(2)}) collective-permute-start(bf16[1024,1408]{1,0:T(8,128)(2,1)} %fusion.47), channel_id=1, source_target_pairs={{0,16},{16,0},{1,17},{17,1},{2,18},{18,2},{3,19},{19,3},{4,20},{20... | collective-permute-start | bytes 8650760 | tf_op jit(solution)/shard_map/ppermute | solution.py:562
  799.0 150.0 %collective-permute-start.5 = (bf16[1408,1024]{1,0:T(8,128)(2,1)}, bf16[1408,1024]{1,0:T(8,128)(2,1)}, u32[]{:S(2)}, u32[]{:S(2)}) collective-permute-start(bf16[1408,1024]{1,0:T(8,128)(2,1)} %fusion.50), channel_id=1, source_target_pairs={{0,16},{16,0},{1,17},{17,1},{2,18},{18,2},{3,19},{19,3},{4,20},{20... | collective-permute-start | bytes 8650760 | tf_op jit(solution)/shard_map/ppermute | solution.py:562
  891.6 57.4 %slice-start.4 = ((s8[16777216]{0:T(1024)(128)(4,1)}), s8[4194304]{0:T(1024)(128)(4,1)S(1)}, s32[]{:S(2)}) async-start(s8[16777216]{0:T(1024)(128)(4,1)} %bitcast.202), calls=%async_computation.16 | async-start | bytes 8388608
  891.6 57.4 %slice-start.5 = ((s8[16777216]{0:T(1024)(128)(4,1)}), s8[4194304]{0:T(1024)(128)(4,1)S(1)}, s32[]{:S(2)}) async-start(s8[16777216]{0:T(1024)(128)(4,1)} %bitcast.202), calls=%async_computation.17 | async-start | bytes 8388608
  911.8 37.2 %slice-start.6 = ((s8[16777216]{0:T(1024)(128)(4,1)}), s8[4194304]{0:T(1024)(128)(4,1)S(1)}, s32[]{:S(2)}) async-start(s8[16777216]{0:T(1024)(128)(4,1)} %bitcast.202), calls=%async_computation.18 | async-start | bytes 8388608
  911.8 37.2 %slice-start.7 = ((s8[16777216]{0:T(1024)(128)(4,1)}), s8[4194304]{0:T(1024)(128)(4,1)S(1)}, s32[]{:S(2)}) async-start(s8[16777216]{0:T(1024)(128)(4,1)} %bitcast.202), calls=%async_computation.19 | async-start | bytes 8388608
  1023.5 87.4 %all-to-all-start.2 = ((bf16[16,64,3,176]{3,1,2,0:T(8,128)(2,1)}), bf16[16,64,3,176]{3,1,2,0:T(8,128)(2,1)}, u32[]{:S(2)}, u32[]{:S(2)}) async-start(bf16[16,64,3,176]{3,1,2,0:T(8,128)(2,1)} %copy.219), calls=%async_computation.5 | async-start | bytes 3145728 | tf_op jit(solution)/shard_map/all_to_all | solution.py:821
  1037.3 69.3 %copy-start.23 = (bf16[512,2048]{1,0:T(8,128)(2,1)}, bf16[512,2048]{1,0:T(8,128)(2,1)S(1)}, u32[]{:S(2)}) copy-start(bf16[512,2048]{1,0:T(8,128)(2,1)S(1)} %get-tuple-element.218) | copy-start | bytes 6291460
  1051.8 75.8 %collective-permute-start.7 = (bf16[1024,1024]{1,0:T(8,128)(2,1)}, bf16[1024,1024]{1,0:T(8,128)(2,1)}, u32[]{:S(2)}, u32[]{:S(2)}) collective-permute-start(bf16[1024,1024]{1,0:T(8,128)(2,1)} %convolution_convert_fusion.5), channel_id=1, source_target_pairs={{0,16},{16,0},{1,17},{17,1},{2,18},{18,2},{3,19},{19,3},{4,20},{20... | collective-permute-start | bytes 6291464 | tf_op jit(solution)/shard_map/ppermute | solution.py:562
  1142.8 15.3 %collective-permute-start.8 = (bf16[512,576]{0,1:T(8,128)(2,1)}, bf16[512,576]{0,1:T(8,128)(2,1)S(1)}, u32[]{:S(2)}, u32[]{:S(2)}) collective-permute-start(bf16[512,576]{0,1:T(8,128)(2,1)} %copy.216), channel_id=1, source_target_pairs={{0,16},{16,0},{1,17},{17,1},{2,18},{18,2},{3,19},{19,3},{4,20},{20... | collective-permute-start | bytes 1769480 | tf_op jit(solution)/shard_map/ppermute | solution.py:562
  1174.8 16.2 %copy-start.16 = (bf16[1,512,2048]{2,1,0:T(8,128)(2,1)S(1)}, bf16[1,512,2048]{2,1,0:T(8,128)(2,1)}, u32[]{:S(2)}) copy-start(bf16[1,512,2048]{2,1,0:T(8,128)(2,1)} %param.18) | copy-start | bytes 6291460
  (54 other events, 305.4 us)
Sparse Core Ops, SparseCore 0:
  10.9 119.2 all-gather.5
  132.3 209.8 all-gather.7
  344.4 168.5 all-gather.9
  660.2 178.5 reduce-scatter.3
  842.7 177.5 reduce-scatter.5
  1024.3 287.2 reduce-scatter.7

commit v4 on v3

--- a/solution.py
+++ b/solution.py
@@ -665,7 +665,12 @@
         shares = [lax.all_gather(v, both, axis=0, tiled=True) for v in shares]
         down_e = weight_parts(expert_down[0], 1, dp_count)
     gains, query_latent, expand_t = shares
-    output_t = lax.all_gather(output_weight.T, both, axis=0, tiled=True)
+    def gather_rows(values):
+        return lax.all_gather(values, "expert", axis=0, tiled=False)
+
+    grads_all = gather_rows(turned(cotangent[0], dp_count))
+    output_t = after(output_weight, (grads_all, query_latent)).T
+    output_t = lax.all_gather(output_t, both, axis=0, tiled=True)
     gains = gains.reshape(shards, 16, -1)
     first_gain = gains[:, 0, :g1].reshape(-1).astype(f32)
     second_gain = gains[:, 1, :g1].reshape(-1).astype(f32)
@@ -739,10 +744,6 @@
     normed_two = middle * scale_two
     ffn_rows = (normed_two * second_gain).astype(bf16)
 
-    def gather_rows(values):
-        return lax.all_gather(values, "expert", axis=0, tiled=False)
-
-    grads_all = gather_rows(turned(cotangent[0], dp_count))
     rows_all = gather_rows(
         after(turned(ffn_rows, dp_count), (grads_all, shared_moved, my_weights))
     )

time: 1440 us -> 1440 us (level)
  waiting for transfers between devices: 196 us -> 224 us
  Pallas kernels: 759 us -> 736 us
    pallas_call x1, Pallas kernels: 202 us -> 177 us  [gather_all(): pl.pallas_call(functools.partial(gather_kernel, chunks, n), in_specs=[pl....]
    all_gather x2, waiting for transfers between devices: 31.3 us -> 46.2 us  [gather_rows(): return lax.all_gather(values, 'expert', axis=0, tiled=False)]
  transfers between devices with their start and end apart: 17 -> 17, of which waited for: 8 -> 9; matrix products, arithmetic and copies ran while one was open for 28% -> 28% of each run, Pallas kernels for 43% -> 41%
where the time goes in v4:
time: 1440 us; the launch traced here: 1430 us
  Pallas kernels  736 us (51%)
  matrix products  271 us (19%)
  waiting for transfers between devices  224 us (16%)
  local copies, waits for them, and re-layouts  101 us (7%)
  other arithmetic  54.1 us (4%)
  starting transfers between devices  21.3 us (1%)
  between operations  15.4 us (1%)
    pallas_call x5, Pallas kernels, by_block(): pl.pallas_call(kernel, grid=(count,), in_specs=[block(a) for a in blocked...  288 us
    dot_general x22, matrix products, mm(): return jnp.einsum(spec, a, b, preferred_element_type=f32)  271 us
    pallas_call x1, Pallas kernels, grad_sums(): pl.pallas_call(functools.partial(grad_sum_kernel, chunks, n), in_specs=[p...  192 us
    pallas_call x1, Pallas kernels, gather_all(): pl.pallas_call(functools.partial(gather_kernel, chunks, n), in_specs=[pl....  177 us
    ppermute x9, waiting for transfers between devices, swap(): return lax.ppermute(values, 'dp', [(0, 1), (1, 0)])  119 us
    reduce_scatter x3, waiting for transfers between devices, scatter_rows(): lax.psum_scatter(flat(values), 'expert', scatter_dimension=0, tiled=True)  51 us
    pallas_call x1, Pallas kernels, attend_back(): pl.pallas_call(functools.partial(attend_back_kernel, sizes), grid=(heads...  50.7 us
    all_gather x2, waiting for transfers between devices, gather_rows(): return lax.all_gather(values, 'expert', axis=0, tiled=False)  46.2 us
  transfers between devices with their start and end apart: 17, of which 9 were waited for; matrix products, arithmetic and copies ran while one was open for 28% of the time, Pallas kernels for 41%

profile of v4, /device:TPU:0, one launch (start us, length us, event | category | flops | bytes accessed | tf_op | source)
XLA Modules:
  0.0 1434.0 jit_solution(12982973983061199819)
XLA Ops:
  13.9 177.4 %gather_all.1 = (bf16[2,2,2,2,2,16,128]{6,5,4,3,2,1,0:T(8,128)(2,1)}, bf16[2,2,2,2,2,64,3712]{6,5,4,3,2,1,0:T(8,128)(2,1)}, bf16[2,2,2,2,2,128,512]{6,5,4,3,2,1,0:T(8,128)(2,1)}, bf16[1408,1024]{1,0:T(8,128)(2,1)}) custom-call(bf16[16,128]{1,0:T(8,128)(2,1)} %fusion.125.refs_0_, bf16[64,3712]{1,0:T(8,128)(2,1)} %fusion.96.refs_1_, ...), custom_call_target="tpu_custom_call" | custom-call | bytes 664200000 | tf_op jit(solution)/shard_map/gather_all/pallas_call | solution.py:424
  191.2 45.3 %all-gather.8.cloned.1.call-done = bf16[8192,2048]{1,0:T(8,128)(2,1)} async-done(((bf16[512,2048]{1,0:T(8,128)(2,1)}), bf16[8192,2048]{1,0:T(8,128)(2,1)}) %all-gather.8.cloned.1.call-update) | async-done | bytes 33554448 | tf_op jit(solution)/shard_map/all_gather | solution.py:669
  252.1 11.8 fusion.59.nope_ref.rope_ref
  271.0 18.3 %collective-permute-done = bf16[512,576]{0,1:T(8,128)(2,1)} collective-permute-done((bf16[512,576]{0,1:T(8,128)(2,1)}, bf16[512,576]{0,1:T(8,128)(2,1)}, u32[]{:S(2)}, u32[]{:S(2)}) %collective-permute-start) | collective-permute-done | bytes 589856 | tf_op jit(solution)/shard_map/ppermute | solution.py:562
  300.1 27.3 %attend.1 = bf16[512,2048]{1,0:T(8,128)(2,1)S(1)} custom-call(f32[512,3712]{1,0:T(8,128)} %copy-done.7, f32[512,3712]{1,0:T(8,128)} %copy-done.7, f32[512,128]{1,0:T(8,128)S(1)} %get-tuple-element.247.cos_ref, f32[512,128]{1,0:T(8,128)S(1)} %get-tuple-element.248.sin_ref, bf16[1024,4096]{1,0:T(8,128)(2,1)} %convolution_convert_fusion.1.kv_ref, ...), custom_call_target="tpu_custom_call" | custom-call | bytes 99630000 | tf_op jit(solution)/shard_map/attend/pallas_call | solution.py:183
  337.1 9.3 multiply_reduce_fusion.2
  359.0 24.7 %collective-permute-done.1 = bf16[1024,528]{0,1:T(8,128)(2,1)S(1)} collective-permute-done((bf16[1024,528]{0,1:T(8,128)(2,1)S(1)}, bf16[1024,528]{0,1:T(8,128)(2,1)S(1)}, u32[]{:S(2)}, u32[]{:S(2)}) %collective-permute-start.1) | collective-permute-done | bytes 1081376 | tf_op jit(solution)/shard_map/ppermute | solution.py:562
  391.6 10.6 all_to_all.22.weight_ref
  420.0 43.0 %experts_hidden.1 = (bf16[16,256,2048]{2,1,0:T(8,128)(2,1)}, bf16[16,256,1408]{2,1,0:T(8,128)(2,1)}) custom-call(s32[16,1,512]{2,1,0:T(1,128)} %copy.209.place_ref, f32[16,1,512]{2,1,0:T(1,128)} %copy-done.40, bf16[16,512,2048]{2,1,0:T(8,128)(2,1)} %bitcast.192, bf16[1408,1024]{1,0:T(8,128)(2,1)} %bitcast.170, bf16[1408,1024]{1,0:T(8,128)(2,1)} %get-tuple-element.65.refs_1_), custom_call_target="tpu_custom_call" | custom-call | flops 32212254720 | bytes 67698688 | tf_op jit(solution)/shard_map/experts_hidden/pallas_call | solution.py:303
  462.9 53.2 %collective-permute-done.2.refs_1_.gate_up_ref = bf16[1024,2816]{1,0:T(8,128)(2,1)} collective-permute-done((bf16[1024,2816]{1,0:T(8,128)(2,1)}, bf16[1024,2816]{1,0:T(8,128)(2,1)}, u32[]{:S(2)}, u32[]{:S(2)}) %collective-permute-start.2) | collective-permute-done | bytes 5767200 | tf_op jit(solution)/shard_map/ppermute | solution.py:562
  517.1 101.7 %experts_forward.1 = (bf16[16,256,2048]{2,1,0:T(8,128)(2,1)}, bf16[16,256,1408]{2,1,0:T(8,128)(2,1)}, bf16[16,256,1408]{2,1,0:T(8,128)(2,1)}, bf16[16,256,1408]{...) custom-call(s32[16,1,512]{2,1,0:T(1,128)} %copy.209.place_ref, ...), custom_call_target="tpu_custom_call" | custom-call | flops 81604378624 | bytes 157319168 | tf_op jit(solution)/shard_map/experts_forward/pallas_call | solution.py:303
  618.9 45.3 %experts_rows.2 = bf16[16,512,1024]{2,1,0:T(8,128)(2,1)} custom-call(s32[16,1,512]{2,1,0:T(1,128)} %copy.209.place_ref, bf16[16,256,1408]{2,1,0:T(8,128)(2,1)} %get-tuple-element.69.d_gate_ref, bf16[16,256,1408]{2,1,0:T(8,128)(2,1)} %get-tuple-element.70.d_up_ref, bf16[16,512,512]{2,1,0:T(8,128)(2,1)} %get-tuple-element.72.d_shared_ref, ...), custom_call_target="tpu_custom_call" | custom-call | flops 36507222016 | bytes 55083008 | tf_op jit(solution)/shard_map/experts_rows/pallas_call | solution.py:303
  664.4 13.0 fusion.70
  677.4 17.9 %fusion.66 = bf16[1024,512]{0,1:T(8,128)(2,1)S(1)} fusion(bf16[8192,512]{1,0:T(8,128)(2,1)} %bitcast.215, bf16[8192,2048]{1,0:T(8,128)(2,1)} %all-gather.10.cloned.1.call-done), kind=kOutput, calls=%fused_computation.85 | convolution fusion | flops 8590458880 | bytes 26214400 | tf_op jit(solution)/shard_map/rd,rf->df/dot_general | solution.py:23
  699.0 45.9 %experts_rows.3 = bf16[16,512,1024]{2,1,0:T(8,128)(2,1)} custom-call(s32[16,1,512]{2,1,0:T(1,128)} %copy.209.place_ref, bf16[16,256,1408]{2,1,0:T(8,128)(2,1)} %get-tuple-element.69.d_gate_ref, bf16[16,256,1408]{2,1,0:T(8,128)(2,1)} %get-tuple-element.70.d_up_ref, bf16[16,512,512]{2,1,0:T(8,128)(2,1)} %get-tuple-element.72.d_shared_ref, ...), custom_call_target="tpu_custom_call" | custom-call | flops 36507222016 | bytes 55083008 | tf_op jit(solution)/shard_map/experts_rows/pallas_call | solution.py:303
  745.5 19.4 %fusion.44 = bf16[1024,1408]{1,0:T(8,128)(2,1)} fusion(bf16[4096,1408]{1,0:T(8,128)(2,1)} %bitcast.213, bf16[4096,2048]{1,0:T(8,128)(2,1)} %bitcast.205), kind=kOutput, calls=%fused_computation.54 | convolution fusion | flops 11812601856 | bytes 22806528 | tf_op jit(solution)/shard_map/rd,rf->df/dot_general | solution.py:23
  765.4 19.4 %fusion.47 = bf16[1024,1408]{1,0:T(8,128)(2,1)} fusion(bf16[4096,1408]{1,0:T(8,128)(2,1)} %bitcast.211, bf16[4096,2048]{1,0:T(8,128)(2,1)} %bitcast.206), kind=kOutput, calls=%fused_computation.55 | convolution fusion | flops 11812601856 | bytes 22806528 | tf_op jit(solution)/shard_map/rd,rf->df/dot_general | solution.py:23
  786.3 16.8 %fusion.50 = bf16[1408,1024]{1,0:T(8,128)(2,1)} fusion(bf16[4096,1408]{1,0:T(8,128)(2,1)} %bitcast.209, bf16[4096,2048]{1,0:T(8,128)(2,1)S(1)} %bitcast.201), kind=kOutput, calls=%fused_computation.56 | convolution fusion | flops 11812601856 | bytes 22806528 | tf_op jit(solution)/shard_map/rf,rd->fd/dot_general | solution.py:23
  803.7 52.6 %experts_output.1 = (bf16[16,512,1664]{2,1,0:T(8,128)(2,1)}, bf16[16,512,384]{2,1,0:T(8,128)(2,1)}) custom-call(s32[16,1,512]{2,1,0:T(1,128)} %copy.209.place_ref, f32[16,1,512]{2,1,0:T(1,128)} %copy-done.40, bf16[16,256,1408]{2,1,0:T(8,128)(2,1)} %get-tuple-element.74.act_ref, bf16[16,512,256]{2,1,0:T(8,128)(2,1)} %get-tuple-element.76.act_s_ref, ...), custom_call_target="tpu_custom_call" | custom-call | flops 40802189312 | bytes 56164352 | tf_op jit(solution)/shard_map/experts_output/pallas_call | solution.py:303
  856.2 18.8 %fusion.6 = f32[1024,512]{0,1:T(8,128)} fusion(bf16[8192,512]{1,0:T(8,128)(2,1)} %bitcast.216, bf16[8192,2048]{1,0:T(8,128)(2,1)} %all-gather.10.cloned.1.call-done), kind=kOutput, calls=%fused_computation.6 | convolution fusion | flops 8589934592 | bytes 27262976 | tf_op jit(solution)/shard_map/rd,rf->df/dot_general | solution.py:23
  875.1 9.5 fusion.4
  895.7 20.2 %convert_add_fusion.2 = f32[1024,1408]{1,0:T(8,128)} fusion(bf16[1024,1408]{1,0:T(8,128)(2,1)} %collective-permute-done.3, bf16[4096,1408]{1,0:T(8,128)(2,1)} %bitcast.214, bf16[4096,2048]{1,0:T(8,128)(2,1)} %bitcast.207), kind=kOutput, calls=%fused_computation.25 | convolution fusion | flops 11814043648 | bytes 28573696 | tf_op jit(solution)/shard_map/rd,rf->df/dot_general | solution.py:23
  915.9 20.1 %convert_add_fusion.1 = f32[1024,1408]{1,0:T(8,128)} fusion(bf16[1024,1408]{1,0:T(8,128)(2,1)} %collective-permute-done.4, bf16[4096,1408]{1,0:T(8,128)(2,1)} %bitcast.212, bf16[4096,2048]{1,0:T(8,128)(2,1)} %bitcast.208), kind=kOutput, calls=%fused_computation.24 | convolution fusion | flops 11814043648 | bytes 28573696 | tf_op jit(solution)/shard_map/rd,rf->df/dot_general | solution.py:23
  936.0 17.1 %collective-permute-done.5 = bf16[1408,1024]{1,0:T(8,128)(2,1)} collective-permute-done((bf16[1408,1024]{1,0:T(8,128)(2,1)}, bf16[1408,1024]{1,0:T(8,128)(2,1)}, u32[]{:S(2)}, u32[]{:S(2)}) %collective-permute-start.5) | collective-permute-done | bytes 2883616 | tf_op jit(solution)/shard_map/ppermute | solution.py:562
  953.2 17.3 %convert_add_fusion = f32[1408,1024]{1,0:T(8,128)} fusion(bf16[1408,1024]{1,0:T(8,128)(2,1)} %collective-permute-done.5, bf16[4096,1408]{1,0:T(8,128)(2,1)} %bitcast.210, bf16[4096,2048]{1,0:T(8,128)(2,1)S(1)} %bitcast.204), kind=kOutput, calls=%fused_computation.23 | convolution fusion | flops 11814043648 | bytes 28573696 | tf_op jit(solution)/shard_map/rf,rd->fd/dot_general | solution.py:23
  973.3 50.9 %reduce-scatter.6.cloned.1.call-done = bf16[512,1024]{1,0:T(8,128)(2,1)} async-done(((bf16[8192,1024]{1,0:T(8,128)(2,1)}), bf16[512,1024]{1,0:T(8,128)(2,1)}) %reduce-scatter.6.cloned.1.call-update) | async-done | bytes 1048592 | tf_op jit(solution)/shard_map/reduce_scatter | solution.py:755
  1041.2 11.8 convolution_convert_fusion.4.grad_ref
  1057.6 50.7 %attend_back.1 = (bf16[512,2048]{1,0:T(8,128)(2,1)S(1)}, bf16[512,1024]{1,0:T(8,128)(2,1)S(1)}, bf16[1024,4096]{1,0:T(8,128)(2,1)}, f32[1024,128]{1,0:T(8,128)S(1)}) custom-call(f32[512,3712]{1,0:T(8,128)} %copy-done.7, f32[512,3712]{1,0:T(8,128)} %copy-done.7, f32[512,128]{1,0:T(8,128)S(1)} %get-tuple-element.247.cos_ref, ...), custom_call_target="tpu_custom_call" | custom-call | bytes 188190000 | tf_op jit(solution)/shard_map/attend_back/pallas_call | solution.py:198
  1146.7 10.0 convolution_convert_fusion.2
  1178.7 14.9 %fusion.35 = (f32[512]{0:T(512)S(1)}, bf16[2048]{0:T(1024)(128)(2,1)S(1)}, f32[512,2048]{1,0:T(8,128)}) fusion(bf16[1,512,2048]{2,1,0:T(8,128)(2,1)} %param.18, f32[2048]{0:T(1024)S(1)} %copy-done.39, f32[512]{0:T(512)S(1)} %copy-done.53, bf16[2048,3712]{1,0:T(8,128)(2,1)} %bitcast.196, bf16[512,3648]{1,0:T(8,128)(2,1)} %concatenate.74), kind=kOutput, calls=%fused_computation.37 | convolution fusion | flops 7791965696 | bytes 25247744 | tf_op jit(solution)/shard_map/rk,dk->rd/dot_general | solution.py:23
  1194.9 14.2 convolution_convert_fusion
  1209.1 192.3 %grad_sums.1 = (f32[64,1024]{1,0:T(8,128)}, f32[64,1024]{1,0:T(8,128)}, f32[512,384]{1,0:T(8,128)}, f32[128,512]{1,0:T(8,128)}, f32[64,3712]{1,0:T(8,128)}, /*index=5*/f32[64,128]{1,0:T(8,128)}) custom-call(bf16[2,2,2,2,64,1024]{5,4,3,2,1,0:T(8,128)(2,1)} %bitcast.173, bf16[2,2,2,2,2,64,1024]{6,5,4,3,2,1,0:T(8,128)(2,1)} %bitcast.165, ...), custom_call_target="tpu_custom_call" | custom-call | bytes 627299968 | tf_op jit(solution)/shard_map/grad_sums/pallas_call | solution.py:541
  (301 shorter events, 217.7 us)
Async XLA Ops:
  7.2 229.3 %all-gather.8.cloned.1.call-start = ((), (), s32[]{:S(2)}) async-start(), calls=%async_computation.10 | async-start | bytes 35651584 | tf_op jit(solution)/shard_map/all_gather | solution.py:669
  10.5 226.0 %copy-start.29 = (bf16[64,2816]{1,0:T(8,128)(2,1)S(1)}, bf16[64,2816]{1,0:T(8,128)(2,1)}, u32[]{:S(2)}) copy-start(bf16[64,2816]{1,0:T(8,128)(2,1)} %param.29) | copy-start | bytes 1081348
  10.5 227.0 %copy-start.30 = (bf16[64,2816]{1,0:T(8,128)(2,1)S(1)}, bf16[64,2816]{1,0:T(8,128)(2,1)}, u32[]{:S(2)}) copy-start(bf16[64,2816]{1,0:T(8,128)(2,1)} %param.30) | copy-start | bytes 1081348
  10.5 326.5 %all-gather.6.cloned.1.call-start = ((), (), s32[]{:S(2)}) async-start(), calls=%async_computation.6 | async-start | bytes 8650752 | tf_op jit(solution)/shard_map/all_gather | solution.py:673
  11.3 227.3 %copy-start.31 = (bf16[2816,64]{0,1:T(8,128)(2,1)S(1)}, bf16[2816,64]{0,1:T(8,128)(2,1)}, u32[]{:S(2)}) copy-start(bf16[2816,64]{0,1:T(8,128)(2,1)} %param.31) | copy-start | bytes 1081348
  243.6 106.2 %all-to-all-start.1 = ((bf16[16,64,3,176]{3,1,2,0:T(8,128)(2,1)}), bf16[16,64,3,176]{3,1,2,0:T(8,128)(2,1)}, u32[]{:S(2)}, u32[]{:S(2)}) async-start(bf16[16,64,3,176]{3,1,2,0:T(8,128)(2,1)} %copy.199), calls=%async_computation.1 | async-start | bytes 3145728 | tf_op jit(solution)/shard_map/all_to_all | solution.py:688
  249.2 267.9 %all-gather.10.cloned.1.call-start = ((), (), s32[]{:S(2)}) async-start(), calls=%async_computation.11 | async-start | bytes 35651584 | tf_op jit(solution)/shard_map/all_gather | solution.py:669
  268.4 20.9 %collective-permute-start = (bf16[512,576]{0,1:T(8,128)(2,1)}, bf16[512,576]{0,1:T(8,128)(2,1)}, u32[]{:S(2)}, u32[]{:S(2)}) collective-permute-start(bf16[512,576]{0,1:T(8,128)(2,1)} %copy.196), channel_id=1, source_target_pairs={{0,16},{16,0},{1,17},{17,1},{2,18},{18,2},{3,19},{19,3},{4,20},{20... | collective-permute-start | bytes 1769480 | tf_op jit(solution)/shard_map/ppermute | solution.py:562
  270.0 76.3 %copy-start.35 = (f32[2048]{0:T(1024)}, f32[2048]{0:T(1024)S(1)}, u32[]{:S(2)}) copy-start(f32[2048]{0:T(1024)S(1)} %reshape.483) | copy-start | bytes 24580
  349.8 620.7 %reduce-scatter.4.cloned.1.call-start = ((), (), s32[]{:S(2)}) async-start(), calls=%async_computation.7 | async-start | bytes 17825792 | tf_op jit(solution)/shard_map/reduce_scatter | solution.py:755
  357.7 30.7 %copy-start.18 = (bf16[1,1024,1408]{2,1,0:T(8,128)(2,1)S(1)}, bf16[1,1024,1408]{2,1,0:T(8,128)(2,1)}, u32[]{:S(2)}) copy-start(bf16[1,1024,1408]{2,1,0:T(8,128)(2,1)} %param.33) | copy-start | bytes 8650756
  357.7 26.0 %collective-permute-start.1 = (bf16[1024,528]{0,1:T(8,128)(2,1)S(1)}, bf16[1024,528]{0,1:T(8,128)(2,1)S(1)}, u32[]{:S(2)}, u32[]{:S(2)}) collective-permute-start(bf16[1024,528]{0,1:T(8,128)(2,1)S(1)} %reshape.454), channel_id=1, source_target_pairs={{0,16},{16,0},{1,17},{17,1},{2,18},{18,2},{3,19},{19,3},{4,20},{20... | collective-permute-start | bytes 3244040 | tf_op jit(solution)/shard_map/ppermute | solution.py:562
  390.2 126.0 %collective-permute-start.2 = (bf16[1024,2816]{1,0:T(8,128)(2,1)}, bf16[1024,2816]{1,0:T(8,128)(2,1)}, u32[]{:S(2)}, u32[]{:S(2)}) collective-permute-start(bf16[1024,2816]{1,0:T(8,128)(2,1)} %constant_dynamic-update-slice_fusion.refs_0_.gate_up_ref), channel_id=1, source_target_pairs={{0,16},{16,0},{1,17},{17,1},{2,18},{18,2},{3,19},{19,3},{4,20},{20... | collective-permute-start | bytes 17301512 | tf_op jit(solution)/shard_map/ppermute | solution.py:562
  664.2 360.1 %reduce-scatter.6.cloned.1.call-start = ((), (), s32[]{:S(2)}) async-start(), calls=%async_computation.8 | async-start | bytes 17825792 | tf_op jit(solution)/shard_map/reduce_scatter | solution.py:755
  697.7 186.9 %collective-permute-start.6 = (bf16[1024,768]{0,1:T(8,128)(2,1)}, bf16[1024,768]{0,1:T(8,128)(2,1)}, u32[]{:S(2)}, u32[]{:S(2)}) collective-permute-start(bf16[1024,768]{0,1:T(8,128)(2,1)} %pad_maximum_fusion.5), channel_id=1, source_target_pairs={{0,16},{16,0},{1,17},{17,1},{2,18},{18,2},{3,19},{19,3},{4,20},{20... | collective-permute-start | bytes 4718600 | tf_op jit(solution)/shard_map/ppermute | solution.py:562
  745.0 676.0 %reduce-scatter.8.cloned.1.call-start = ((), (), s32[]{:S(2)}) async-start(), calls=%async_computation.9 | async-start | bytes 28966912 | tf_op jit(solution)/shard_map/reduce_scatter | solution.py:755
  745.5 40.8 %slice-start = ((s8[16777216]{0:T(1024)(128)(4,1)}), s8[4194304]{0:T(1024)(128)(4,1)S(1)}, s32[]{:S(2)}) async-start(s8[16777216]{0:T(1024)(128)(4,1)} %bitcast.199), calls=%async_computation.12 | async-start | bytes 8388608
  745.5 40.8 %slice-start.1 = ((s8[16777216]{0:T(1024)(128)(4,1)}), s8[4194304]{0:T(1024)(128)(4,1)S(1)}, s32[]{:S(2)}) async-start(s8[16777216]{0:T(1024)(128)(4,1)} %bitcast.199), calls=%async_computation.13 | async-start | bytes 8388608
  764.9 130.8 %collective-permute-start.3 = (bf16[1024,1408]{1,0:T(8,128)(2,1)}, bf16[1024,1408]{1,0:T(8,128)(2,1)}, u32[]{:S(2)}, u32[]{:S(2)}) collective-permute-start(bf16[1024,1408]{1,0:T(8,128)(2,1)} %fusion.44), channel_id=1, source_target_pairs={{0,16},{16,0},{1,17},{17,1},{2,18},{18,2},{3,19},{19,3},{4,20},{20... | collective-permute-start | bytes 8650760 | tf_op jit(solution)/shard_map/ppermute | solution.py:562
  765.4 20.9 %slice-start.2 = ((s8[16777216]{0:T(1024)(128)(4,1)}), s8[4194304]{0:T(1024)(128)(4,1)S(1)}, s32[]{:S(2)}) async-start(s8[16777216]{0:T(1024)(128)(4,1)} %bitcast.199), calls=%async_computation.14 | async-start | bytes 8388608
  765.4 20.9 %slice-start.3 = ((s8[16777216]{0:T(1024)(128)(4,1)}), s8[4194304]{0:T(1024)(128)(4,1)S(1)}, s32[]{:S(2)}) async-start(s8[16777216]{0:T(1024)(128)(4,1)} %bitcast.199), calls=%async_computation.15 | async-start | bytes 8388608
  784.8 131.0 %collective-permute-start.4 = (bf16[1024,1408]{1,0:T(8,128)(2,1)}, bf16[1024,1408]{1,0:T(8,128)(2,1)}, u32[]{:S(2)}, u32[]{:S(2)}) collective-permute-start(bf16[1024,1408]{1,0:T(8,128)(2,1)} %fusion.47), channel_id=1, source_target_pairs={{0,16},{16,0},{1,17},{17,1},{2,18},{18,2},{3,19},{19,3},{4,20},{20... | collective-permute-start | bytes 8650760 | tf_op jit(solution)/shard_map/ppermute | solution.py:562
  803.1 150.0 %collective-permute-start.5 = (bf16[1408,1024]{1,0:T(8,128)(2,1)}, bf16[1408,1024]{1,0:T(8,128)(2,1)}, u32[]{:S(2)}, u32[]{:S(2)}) collective-permute-start(bf16[1408,1024]{1,0:T(8,128)(2,1)} %fusion.50), channel_id=1, source_target_pairs={{0,16},{16,0},{1,17},{17,1},{2,18},{18,2},{3,19},{19,3},{4,20},{20... | collective-permute-start | bytes 8650760 | tf_op jit(solution)/shard_map/ppermute | solution.py:562
  895.7 57.5 %slice-start.4 = ((s8[16777216]{0:T(1024)(128)(4,1)}), s8[4194304]{0:T(1024)(128)(4,1)S(1)}, s32[]{:S(2)}) async-start(s8[16777216]{0:T(1024)(128)(4,1)} %bitcast.202), calls=%async_computation.16 | async-start | bytes 8388608
  895.7 57.5 %slice-start.5 = ((s8[16777216]{0:T(1024)(128)(4,1)}), s8[4194304]{0:T(1024)(128)(4,1)S(1)}, s32[]{:S(2)}) async-start(s8[16777216]{0:T(1024)(128)(4,1)} %bitcast.202), calls=%async_computation.17 | async-start | bytes 8388608
  915.9 37.3 %slice-start.6 = ((s8[16777216]{0:T(1024)(128)(4,1)}), s8[4194304]{0:T(1024)(128)(4,1)S(1)}, s32[]{:S(2)}) async-start(s8[16777216]{0:T(1024)(128)(4,1)} %bitcast.202), calls=%async_computation.18 | async-start | bytes 8388608
  915.9 37.3 %slice-start.7 = ((s8[16777216]{0:T(1024)(128)(4,1)}), s8[4194304]{0:T(1024)(128)(4,1)S(1)}, s32[]{:S(2)}) async-start(s8[16777216]{0:T(1024)(128)(4,1)} %bitcast.202), calls=%async_computation.19 | async-start | bytes 8388608
  1027.5 87.4 %all-to-all-start.2 = ((bf16[16,64,3,176]{3,1,2,0:T(8,128)(2,1)}), bf16[16,64,3,176]{3,1,2,0:T(8,128)(2,1)}, u32[]{:S(2)}, u32[]{:S(2)}) async-start(bf16[16,64,3,176]{3,1,2,0:T(8,128)(2,1)} %copy.219), calls=%async_computation.5 | async-start | bytes 3145728 | tf_op jit(solution)/shard_map/all_to_all | solution.py:822
  1041.2 69.3 %copy-start.23 = (bf16[512,2048]{1,0:T(8,128)(2,1)}, bf16[512,2048]{1,0:T(8,128)(2,1)S(1)}, u32[]{:S(2)}) copy-start(bf16[512,2048]{1,0:T(8,128)(2,1)S(1)} %get-tuple-element.220) | copy-start | bytes 6291460
  1055.8 75.8 %collective-permute-start.7 = (bf16[1024,1024]{1,0:T(8,128)(2,1)}, bf16[1024,1024]{1,0:T(8,128)(2,1)}, u32[]{:S(2)}, u32[]{:S(2)}) collective-permute-start(bf16[1024,1024]{1,0:T(8,128)(2,1)} %convolution_convert_fusion.5), channel_id=1, source_target_pairs={{0,16},{16,0},{1,17},{17,1},{2,18},{18,2},{3,19},{19,3},{4,20},{20... | collective-permute-start | bytes 6291464 | tf_op jit(solution)/shard_map/ppermute | solution.py:562
  1146.7 15.2 %collective-permute-start.8 = (bf16[512,576]{0,1:T(8,128)(2,1)}, bf16[512,576]{0,1:T(8,128)(2,1)S(1)}, u32[]{:S(2)}, u32[]{:S(2)}) collective-permute-start(bf16[512,576]{0,1:T(8,128)(2,1)} %copy.216), channel_id=1, source_target_pairs={{0,16},{16,0},{1,17},{17,1},{2,18},{18,2},{3,19},{19,3},{4,20},{20... | collective-permute-start | bytes 1769480 | tf_op jit(solution)/shard_map/ppermute | solution.py:562
  1178.7 16.2 %copy-start.16 = (bf16[1,512,2048]{2,1,0:T(8,128)(2,1)S(1)}, bf16[1,512,2048]{2,1,0:T(8,128)(2,1)}, u32[]{:S(2)}) copy-start(bf16[1,512,2048]{2,1,0:T(8,128)(2,1)} %param.18) | copy-start | bytes 6291460
  (54 other events, 325.4 us)
Sparse Core Ops, SparseCore 0:
  10.6 225.8 all-gather.7
  239.4 97.6 all-gather.5
  349.9 167.1 all-gather.9
  664.3 178.4 reduce-scatter.3
  846.8 177.4 reduce-scatter.5
  1028.2 287.2 reduce-scatter.7
